TPU v7x, 256 devices: a whole 4x4x8 slice. The times are simulated.
256 devices in a mesh: seq: 32 (over x, z), col: 8 (over y, core).
Axes of the slice: x: 4, y: 4, z: 8, core: 2. Of those that a mesh axis runs over, the one named last changes fastest.
Arguments:
- embedded_alignment: bfloat16 [256, 512, 768], P('seq', 'col'), may hold values from -5 to 5
- horizontal_input_projections: bfloat16 [768, 2304], replicated, may hold values from -0.29228357 to 0.29228357
- horizontal_final_projection: bfloat16 [768, 768], replicated, may hold values from -0.21875 to 0.21875
- vertical_input_projections: bfloat16 [768, 2304], replicated, may hold values from -0.8660254 to 0.8660254
- vertical_final_projection: bfloat16 [768, 768], replicated, may hold values from -0.21875 to 0.21875
Outputs:
- mixed_msa: bfloat16 [256, 512, 768], P('seq', 'col')
All inputs are finite; a program needn't handle non-finite values.
Results may differ from a plain program's by a relative error of at most 0.028.
Values may be sent and summed in bfloat16 or wider, within the bound.
No kernel may reach another device: no remote copies, remote signals or barrier semaphores. Data moves between devices by JAX's collectives and lax.ppermute only.
A program may use at most 128 MiB of HBM per device.

v0:
```python
import jax
import jax.numpy as jnp
from jax import lax
from jax.sharding import PartitionSpec as P

FOCUS_BRANCHES = 12


epsilon = 1e-05


def layer_norm(embedding_entries):
    row_mean = jnp.mean(embedding_entries, axis=-1, keepdims=True)
    centered = embedding_entries - row_mean
    spread = jnp.mean(centered * centered, axis=-1, keepdims=True)
    return centered * lax.rsqrt(spread + epsilon)


def softmax_last(scores):
    row_maximum = jnp.max(scores, axis=-1, keepdims=True)
    powers = jnp.exp(scores - row_maximum)
    return powers / jnp.sum(powers, axis=-1, keepdims=True)


def attend_columns(col_block, vertical_input_projections, vertical_final_projection):
    seq_count, col_count, embedding_entries = col_block.shape
    head_size = embedding_entries // FOCUS_BRANCHES
    normed = layer_norm(col_block.astype(jnp.float32)).astype(jnp.bfloat16)
    projected = jnp.dot(
        normed.reshape(seq_count * col_count, embedding_entries),
        vertical_input_projections,
        preferred_element_type=jnp.float32,
    ).astype(jnp.bfloat16)
    projected = projected.reshape(seq_count, col_count, 3, FOCUS_BRANCHES, head_size)
    queries = projected[:, :, 0]
    key_heads = projected[:, :, 1]
    value_heads = projected[:, :, 2]
    scores = jnp.einsum(
        "rchd,schd->chrs", queries, key_heads, preferred_element_type=jnp.float32
    ) * head_size ** (-0.5)
    weights = softmax_last(scores).astype(jnp.bfloat16)
    context = jnp.einsum(
        "chrs,schd->rchd", weights, value_heads, preferred_element_type=jnp.float32
    ).astype(jnp.bfloat16)
    update = jnp.dot(
        context.reshape(seq_count * col_count, embedding_entries),
        vertical_final_projection,
        preferred_element_type=jnp.float32,
    )
    return (
        col_block.astype(jnp.float32) + update.reshape(seq_count, col_count, embedding_entries)
    ).astype(jnp.bfloat16)


def per_device(
    embedded_alignment,
    horizontal_input_projections,
    horizontal_final_projection,
    vertical_input_projections,
    vertical_final_projection,
):
    shard_lineage_count, shard_site_count, embedding_entries = embedded_alignment.shape
    head_size = embedding_entries // FOCUS_BRANCHES
    seq_devices = lax.axis_size("seq")
    total_seqs = shard_lineage_count * seq_devices
    residue_lineage_grid = embedded_alignment.reshape(
        shard_lineage_count * shard_site_count, embedding_entries
    )
    normed = layer_norm(residue_lineage_grid.astype(jnp.float32)).astype(jnp.bfloat16)
    queries = jnp.dot(
        normed,
        horizontal_input_projections[:, :embedding_entries],
        preferred_element_type=jnp.float32,
    ).astype(jnp.bfloat16)
    queries = queries.reshape(shard_lineage_count, shard_site_count, FOCUS_BRANCHES, head_size)
    portion = lax.all_gather(
        normed.reshape(shard_lineage_count, shard_site_count, embedding_entries),
        "col",
        axis=1,
        tiled=True,
    )
    col_count = portion.shape[1]
    paired = jnp.dot(
        portion.reshape(shard_lineage_count * col_count, embedding_entries),
        horizontal_input_projections[:, embedding_entries:],
        preferred_element_type=jnp.float32,
    )
    key_values = paired.astype(jnp.bfloat16).reshape(
        shard_lineage_count, col_count, 2 * embedding_entries
    )
    all_cols = key_values.shape[1]
    key_heads = key_values[:, :, :embedding_entries].reshape(
        shard_lineage_count, all_cols, FOCUS_BRANCHES, head_size
    )
    partial_value = jnp.einsum(
        "rihd,rjhd->hij", queries, key_heads, preferred_element_type=jnp.float32
    )
    logit_scale = (head_size * total_seqs) ** (-0.5)
    raw_score_grand_addition = lax.psum(partial_value.astype(jnp.bfloat16), "seq").astype(
        jnp.float32
    )
    weights = softmax_last(raw_score_grand_addition * logit_scale).astype(jnp.bfloat16)
    value_heads = key_values[:, :, embedding_entries:].reshape(
        shard_lineage_count, all_cols, FOCUS_BRANCHES, head_size
    )
    context = jnp.einsum("hij,rjhd->rihd", weights, value_heads, preferred_element_type=jnp.float32)
    context = context.reshape(shard_lineage_count, shard_site_count, embedding_entries)
    update = jnp.dot(
        context.astype(jnp.bfloat16).reshape(
            shard_lineage_count * shard_site_count, embedding_entries
        ),
        horizontal_final_projection,
        preferred_element_type=jnp.float32,
    )
    horizontal_context_result = (residue_lineage_grid.astype(jnp.float32) + update).astype(
        jnp.bfloat16
    )
    column_runs = shard_site_count // seq_devices
    split_result = horizontal_context_result.reshape(
        shard_lineage_count, seq_devices, column_runs, embedding_entries
    )
    col_block = lax.all_to_all(split_result, "seq", split_axis=1, concat_axis=0, tiled=True)
    flat_block = col_block.reshape(col_block.shape[0], col_block.shape[2], embedding_entries)
    done = attend_columns(flat_block, vertical_input_projections, vertical_final_projection)
    finished = done.reshape(col_block.shape)
    returned = lax.all_to_all(finished, "seq", split_axis=0, concat_axis=1, tiled=True)
    return returned.reshape(shard_lineage_count, shard_site_count, embedding_entries)


def solution(mesh):
    placed = (P("seq", "col", None), P(), P(), P(), P())
    return jax.shard_map(
        per_device, mesh=mesh, in_specs=placed, out_specs=P("seq", "col", None), check_vma=False
    )
```

profile of v0, /device:TPU:32, one launch (start us, length us, event | category | flops | bytes accessed | tf_op | source)
XLA Modules:
  0.0 374.1 jit_solution(3935782387965405794)
XLA Ops:
  8.0 1.5 fusion.20
  12.3 2.9 convolution_convert_fusion.2
  15.3 3.8 %reshape.151 = bf16[8,64,12,64]{3,2,1,0:T(8,128)(2,1)} reshape(bf16[512,768]{1,0:T(8,128)(2,1)} %convolution_convert_fusion.2) | data formatting | bytes 1572864 | tf_op jit(solution)/shard_map/reshape | solution.py:75
  19.0 37.9 %all-gather.2.cloned.1.call-done = bf16[8,512,768]{2,1,0:T(8,128)(2,1)} async-done(((bf16[8,64,768]{2,1,0:T(8,128)(2,1)}), bf16[8,512,768]{2,1,0:T(8,128)(2,1)}) %all-gather.2.cloned.1.call-update) | async-done | bytes 6291472 | tf_op jit(solution)/shard_map/all_gather | solution.py:76
  57.0 12.8 %convolution_convert_fusion = bf16[4096,1536]{1,0:T(8,128)(2,1)S(1)} fusion(bf16[4096,768]{1,0:T(8,128)(2,1)} %bitcast.78, bf16[768,2304]{1,0:T(8,128)(2,1)} %param.6), kind=kOutput, calls=%fused_computation.2 | convolution fusion | flops 9669967872 | bytes 21233664 | tf_op jit(solution)/shard_map/dot_general | solution.py:83
  69.8 5.1 %fusion.52 = (bf16[8,512,768]{2,1,0:T(8,128)(2,1)}, bf16[8,512,768]{2,1,0:T(8,128)(2,1)}) fusion(bf16[8,512,1536]{2,1,0:T(8,128)(2,1)S(1)} %bitcast.74), kind=kLoop, calls=%fused_computation.62 | loop fusion | bytes 25165824 | tf_op jit(solution)/shard_map/slice | solution.py:92
  74.8 8.7 %copy.52 = bf16[8,512,768]{1,2,0:T(8,128)(2,1)} copy(bf16[8,512,768]{2,1,0:T(8,128)(2,1)} %get-tuple-element.5) | data formatting | bytes 12582912
  83.5 5.6 %bitcast_convert_fusion = bf16[12,64,512]{2,1,0:T(8,128)(2,1)} fusion(bf16[8,512,12,64]{1,3,2,0:T(8,128)(2,1)} %bitcast.76, bf16[8,64,12,64]{3,2,1,0:T(8,128)(2,1)} %reshape.151), kind=kOutput, calls=%fused_computation.20 | convolution fusion | flops 403046400 | bytes 7864320 | tf_op jit(solution)/shard_map/rihd,rjhd->hij/dot_general | solution.py:95
  89.2 8.6 %copy.51 = bf16[8,512,768]{1,2,0:T(8,128)(2,1)} copy(bf16[8,512,768]{2,1,0:T(8,128)(2,1)} %get-tuple-element.6) | data formatting | bytes 12582912
  97.8 139.1 %all-reduce.2.cloned.1.call-done = bf16[12,64,512]{2,1,0:T(8,128)(2,1)} async-done(((bf16[12,64,512]{2,1,0:T(8,128)(2,1)}), bf16[12,64,512]{2,1,0:T(8,128)(2,1)}) %all-reduce.2.cloned.1.call-update) | async-done | bytes 786448 | tf_op jit(solution)/shard_map/psum | solution.py:99
  236.9 1.6 fusion.54
  238.5 6.0 %fusion.27 = bf16[8,64,12,64]{1,3,0,2:T(8,128)(2,1)} fusion(bf16[8,512,12,64]{1,3,2,0:T(8,128)(2,1)} %bitcast.75, f32[12,64]{1,0:T(8,128)S(1)} %fusion.54, bf16[12,64,512]{2,1,0:T(8,128)(2,1)} %all-reduce.2.cloned.1.call-done), kind=kOutput, calls=%fused_computation.39 | convolution fusion | flops 405013760 | bytes 7867392 | tf_op jit(solution)/shard_map/hij,rjhd->rihd/dot_general | solution.py:106
  244.5 3.8 %copy.35 = bf16[8,64,12,64]{1,0,3,2:T(8,128)(2,1)} copy(bf16[8,64,12,64]{1,3,0,2:T(8,128)(2,1)} %fusion.27) | data formatting | bytes 1572864 | tf_op jit(solution)/shard_map/convert_element_type | solution.py:109
  248.3 3.5 convert_element_type.104
  251.7 3.4 fusion.24
  255.2 2.8 reshape.138
  258.0 1.7 copy.36
  259.7 25.4 %all_to_all.24 = bf16[8,32,2,768]{3,2,0,1:T(2,128)(2,1)S(1)} all-to-all(bf16[8,32,2,768]{3,2,0,1:T(2,128)(2,1)S(1)} %copy.36), channel_id=1, replica_groups=mesh['seq'=32,'col'=8] {'seq'}, dimensions={1} | all-to-all | bytes 1572864 | tf_op jit(solution)/shard_map/all_to_all | solution.py:122
  288.3 2.5 multiply_reduce_fusion.1
  292.5 3.2 convert_bitcast_fusion
  295.7 3.2 reshape.144
  298.9 4.9 %convolution_convert_fusion.1 = bf16[512,2304]{1,0:T(8,128)(2,1)} fusion(bf16[768,2304]{1,0:T(8,128)(2,1)S(1)} %copy-done, f32[512,768]{1,0:T(8,128)} %reshape.144, f32[512]{0:T(512)S(1)} %rsqrt.26, f32[512]{0:T(512)S(1)} %div.38), kind=kOutput, calls=%fused_computation.11 | convolution fusion | flops 1814298624 | bytes 7475200 | tf_op jit(solution)/shard_map/dot_general | solution.py:29
  303.8 8.2 %reshape.139 = bf16[256,2,3,12,64]{4,3,2,1,0:T(8,128)(2,1)} reshape(bf16[512,2304]{1,0:T(8,128)(2,1)} %convolution_convert_fusion.1) | data formatting | bytes 4718592 | tf_op jit(solution)/shard_map/reshape | solution.py:34
  312.0 6.0 %fusion.53 = (bf16[256,2,1,12,64]{4,3,2,1,0:T(8,128)(2,1)}, bf16[256,2,1,12,64]{4,3,2,1,0:T(8,128)(2,1)}, bf16[256,2,1,12,64]{4,3,2,1,0:T(8,128)(2,1)}) fusion(bf16[256,2,3,12,64]{4,3,2,1,0:T(8,128)(2,1)} %reshape.139), kind=kLoop, calls=%fused_computation.63 | loop fusion | bytes 4718592 | tf_op jit(solution)/shard_map/slice | solution.py:37
  318.0 3.2 copy.54
  321.2 3.2 copy.55
  324.4 2.4 fusion.40
  326.8 4.8 %fusion.55 = (f32[2,12,256]{2,1,0:T(8,128)}, f32[2,12,256,256]{2,3,1,0:T(8,128)}) fusion(f32[2,12,256,256]{2,3,1,0:T(8,128)S(1)} %fusion.40), kind=kOutput, calls=%fused_computation.65 | output fusion | flops 6291711 | bytes 12607488 | tf_op jit(solution)/shard_map/sub | solution.py:21
  331.7 3.2 copy.53
  334.9 3.8 %fusion.30 = bf16[2,12,64,256]{3,2,1,0:T(8,128)(2,1)S(1)} fusion(f32[2,12,256,256]{2,3,1,0:T(8,128)} %get-tuple-element.11, f32[2,12,256]{2,1,0:T(8,128)} %get-tuple-element.10, bf16[256,2,1,12,64]{0,4,3,1,2:T(8,128)(2,1)} %copy.53), kind=kOutput, calls=%fused_computation.41 | convolution fusion | flops 204865536 | bytes 7888896 | tf_op jit(solution)/shard_map/chrs,schd->rchd/dot_general | solution.py:42
  340.3 22.5 %all_to_all.25 = bf16[256,1,2,768]{3,2,1,0:T(2,128)(2,1)S(1)} all-to-all(bf16[256,1,2,768]{3,2,1,0:T(2,128)(2,1)S(1)} %copy.43), channel_id=1, replica_groups=mesh['seq'=32,'col'=8] {'seq'}, dimensions={0} | all-to-all | bytes 1572864 | tf_op jit(solution)/shard_map/all_to_all | solution.py:126
  364.3 3.0 reshape.141
  (29 shorter events, 12.3 us)
Async XLA Ops:
  6.5 292.4 %copy-start = (bf16[768,2304]{1,0:T(8,128)(2,1)S(1)}, bf16[768,2304]{1,0:T(8,128)(2,1)}, u32[]{:S(2)}) copy-start(bf16[768,2304]{1,0:T(8,128)(2,1)} %param.8) | copy-start | bytes 10616836
  6.5 50.5 %all-gather.2.cloned.1.call-start = ((), (), s32[]{:S(2)}) async-start(), calls=%async_computation.2 | async-start | bytes 7077888 | tf_op jit(solution)/shard_map/all_gather | solution.py:76
  6.5 3.0 copy-start.1
  10.7 226.1 %all-reduce.2.cloned.1.call-start = ((), (), s32[]{:S(2)}) async-start(), calls=%async_computation.3 | async-start | bytes 1572864 | tf_op jit(solution)/shard_map/psum | solution.py:99
  285.1 0.9 copy-start.2
  334.9 3.8 %copy-start.3 = (f32[32,8,1,2,768]{4,3,1,0,2:T(2,128)S(1)}, f32[32,8,1,2,768]{4,3,1,0,2:T(2,128)}, u32[]{:S(2)}) copy-start(f32[32,8,1,2,768]{4,3,1,0,2:T(2,128)} %convert_bitcast_fusion) | copy-start | bytes 4718596
  334.9 3.8 %copy-start.4 = (bf16[768,768]{1,0:T(8,128)(2,1)S(1)}, bf16[768,768]{1,0:T(8,128)(2,1)}, u32[]{:S(2)}) copy-start(bf16[768,768]{1,0:T(8,128)(2,1)} %param.9) | copy-start | bytes 3538948
Sparse Core Ops, SparseCore 0:
  10.9 46.0 all-gather.1
  89.3 147.5 all-reduce.1
where the time goes:
time: 375 us; the launch traced here: 374 us
  waiting for transfers between devices  177 us (47%)
  local copies, waits for them, and re-layouts  73.3 us (20%)
  blocking collectives  47.9 us (13%)
  matrix products  42.6 us (11%)
  other arithmetic  19.6 us (5%)
  between operations  13.5 us (4%)
    psum x1, waiting for transfers between devices, per_device(): lax.psum(partial_value.astype(jnp.bfloat16), 'seq').astype(jnp.float32)  139 us
    all_gather x1, waiting for transfers between devices, per_device(): lax.all_gather(normed.reshape(shard_lineage_count, shard_site_count, embe...  37.9 us
    unnamed x15, local copies, waits for them, and re-layouts  27.8 us
    all_to_all x1, blocking collectives, per_device(): lax.all_to_all(split_result, 'seq', split_axis=1, concat_axis=0, tiled=True)  25.4 us
    all_to_all x1, blocking collectives, per_device(): lax.all_to_all(finished, 'seq', split_axis=0, concat_axis=1, tiled=True)  22.5 us
    dot_general x1, matrix products, per_device(): jnp.dot(portion.reshape(shard_lineage_count * col_count, embedding_entrie...  12.8 us
    reshape x1, local copies, waits for them, and re-layouts, attend_columns(): projected.reshape(seq_count, col_count, 3, FOCUS_BRANCHES, head_size)  8.2 us
  transfers between devices with their start and end apart: 2, of which 2 were waited for; matrix products, arithmetic and copies ran while one was open for 5% of the time, Pallas kernels for 0%

commit v1 on v0

v1 whole, which is shorter than its diff:
```python
import functools

import jax
import jax.numpy as jnp
from jax import lax
from jax.experimental import pallas as pl
from jax.experimental.pallas import tpu as pltpu
from jax.sharding import Mesh, PartitionSpec as P

HEADS = 12
PAIRS = 6
D = 768
R = 8
I = 64
EPS = 1e-05
LOG2E = 1.4426950408889634
NT = (((1,), (1,)), ((), ()))
BF = jnp.bfloat16
F32 = jnp.float32
VMEM = pl.BlockSpec(memory_space=pltpu.VMEM)
MB = 1024 * 1024


def params(limit=32 * MB):
    return pltpu.CompilerParams(vmem_limit_bytes=limit)


def cost(flops, bytes_accessed, transcendentals=0):
    return pl.CostEstimate(
        flops=int(flops), bytes_accessed=int(bytes_accessed), transcendentals=int(transcendentals)
    )


def layer_norm(x):
    mean = jnp.mean(x, axis=-1, keepdims=True)
    centered = x - mean
    spread = jnp.mean(centered * centered, axis=-1, keepdims=True)
    return centered * lax.rsqrt(spread + EPS)


def first_head(rows):
    return lax.broadcasted_iota(jnp.int32, (rows, 128), 1) < 64


def query_kernel(x_ref, w_ref, q_ref):
    x = x_ref[...].astype(F32).reshape(2 * I, D)
    normed = layer_norm(x).astype(BF)
    q = jnp.dot(normed, w_ref[...], preferred_element_type=F32).astype(BF)
    first = first_head(I)
    zero = jnp.zeros((I, 128), BF)
    for p in range(PAIRS):
        for r in range(2):
            block = q[r * I : (r + 1) * I, p * 128 : (p + 1) * 128]
            q_ref[p, 0:I, r * 128 : (r + 1) * 128] = jnp.where(first, block, zero)
            q_ref[p, I : 2 * I, r * 128 : (r + 1) * 128] = jnp.where(first, zero, block)


def masked_queries(x, w):
    return pl.pallas_call(
        query_kernel,
        grid=(R // 2,),
        out_shape=jax.ShapeDtypeStruct((PAIRS, 2 * I, R * 128), BF),
        in_specs=[
            pl.BlockSpec((2, I, D), lambda s: (s, 0, 0)),
            pl.BlockSpec((D, D), lambda s: (0, 0)),
        ],
        out_specs=pl.BlockSpec((PAIRS, 2 * I, 256), lambda s: (0, 0, s)),
        compiler_params=params(),
        cost_estimate=cost(2 * R * I * D * D, 4e6),
        name="queries",
    )(x, w)


def pair_kernel(a_ref, b_ref, wk_ref, wv_ref, q_ref, logit_ref, v_ref, acc):
    s = pl.program_id(0)
    rows = []
    for r in range(2):
        rows.append(a_ref[r].astype(F32))
        rows.append(b_ref[r].astype(F32))
    normed = layer_norm(jnp.concatenate(rows, axis=0)).astype(BF)
    k = jnp.dot(normed, wk_ref[...], preferred_element_type=F32).astype(BF)
    for p in range(PAIRS):
        lanes = slice(p * 128, (p + 1) * 128)
        keys = jnp.concatenate([k[0:128, lanes], k[128:256, lanes]], axis=1)
        part = lax.dot_general(q_ref[p], keys, NT, preferred_element_type=F32)

        @pl.when(s == 0)
        def _():
            acc[p] = part

        @pl.when(s > 0)
        def _():
            acc[p] += part

    v = jnp.dot(normed, wv_ref[...], preferred_element_type=F32).astype(BF)
    for p in range(PAIRS):
        lanes = slice(p * 128, (p + 1) * 128)
        v_ref[p, :, 0:128] = v[0:128, lanes]
        v_ref[p, :, 128:256] = v[128:256, lanes]

    @pl.when(s == R // 2 - 1)
    def _():
        logit_ref[...] = acc[...].astype(BF)


def keys_values(a, b, w, q):
    return pl.pallas_call(
        pair_kernel,
        grid=(R // 2,),
        out_shape=(
            jax.ShapeDtypeStruct((PAIRS, 2 * I, 128), BF),
            jax.ShapeDtypeStruct((PAIRS, 128, R * 128), BF),
        ),
        in_specs=[
            pl.BlockSpec((2, I, D), lambda s: (s, 0, 0)),
            pl.BlockSpec((2, I, D), lambda s: (s, 0, 0)),
            pl.BlockSpec((D, D), lambda s: (0, 1)),
            pl.BlockSpec((D, D), lambda s: (0, 2)),
            pl.BlockSpec((PAIRS, 2 * I, 256), lambda s: (0, 0, s)),
        ],
        out_specs=(
            pl.BlockSpec((PAIRS, 2 * I, 128), lambda s: (0, 0, 0)),
            pl.BlockSpec((PAIRS, 128, 256), lambda s: (0, 0, s)),
        ),
        scratch_shapes=[pltpu.VMEM((PAIRS, 2 * I, 128), F32)],
        compiler_params=params(),
        cost_estimate=cost(2 * 1024 * D * 2 * D + 2 * D * 1024 * 128, 8e6),
        name="keys_values",
    )(a, b, w, w, q)


def weight_kernel(scale, copies, *refs):
    out = refs[-1]
    totals = [jnp.sum(ref[...].astype(F32), axis=0) for ref in refs[:-1]]
    logits = jnp.concatenate(totals, axis=1)
    top = jnp.max(logits, axis=-1, keepdims=True)
    powers = jnp.exp2((logits - top) * (scale * LOG2E))
    weights = powers / jnp.sum(powers, axis=-1, keepdims=True)
    weights = weights.astype(BF)
    for c in range(copies):
        out[c] = weights


def row_weights(parts, scale, copies):
    rows = parts[0].shape[1]
    return pl.pallas_call(
        functools.partial(weight_kernel, scale, copies),
        out_shape=jax.ShapeDtypeStruct((copies, rows, 512), BF),
        in_specs=[VMEM] * len(parts),
        out_specs=VMEM,
        compiler_params=params(),
        cost_estimate=cost(1e6, 1.2e6),
        name="row_weights",
    )(*parts)


def reorder(major, minor):
    n = major * minor
    to = lax.broadcasted_iota(jnp.int32, (n, n), 0)
    at = lax.broadcasted_iota(jnp.int32, (n, n), 1)
    source = lax.rem(to, major) * minor + lax.div(to, major)
    return jnp.where(at == source, 1.0, 0.0).astype(BF)


def context_kernel(place_ref, w0, w1, w2, w3, v0, v1, v2, v3, x_ref, wo_ref, first_ref, second_ref, wall, ctx):
    p = pl.program_id(0)

    @pl.when(p == 0)
    def _():
        place = place_ref[0]
        for step, w in enumerate((w0, w1, w2, w3)):
            wall[lax.rem(place + step, 4)] = w[...]

    start = pl.multiple_of(p * 128, 64)
    left = wall[lax.div(start, 192), pl.ds(pl.multiple_of(lax.rem(start, 192), 64), 64), :]
    start = start + 64
    right = wall[lax.div(start, 192), pl.ds(pl.multiple_of(lax.rem(start, 192), 64), 64), :]
    weights = jnp.concatenate([left, right], axis=0)
    values = jnp.concatenate([v0[0], v1[0], v2[0], v3[0]], axis=0)
    both = jnp.dot(weights, values, preferred_element_type=F32)
    first = first_head(I)
    for r in range(R):
        lanes = slice(r * 128, (r + 1) * 128)
        ctx[p, r * I : (r + 1) * I, :] = jnp.where(first, both[:I, lanes], both[I:, lanes]).astype(BF)

    @pl.when(p == PAIRS - 1)
    def _():
        context = jnp.concatenate([ctx[n] for n in range(PAIRS)], axis=1)
        update = jnp.dot(context, wo_ref[...], preferred_element_type=F32)
        after = (x_ref[...].astype(F32).reshape(R * I, D) + update).astype(BF)
        swap = reorder(R, I // 2)
        for half, ref in enumerate((first_ref, second_ref)):
            part = jnp.concatenate(
                [after[r * I + half * 32 : r * I + half * 32 + 32] for r in range(R)], axis=0
            )
            ref[...] = jnp.dot(swap, part, preferred_element_type=F32).astype(BF)


def row_context(place, weights, values, x, wo):
    whole = pl.BlockSpec((192, 512), lambda p: (0, 0))
    value = pl.BlockSpec((1, 128, R * 128), lambda p: (p, 0, 0))
    half = pl.BlockSpec((R * I // 2, D), lambda p: (0, 0))
    return pl.pallas_call(
        context_kernel,
        grid=(PAIRS,),
        out_shape=(jax.ShapeDtypeStruct((R * I // 2, D), BF),) * 2,
        in_specs=[pl.BlockSpec(memory_space=pltpu.SMEM)]
        + [whole] * 4
        + [value] * 4
        + [pl.BlockSpec((R, I, D), lambda p: (0, 0, 0)), pl.BlockSpec((D, D), lambda p: (0, 0))],
        out_specs=(half, half),
        scratch_shapes=[pltpu.VMEM((4, 192, 512), BF), pltpu.VMEM((PAIRS, R * I, 128), BF)],
        compiler_params=params(),
        cost_estimate=cost(2e9, 1e7),
        name="row_context",
    )(place, *weights, *values, x, wo)


def column_kernel(x_ref, w_ref, wo_ref, out_ref):
    x = x_ref[...].astype(F32).reshape(256, D)
    normed = layer_norm(x).astype(BF)
    qkv = jnp.dot(normed, w_ref[...], preferred_element_type=F32).astype(BF)
    first = first_head(256)
    zero = jnp.zeros((256, 128), BF)
    pieces = []
    for p in range(PAIRS):
        q = qkv[:, p * 128 : (p + 1) * 128]
        k = qkv[:, D + p * 128 : D + (p + 1) * 128]
        v = qkv[:, 2 * D + p * 128 : 2 * D + (p + 1) * 128]
        both = jnp.concatenate([jnp.where(first, q, zero), jnp.where(first, zero, q)], axis=0)
        scores = lax.dot_general(both, k, NT, preferred_element_type=F32)
        top = jnp.max(scores, axis=-1, keepdims=True)
        powers = jnp.exp2((scores - top) * (64**-0.5 * LOG2E))
        total = jnp.sum(powers, axis=-1, keepdims=True)
        mixed = jnp.dot(powers.astype(BF), v, preferred_element_type=F32) / total
        pieces.append(jnp.where(first, mixed[:256], mixed[256:]).astype(BF))
    context = jnp.concatenate(pieces, axis=1)
    update = jnp.dot(context, wo_ref[...], preferred_element_type=F32)
    out_ref[...] = (x + update).reshape(32, R, D).astype(BF)


def attend_column(x, w, wo):
    return pl.pallas_call(
        column_kernel,
        out_shape=jax.ShapeDtypeStruct((32, R, D), BF),
        in_specs=[VMEM] * 3,
        out_specs=VMEM,
        compiler_params=params(),
        cost_estimate=cost(2.5e9, 6e6, 800000),
        name="column",
    )(x, w, wo)


def finish_kernel(first_ref, second_ref, out_ref):
    swap = reorder(I // 2, R)
    for half, ref in enumerate((first_ref, second_ref)):
        rows = jnp.dot(swap, ref[...], preferred_element_type=F32).astype(BF)
        for r in range(R):
            out_ref[r, half * 32 : half * 32 + 32, :] = rows[r * 32 : r * 32 + 32]


def finish(first, second):
    return pl.pallas_call(
        finish_kernel,
        out_shape=jax.ShapeDtypeStruct((R, I, D), BF),
        in_specs=[VMEM] * 2,
        out_specs=VMEM,
        compiler_params=params(),
        cost_estimate=cost(4e8, 1.6e6),
        name="finish",
    )(first, second)


def shift(n, by):
    return [(i, (i + by) % n) for i in range(n)]


def per_device(x, w_row, wo_row, w_col, wo_col):
    seq = ("x", "z")
    other = functools.partial(lax.ppermute, axis_name="core", perm=shift(2, 1))
    partner = other(x)
    below = lax.ppermute(x, "y", shift(4, 1))
    above = lax.ppermute(x, "y", shift(4, 3))
    across = lax.ppermute(x, "y", shift(4, 2))
    q = masked_queries(x, w_row)
    parts = []
    values = []
    for own, mate in ((x, partner), (below, None), (above, None), (across, None)):
        mate = other(own) if mate is None else mate
        logits, v = keys_values(own, mate, w_row, q)
        values.append(v)
        logits = logits.reshape(32, 24, 128)
        parts.append(lax.all_to_all(logits, seq, 0, 0, tiled=True))
    scale = float((64 * 256) ** -0.5)
    copies = row_weights(parts, scale, 8)
    mine = lax.all_to_all(copies, "z", 0, 0, tiled=True).reshape(192, 512)
    weights = [mine] + [lax.ppermute(mine, "x", shift(4, -k)) for k in (1, 2, 3)]
    place = lax.axis_index("x").astype(jnp.int32).reshape(1)
    halves = row_context(place, weights, values, x, wo_row)
    done = []
    for half in halves:
        column = lax.all_to_all(half.reshape(32, R, D), seq, 0, 0, tiled=True)
        column = attend_column(column, w_col, wo_col)
        done.append(lax.all_to_all(column, seq, 0, 0, tiled=True).reshape(256, D))
    return finish(*done)


def solution(mesh):
    chips = Mesh(mesh.devices.reshape(4, 8, 4, 2), ("x", "z", "y", "core"))
    rows = P(("x", "z"), ("y", "core"), None)
    return jax.shard_map(
        per_device, mesh=chips, in_specs=(rows, P(), P(), P(), P()), out_specs=rows, check_vma=False
    )
```

time: 375 us -> 251 us (0.67)
  the two profiles are of different devices: /device:TPU:32 before, /device:TPU:56 now
where the time goes in v1:
time: 251 us; the launch traced here: 250 us
  blocking collectives  65.7 us (26%)
  waiting for transfers between devices  56.7 us (23%)
  Pallas kernels  55.7 us (22%)
  starting transfers between devices  45.9 us (18%)
  local copies, waits for them, and re-layouts  25.6 us (10%)
    pallas_call x4, Pallas kernels, keys_values(): pl.pallas_call(pair_kernel, grid=(R // 2,), out_shape=(jax.ShapeDtypeStru...  40.4 us
    all_to_all x3, starting transfers between devices, per_device(): parts.append(lax.all_to_all(logits, seq, 0, 0, tiled=True))  30.9 us
    unnamed x48, local copies, waits for them, and re-layouts  25.6 us
    all_to_all x1, blocking collectives, per_device(): parts.append(lax.all_to_all(logits, seq, 0, 0, tiled=True))  20.4 us
    ppermute x1, waiting for transfers between devices, per_device(): below = lax.ppermute(x, 'y', shift(4, 1))  17.5 us
    all_to_all x1, blocking collectives, per_device(): column = lax.all_to_all(half.reshape(32, R, D), seq, 0, 0, tiled=True)  17 us
    ppermute x1, waiting for transfers between devices, per_device(): above = lax.ppermute(x, 'y', shift(4, 3))  16.9 us
    all_to_all x1, blocking collectives, per_device(): done.append(lax.all_to_all(column, seq, 0, 0, tiled=True).reshape(256, D))  16.6 us
  transfers between devices with their start and end apart: 15, of which 7 were waited for; matrix products, arithmetic and copies ran while one was open for 0% of the time, Pallas kernels for 20%

profile of v1, /device:TPU:56, one launch (start us, length us, event | category | flops | bytes accessed | tf_op | source)
XLA Modules:
  0.0 249.8 jit_solution(333574777330243349)
XLA Ops:
  0.2 1.8 collective-permute-start.3
  3.3 17.5 %collective-permute-done.1.a_ref = bf16[8,64,768]{2,1,0:T(8,128)(2,1)} collective-permute-done((bf16[8,64,768]{2,1,0:T(8,128)(2,1)}, bf16[8,64,768]{2,1,0:T(8,128)(2,1)}, u32[]{:S(2)}, u32[]{:S(2)}) %collective-permute-start.1) | collective-permute-done | bytes 786464 | tf_op jit(solution)/shard_map/ppermute | solution.py:282
  20.7 16.9 %collective-permute-done.3.a_ref = bf16[8,64,768]{2,1,0:T(8,128)(2,1)} collective-permute-done((bf16[8,64,768]{2,1,0:T(8,128)(2,1)}, bf16[8,64,768]{2,1,0:T(8,128)(2,1)}, u32[]{:S(2)}, u32[]{:S(2)}) %collective-permute-start.3) | collective-permute-done | bytes 786464 | tf_op jit(solution)/shard_map/ppermute | solution.py:283
  37.7 2.0 copy-done
  40.8 2.4 queries.1.q_ref
  43.2 9.5 %keys_values.4 = (bf16[6,128,128]{2,1,0:T(8,128)(2,1)S(1)}, bf16[6,128,1024]{2,1,0:T(8,128)(2,1)S(1)}) custom-call(bf16[8,64,768]{2,1,0:T(8,128)(2,1)S(1)} %copy-done.6, bf16[8,64,768]{2,1,0:T(8,128)(2,1)S(1)} %collective-permute-done.b_ref, bf16[768,2304]{1,0:T(8,128)(2,1)S(1)} %copy-done, bf16[768,2304]{1,0:T(8,128)(2,1)S(1)} %copy-done, ...), custom_call_target="tpu_custom_call" | custom-call | flops 2617245696 | bytes 8000000 | tf_op jit(solution)/shard_map/keys_values/pallas_call | solution.py:107
  54.6 11.2 %all-to-all-start = ((bf16[32,24,128]{2,1,0:T(8,128)(2,1)}), bf16[32,24,128]{2,1,0:T(8,128)(2,1)}, u32[]{:S(2)}, u32[]{:S(2)}) async-start(bf16[32,24,128]{2,1,0:T(8,128)(2,1)} %bitcast.17), calls=%async_computation | async-start | bytes 393216 | tf_op jit(solution)/shard_map/all_to_all | solution.py:293
  67.4 10.3 %keys_values.5 = (bf16[6,128,128]{2,1,0:T(8,128)(2,1)S(1)}, bf16[6,128,1024]{2,1,0:T(8,128)(2,1)S(1)}) custom-call(bf16[8,64,768]{2,1,0:T(8,128)(2,1)} %collective-permute-done.1.a_ref, bf16[8,64,768]{2,1,0:T(8,128)(2,1)} %collective-permute-done.2.b_ref, bf16[768,2304]{1,0:T(8,128)(2,1)S(1)} %copy-done.1, bf16[768,2304]{1,0:T(8,128)(2,1)S(1)} %copy-done.1, ...), custom_call_target="tpu_custom_call" | custom-call | flops 2617245696 | bytes 8000000 | tf_op jit(solution)/shard_map/keys_values/pallas_call | solution.py:107
  79.5 9.8 %all-to-all-start.1 = ((bf16[32,24,128]{2,1,0:T(8,128)(2,1)}), bf16[32,24,128]{2,1,0:T(8,128)(2,1)}, u32[]{:S(2)}, u32[]{:S(2)}) async-start(bf16[32,24,128]{2,1,0:T(8,128)(2,1)} %bitcast.19), calls=%async_computation.1 | async-start | bytes 393216 | tf_op jit(solution)/shard_map/all_to_all | solution.py:293
  90.8 10.3 %keys_values.6 = (bf16[6,128,128]{2,1,0:T(8,128)(2,1)S(1)}, bf16[6,128,1024]{2,1,0:T(8,128)(2,1)S(1)}) custom-call(bf16[8,64,768]{2,1,0:T(8,128)(2,1)} %collective-permute-done.3.a_ref, bf16[8,64,768]{2,1,0:T(8,128)(2,1)} %collective-permute-done.4.b_ref, bf16[768,2304]{1,0:T(8,128)(2,1)S(1)} %copy-done.1, bf16[768,2304]{1,0:T(8,128)(2,1)S(1)} %copy-done.1, ...), custom_call_target="tpu_custom_call" | custom-call | flops 2617245696 | bytes 8000000 | tf_op jit(solution)/shard_map/keys_values/pallas_call | solution.py:107
  102.9 9.8 %all-to-all-start.2 = ((bf16[32,24,128]{2,1,0:T(8,128)(2,1)}), bf16[32,24,128]{2,1,0:T(8,128)(2,1)}, u32[]{:S(2)}, u32[]{:S(2)}) async-start(bf16[32,24,128]{2,1,0:T(8,128)(2,1)} %bitcast.18), calls=%async_computation.2 | async-start | bytes 393216 | tf_op jit(solution)/shard_map/all_to_all | solution.py:293
  114.2 10.3 %keys_values.7 = (bf16[6,128,128]{2,1,0:T(8,128)(2,1)S(1)}, bf16[6,128,1024]{2,1,0:T(8,128)(2,1)S(1)}) custom-call(bf16[8,64,768]{2,1,0:T(8,128)(2,1)} %collective-permute-done.5.a_ref, bf16[8,64,768]{2,1,0:T(8,128)(2,1)} %collective-permute-done.6.b_ref, bf16[768,2304]{1,0:T(8,128)(2,1)S(1)} %copy-done.1, bf16[768,2304]{1,0:T(8,128)(2,1)S(1)} %copy-done.1, ...), custom_call_target="tpu_custom_call" | custom-call | flops 2617245696 | bytes 8000000 | tf_op jit(solution)/shard_map/keys_values/pallas_call | solution.py:107
  126.4 20.4 %all_to_all.45.refs_3_ = bf16[32,24,128]{2,1,0:T(8,128)(2,1)S(1)} all-to-all(bf16[32,24,128]{2,1,0:T(8,128)(2,1)} %bitcast.20), channel_id=1, replica_groups=mesh['x'=4,'z'=8,'y'=4,'core'=2] {'x','z'}, dimensions={0} | all-to-all | bytes 393216 | tf_op jit(solution)/shard_map/all_to_all | solution.py:293
  146.8 1.4 row_weights.1
  148.2 11.6 %all_to_all.46 = bf16[8,24,512]{2,1,0:T(8,128)(2,1)S(1)} all-to-all(bf16[8,24,512]{2,1,0:T(8,128)(2,1)S(1)} %row_weights.1), channel_id=1, replica_groups=mesh['x'=4,'z'=8,'y'=4,'core'=2] {'z'}, dimensions={0} | all-to-all | bytes 393216 | tf_op jit(solution)/shard_map/all_to_all | solution.py:296
  161.0 1.5 collective-permute-start.8
  162.6 3.1 %collective-permute-done.7.w1 = bf16[192,512]{1,0:T(8,128)(2,1)S(1)} collective-permute-done((bf16[192,512]{1,0:T(8,128)(2,1)S(1)}, bf16[192,512]{1,0:T(8,128)(2,1)S(1)}, u32[]{:S(2)}, u32[]{:S(2)}) %collective-permute-start.7) | collective-permute-done | bytes 196640 | tf_op jit(solution)/shard_map/ppermute | solution.py:297
  165.7 2.6 %collective-permute-done.8.w2 = bf16[192,512]{1,0:T(8,128)(2,1)S(1)} collective-permute-done((bf16[192,512]{1,0:T(8,128)(2,1)S(1)}, bf16[192,512]{1,0:T(8,128)(2,1)S(1)}, u32[]{:S(2)}, u32[]{:S(2)}) %collective-permute-start.8) | collective-permute-done | bytes 196640 | tf_op jit(solution)/shard_map/ppermute | solution.py:297
  168.3 2.0 collective-permute-done.9.w3
  170.3 1.4 copy-done.9
  171.7 1.4 copy-done.11
  177.2 4.1 %row_context.1 = (bf16[256,768]{1,0:T(8,128)(2,1)S(1)}, bf16[256,768]{1,0:T(8,128)(2,1)}) custom-call(s32[1]{0:T(128)} %bitcast.place_ref, bf16[192,512]{1,0:T(8,128)(2,1)S(1)} %bitcast.15, bf16[192,512]{1,0:T(8,128)(2,1)S(1)} %collective-permute-done.7.w1, bf16[192,512]{1,0:T(8,128)(2,1)S(1)} %collective-permute-done.8.w2, ...), custom_call_target="tpu_custom_call" | custom-call | flops 2000000000 | bytes 10000000 | tf_op jit(solution)/shard_map/row_context/pallas_call | solution.py:203
  181.3 17.0 %all_to_all.47.x_ref = bf16[32,8,768]{2,1,0:T(8,128)(2,1)S(1)} all-to-all(bf16[32,8,768]{2,1,0:T(8,128)(2,1)S(1)} %bitcast.16), channel_id=1, replica_groups=mesh['x'=4,'z'=8,'y'=4,'core'=2] {'x','z'}, dimensions={0} | all-to-all | bytes 786432 | tf_op jit(solution)/shard_map/all_to_all | solution.py:302
  198.4 4.4 %all-to-all-start.7 = ((bf16[32,8,768]{2,1,0:T(8,128)(2,1)}), bf16[32,8,768]{2,1,0:T(8,128)(2,1)S(1)}, u32[]{:S(2)}, u32[]{:S(2)}) async-start(bf16[32,8,768]{2,1,0:T(8,128)(2,1)} %bitcast.8), calls=%async_computation.7 | async-start | bytes 786432 | tf_op jit(solution)/shard_map/all_to_all | solution.py:302
  202.8 2.0 copy-done.21
  204.7 3.4 %column.2 = bf16[32,8,768]{2,1,0:T(8,128)(2,1)} custom-call(bf16[32,8,768]{2,1,0:T(8,128)(2,1)S(1)} %all_to_all.47.x_ref, bf16[768,2304]{1,0:T(8,128)(2,1)S(1)} %copy-done.21, bf16[768,768]{1,0:T(8,128)(2,1)S(1)} %copy-done.23), custom_call_target="tpu_custom_call" | custom-call | flops 2500000000 | bytes 6000000 | tf_op jit(solution)/shard_map/column/pallas_call | solution.py:243
  208.2 6.9 %all-to-all-done.7.x_ref = bf16[32,8,768]{2,1,0:T(8,128)(2,1)S(1)} async-done(((bf16[32,8,768]{2,1,0:T(8,128)(2,1)}), bf16[32,8,768]{2,1,0:T(8,128)(2,1)S(1)}, u32[]{:S(2)}, u32[]{:S(2)}) %all-to-all-start.7) | async-done | bytes 393248 | tf_op jit(solution)/shard_map/all_to_all | solution.py:302
  215.1 4.5 %all-to-all-start.6 = ((bf16[32,8,768]{2,1,0:T(8,128)(2,1)}), bf16[32,8,768]{2,1,0:T(8,128)(2,1)S(1)}, u32[]{:S(2)}, u32[]{:S(2)}) async-start(bf16[32,8,768]{2,1,0:T(8,128)(2,1)} %column.2), calls=%async_computation.6 | async-start | bytes 786432 | tf_op jit(solution)/shard_map/all_to_all | solution.py:304
  219.6 2.0 copy-done.22
  221.6 2.7 %column.3 = bf16[32,8,768]{2,1,0:T(8,128)(2,1)S(1)} custom-call(bf16[32,8,768]{2,1,0:T(8,128)(2,1)S(1)} %all-to-all-done.7.x_ref, bf16[768,2304]{1,0:T(8,128)(2,1)S(1)} %copy-done.22, bf16[768,768]{1,0:T(8,128)(2,1)S(1)} %copy-done.23), custom_call_target="tpu_custom_call" | custom-call | flops 2500000000 | bytes 6000000 | tf_op jit(solution)/shard_map/column/pallas_call | solution.py:243
  224.3 7.7 %all-to-all-done.6 = bf16[32,8,768]{2,1,0:T(8,128)(2,1)S(1)} async-done(((bf16[32,8,768]{2,1,0:T(8,128)(2,1)}), bf16[32,8,768]{2,1,0:T(8,128)(2,1)S(1)}, u32[]{:S(2)}, u32[]{:S(2)}) %all-to-all-start.6) | async-done | bytes 393248 | tf_op jit(solution)/shard_map/all_to_all | solution.py:304
  232.0 16.6 %all_to_all.48 = bf16[32,8,768]{2,1,0:T(8,128)(2,1)S(1)} all-to-all(bf16[32,8,768]{2,1,0:T(8,128)(2,1)S(1)} %column.3), channel_id=1, replica_groups=mesh['x'=4,'z'=8,'y'=4,'core'=2] {'x','z'}, dimensions={0} | all-to-all | bytes 786432 | tf_op jit(solution)/shard_map/all_to_all | solution.py:304
  (60 shorter events, 20.9 us)
Async XLA Ops:
  0.0 20.7 %collective-permute-start.1 = (bf16[8,64,768]{2,1,0:T(8,128)(2,1)}, bf16[8,64,768]{2,1,0:T(8,128)(2,1)}, u32[]{:S(2)}, u32[]{:S(2)}) collective-permute-start(bf16[8,64,768]{2,1,0:T(8,128)(2,1)} %x_ref.3), channel_id=1, source_target_pairs={{0,2},{2,4},{4,6},{6,0},{1,3},{3,5},{5,7},{7,1},{8,10},{10,12},{12... | collective-permute-start | bytes 2359304 | tf_op jit(solution)/shard_map/ppermute | solution.py:282
  0.2 37.4 %collective-permute-start.3 = (bf16[8,64,768]{2,1,0:T(8,128)(2,1)}, bf16[8,64,768]{2,1,0:T(8,128)(2,1)}, u32[]{:S(2)}, u32[]{:S(2)}) collective-permute-start(bf16[8,64,768]{2,1,0:T(8,128)(2,1)} %x_ref.3), channel_id=1, source_target_pairs={{0,6},{2,0},{4,2},{6,4},{1,7},{3,1},{5,3},{7,5},{8,14},{10,8},{12,... | collective-permute-start | bytes 2359304 | tf_op jit(solution)/shard_map/ppermute | solution.py:283
  2.0 41.2 %collective-permute-start = (bf16[8,64,768]{2,1,0:T(8,128)(2,1)}, bf16[8,64,768]{2,1,0:T(8,128)(2,1)S(1)}, u32[]{:S(2)}, u32[]{:S(2)}) collective-permute-start(bf16[8,64,768]{2,1,0:T(8,128)(2,1)} %x_ref.3), channel_id=1, source_target_pairs={{0,1},{1,0},{2,3},{3,2},{4,5},{5,4},{6,7},{7,6},{8,9},{9,8},{10,11... | collective-permute-start | bytes 2359304 | tf_op jit(solution)/shard_map/ppermute | solution.py:281
  2.0 63.8 %collective-permute-start.5 = (bf16[8,64,768]{2,1,0:T(8,128)(2,1)}, bf16[8,64,768]{2,1,0:T(8,128)(2,1)}, u32[]{:S(2)}, u32[]{:S(2)}) collective-permute-start(bf16[8,64,768]{2,1,0:T(8,128)(2,1)} %x_ref.3), channel_id=1, source_target_pairs={{0,4},{2,6},{4,0},{6,2},{1,5},{3,7},{5,1},{7,3},{8,12},{10,14},{12... | collective-permute-start | bytes 2359304 | tf_op jit(solution)/shard_map/ppermute | solution.py:284
  20.7 45.2 %collective-permute-start.2 = (bf16[8,64,768]{2,1,0:T(8,128)(2,1)}, bf16[8,64,768]{2,1,0:T(8,128)(2,1)}, u32[]{:S(2)}, u32[]{:S(2)}) collective-permute-start(bf16[8,64,768]{2,1,0:T(8,128)(2,1)} %collective-permute-done.1.a_ref), channel_id=1, source_target_pairs={{0,1},{1,0},{2,3},{3,2},{4,5},{5,4},{6,7},{7,6},{8,9},{9,8},{10,11... | collective-permute-start | bytes 2359304 | tf_op jit(solution)/shard_map/ppermute | solution.py:289
  37.7 51.7 %collective-permute-start.4 = (bf16[8,64,768]{2,1,0:T(8,128)(2,1)}, bf16[8,64,768]{2,1,0:T(8,128)(2,1)}, u32[]{:S(2)}, u32[]{:S(2)}) collective-permute-start(bf16[8,64,768]{2,1,0:T(8,128)(2,1)} %collective-permute-done.3.a_ref), channel_id=1, source_target_pairs={{0,1},{1,0},{2,3},{3,2},{4,5},{5,4},{6,7},{7,6},{8,9},{9,8},{10,11... | collective-permute-start | bytes 2359304 | tf_op jit(solution)/shard_map/ppermute | solution.py:289
  37.7 2.0 copy-start
  43.2 9.6 %copy-start.2 = (bf16[6,128,1024]{2,1,0:T(8,128)(2,1)}, bf16[6,128,1024]{2,1,0:T(8,128)(2,1)S(1)}, u32[]{:S(2)}) copy-start(bf16[6,128,1024]{2,1,0:T(8,128)(2,1)S(1)} %queries.1.q_ref) | copy-start | bytes 4718596
  43.2 22.8 %copy-start.1 = (bf16[768,2304]{1,0:T(8,128)(2,1)S(1)}, bf16[768,2304]{1,0:T(8,128)(2,1)}, u32[]{:S(2)}) copy-start(bf16[768,2304]{1,0:T(8,128)(2,1)} %wv_ref.7) | copy-start | bytes 10616836
  52.8 1.2 copy-start.8
  54.6 24.9 %all-to-all-start = ((bf16[32,24,128]{2,1,0:T(8,128)(2,1)}), bf16[32,24,128]{2,1,0:T(8,128)(2,1)}, u32[]{:S(2)}, u32[]{:S(2)}) async-start(bf16[32,24,128]{2,1,0:T(8,128)(2,1)} %bitcast.17), calls=%async_computation | async-start | bytes 393216 | tf_op jit(solution)/shard_map/all_to_all | solution.py:293
  65.9 46.9 %collective-permute-start.6 = (bf16[8,64,768]{2,1,0:T(8,128)(2,1)}, bf16[8,64,768]{2,1,0:T(8,128)(2,1)}, u32[]{:S(2)}, u32[]{:S(2)}) collective-permute-start(bf16[8,64,768]{2,1,0:T(8,128)(2,1)} %collective-permute-done.5.a_ref), channel_id=1, source_target_pairs={{0,1},{1,0},{2,3},{3,2},{4,5},{5,4},{6,7},{7,6},{8,9},{9,8},{10,11... | collective-permute-start | bytes 2359304 | tf_op jit(solution)/shard_map/ppermute | solution.py:289
  66.0 1.4 copy-start.3
  79.5 23.4 %all-to-all-start.1 = ((bf16[32,24,128]{2,1,0:T(8,128)(2,1)}), bf16[32,24,128]{2,1,0:T(8,128)(2,1)}, u32[]{:S(2)}, u32[]{:S(2)}) async-start(bf16[32,24,128]{2,1,0:T(8,128)(2,1)} %bitcast.19), calls=%async_computation.1 | async-start | bytes 393216 | tf_op jit(solution)/shard_map/all_to_all | solution.py:293
  89.4 1.4 copy-start.4
  102.9 23.4 %all-to-all-start.2 = ((bf16[32,24,128]{2,1,0:T(8,128)(2,1)}), bf16[32,24,128]{2,1,0:T(8,128)(2,1)}, u32[]{:S(2)}, u32[]{:S(2)}) async-start(bf16[32,24,128]{2,1,0:T(8,128)(2,1)} %bitcast.18), calls=%async_computation.2 | async-start | bytes 393216 | tf_op jit(solution)/shard_map/all_to_all | solution.py:293
  112.8 1.4 copy-start.5
  124.5 1.2 copy-start.14
  126.4 43.9 %copy-start.7 = (bf16[8,64,768]{2,1,0:T(8,128)(2,1)S(1)}, bf16[8,64,768]{2,1,0:T(8,128)(2,1)}, u32[]{:S(2)}) copy-start(bf16[8,64,768]{2,1,0:T(8,128)(2,1)} %x_ref.3) | copy-start | bytes 2359300
  159.8 5.8 %collective-permute-start.7 = (bf16[192,512]{1,0:T(8,128)(2,1)S(1)}, bf16[192,512]{1,0:T(8,128)(2,1)S(1)}, u32[]{:S(2)}, u32[]{:S(2)}) collective-permute-start(bf16[192,512]{1,0:T(8,128)(2,1)S(1)} %bitcast.12), channel_id=1, source_target_pairs={{0,192},{64,0},{128,64},{192,128},{1,193},{65,1},{129,65},{193,129... | collective-permute-start | bytes 589832 | tf_op jit(solution)/shard_map/ppermute | solution.py:297
  161.0 7.3 %collective-permute-start.8 = (bf16[192,512]{1,0:T(8,128)(2,1)S(1)}, bf16[192,512]{1,0:T(8,128)(2,1)S(1)}, u32[]{:S(2)}, u32[]{:S(2)}) collective-permute-start(bf16[192,512]{1,0:T(8,128)(2,1)S(1)} %bitcast.13), channel_id=1, source_target_pairs={{0,128},{64,192},{128,0},{192,64},{1,129},{65,193},{129,1},{193,65... | collective-permute-start | bytes 589832 | tf_op jit(solution)/shard_map/ppermute | solution.py:297
  162.5 7.8 %collective-permute-start.9 = (bf16[192,512]{1,0:T(8,128)(2,1)S(1)}, bf16[192,512]{1,0:T(8,128)(2,1)S(1)}, u32[]{:S(2)}, u32[]{:S(2)}) collective-permute-start(bf16[192,512]{1,0:T(8,128)(2,1)S(1)} %bitcast.14), channel_id=1, source_target_pairs={{0,64},{64,128},{128,192},{192,0},{1,65},{65,129},{129,193},{193,1... | collective-permute-start | bytes 589832 | tf_op jit(solution)/shard_map/ppermute | solution.py:297
  170.3 1.4 copy-start.9
  171.7 1.4 copy-start.11
  173.1 1.4 copy-start.13
  174.5 1.4 copy-start.15
  175.9 1.3 copy-start.16
  181.3 21.4 %copy-start.23 = (bf16[768,768]{1,0:T(8,128)(2,1)S(1)}, bf16[768,768]{1,0:T(8,128)(2,1)}, u32[]{:S(2)}) copy-start(bf16[768,768]{1,0:T(8,128)(2,1)} %wo_ref.5) | copy-start | bytes 3538948
  198.4 16.7 %all-to-all-start.7 = ((bf16[32,8,768]{2,1,0:T(8,128)(2,1)}), bf16[32,8,768]{2,1,0:T(8,128)(2,1)S(1)}, u32[]{:S(2)}, u32[]{:S(2)}) async-start(bf16[32,8,768]{2,1,0:T(8,128)(2,1)} %bitcast.8), calls=%async_computation.7 | async-start | bytes 786432 | tf_op jit(solution)/shard_map/all_to_all | solution.py:302
  202.7 2.0 copy-start.21
  215.1 16.9 %all-to-all-start.6 = ((bf16[32,8,768]{2,1,0:T(8,128)(2,1)}), bf16[32,8,768]{2,1,0:T(8,128)(2,1)S(1)}, u32[]{:S(2)}, u32[]{:S(2)}) async-start(bf16[32,8,768]{2,1,0:T(8,128)(2,1)} %column.2), calls=%async_computation.6 | async-start | bytes 786432 | tf_op jit(solution)/shard_map/all_to_all | solution.py:304
  219.6 2.0 copy-start.22
  (7 other events, 6.2 us)

commit v2 on v1

v2 whole, which is shorter than its diff:
```python
import functools

import jax
import jax.numpy as jnp
from jax import lax
from jax.experimental import pallas as pl
from jax.experimental.pallas import tpu as pltpu
from jax.sharding import Mesh, PartitionSpec as P

HEADS = 12
PAIRS = 6
D = 768
R = 8
I = 64
EPS = 1e-05
LOG2E = 1.4426950408889634
NT = (((1,), (1,)), ((), ()))
BF = jnp.bfloat16
F32 = jnp.float32
VMEM = pl.BlockSpec(memory_space=pltpu.VMEM)
MB = 1024 * 1024


def params(limit=48 * MB):
    return pltpu.CompilerParams(vmem_limit_bytes=limit)


def cost(flops, bytes_accessed, transcendentals=0):
    return pl.CostEstimate(
        flops=int(flops), bytes_accessed=int(bytes_accessed), transcendentals=int(transcendentals)
    )


def layer_norm(x):
    mean = jnp.mean(x, axis=-1, keepdims=True)
    centered = x - mean
    spread = jnp.mean(centered * centered, axis=-1, keepdims=True)
    return centered * lax.rsqrt(spread + EPS)


def first_head(rows):
    return lax.broadcasted_iota(jnp.int32, (rows, 128), 1) < 64


def store_block(ref, at, first, rows):
    for p in range(PAIRS):
        for r in range(rows.shape[0] // I):
            lanes = (first + r) * 128
            piece = rows[r * I : (r + 1) * I, p * 128 : (p + 1) * 128]
            ref[p, at : at + I, lanes : lanes + 128] = piece


def store_logits(place_ref, q_ref, keys, rows, out_refs):
    first = lax.rem(lax.broadcasted_iota(jnp.int32, (I, R * 128), 1), 128) < 64
    zero = jnp.zeros((I, R * 128), BF)
    core, place = place_ref[0], place_ref[1]
    for p in range(PAIRS):
        masked = []
        for part in range(2):
            q = q_ref[p, part * I : (part + 1) * I]
            masked += [jnp.where(first, q, zero), jnp.where(first, zero, q)]
        logits = lax.dot_general(
            jnp.concatenate(masked, axis=0), keys[p], NT, preferred_element_type=F32
        )
        for n in range(4):
            group, at = divmod(2 * p + n % 2, 3)
            owner = core if n < 2 else 1 - core
            rows[owner, group, at * I : (at + 1) * I] = logits[n * I : (n + 1) * I]
    for k, ref in enumerate(out_refs):
        group = lax.rem(place + k, 4)
        both = [rows[c, group].reshape(8, 24, 128) for c in range(2)]
        ref[...] = jnp.concatenate(both, axis=1).astype(BF)


def normed_rows(ref, s):
    return layer_norm(ref[4 * s : 4 * s + 4].astype(F32).reshape(4 * I, D)).astype(BF)


def project(rows, w_ref):
    return jnp.dot(rows, w_ref[...], preferred_element_type=F32).astype(BF)


def own_kernel(x_ref, mate_ref, wq_ref, wk_ref, wv_ref, q_ref, k_ref, v_ref):
    for s in range(2):
        rows = normed_rows(x_ref, s)
        store_block(q_ref, 0, 4 * s, project(rows, wq_ref))
        store_block(k_ref, 0, 4 * s, project(rows, wk_ref))
        store_block(v_ref, 0, 4 * s, project(rows, wv_ref))
        store_block(q_ref, I, 4 * s, project(normed_rows(mate_ref, s), wq_ref))


def near_kernel(place_ref, key_ref, a_ref, b_ref, wk_ref, q_ref, wv_ref, *refs):
    out_refs, (v_ref, bkey_ref, keys, rows) = refs[:4], refs[4:]
    keys[:, :I] = key_ref[...]
    for s in range(2):
        normed = normed_rows(a_ref, s)
        store_block(keys, I, 4 * s, project(normed, wk_ref))
        store_block(v_ref, 0, 4 * s, project(normed, wv_ref))
    store_logits(place_ref, q_ref, keys, rows, out_refs)
    for s in range(2):
        normed = normed_rows(b_ref, s)
        store_block(bkey_ref, 0, 4 * s, project(normed, wk_ref))
        store_block(v_ref, I, 4 * s, project(normed, wv_ref))


def far_kernel(place_ref, key_ref, far_ref, wk_ref, q_ref, *refs):
    out_refs, (keys, rows) = refs[:4], refs[4:]
    keys[:, :I] = key_ref[...]
    for s in range(2):
        store_block(keys, I, 4 * s, project(normed_rows(far_ref, s), wk_ref))
    store_logits(place_ref, q_ref, keys, rows, out_refs)


def value_kernel(far_ref, wv_ref, v_ref):
    for s in range(2):
        store_block(v_ref, 0, 4 * s, project(normed_rows(far_ref, s), wv_ref))


SMEM = pl.BlockSpec(memory_space=pltpu.SMEM)


def block(*shape):
    return pl.BlockSpec(shape, lambda s: (0,) * len(shape))


def weight(part):
    return pl.BlockSpec((D, D), lambda s: (0, part))


LOGITS = jax.ShapeDtypeStruct((8, 48, 128), BF)
ONE = jax.ShapeDtypeStruct((PAIRS, I, R * 128), BF)
TWO = jax.ShapeDtypeStruct((PAIRS, 2 * I, R * 128), BF)
ROWS = pltpu.VMEM((2, 4, 192, 128), F32)
KEYS = pltpu.VMEM((PAIRS, 128, R * 128), BF)


def own_projections(x, mate, w):
    whole, one, two = block(R, I, D), block(*ONE.shape), block(*TWO.shape)
    return pl.pallas_call(
        own_kernel,
        grid=(1,),
        out_shape=(TWO, ONE, ONE),
        in_specs=[whole, whole, weight(0), weight(1), weight(2)],
        out_specs=(two, one, one),
        compiler_params=params(64 * MB),
        cost_estimate=cost(2.4e9, 9e6),
        name="own_projections",
    )(x, mate, w, w, w)


def near_logits(place, keys, a, b, w, q):
    whole, one, two = block(R, I, D), block(*ONE.shape), block(*TWO.shape)
    return pl.pallas_call(
        near_kernel,
        grid=(1,),
        out_shape=[LOGITS] * 4 + [TWO, ONE],
        in_specs=[SMEM, one, whole, whole, weight(1), two, weight(2)],
        out_specs=[block(8, 48, 128)] * 4 + [two, one],
        scratch_shapes=[KEYS, ROWS],
        compiler_params=params(64 * MB),
        cost_estimate=cost(4e9, 9e6),
        name="near_logits",
    )(place, keys, a, b, w, q, w)


def far_logits(place, keys, far, w, q):
    return pl.pallas_call(
        far_kernel,
        grid=(1,),
        out_shape=[LOGITS] * 4,
        in_specs=[SMEM, block(*ONE.shape), block(R, I, D), weight(1), block(*TWO.shape)],
        out_specs=[block(8, 48, 128)] * 4,
        scratch_shapes=[KEYS, ROWS],
        compiler_params=params(64 * MB),
        cost_estimate=cost(2e9, 6e6),
        name="far_logits",
    )(place, keys, far, w, q)


def far_values(far, w):
    return pl.pallas_call(
        value_kernel,
        grid=(1,),
        out_shape=ONE,
        in_specs=[block(R, I, D), weight(2)],
        out_specs=block(*ONE.shape),
        compiler_params=params(64 * MB),
        cost_estimate=cost(1.2e9, 4e6),
        name="far_values",
    )(far, w)


def gather_kernel(*refs):
    out_ref = refs[-1]
    for half in range(2):
        total = refs[4 * half][...].astype(F32)
        for ref in refs[4 * half + 1 : 4 * half + 4]:
            total += ref[...].astype(F32)
        out_ref[:, :, half * 128 : half * 128 + 128] = total.astype(BF)


def sum_x(near, far):
    return pl.pallas_call(
        gather_kernel,
        out_shape=jax.ShapeDtypeStruct((8, 48, 256), BF),
        in_specs=[VMEM] * 8,
        out_specs=VMEM,
        compiler_params=params(64 * MB),
        cost_estimate=cost(1e6, 1e6),
        name="sum_x",
    )(*near, *far)


def sum_kernel(place_ref, parts_ref, mine_ref, mates_ref, rows):
    rows[...] = jnp.sum(parts_ref[...].astype(F32), axis=0).reshape(2, 24, 256)
    core = place_ref[0]
    mine_ref[...] = rows[core]
    mates_ref[...] = rows[1 - core]


def sum_z(place, parts):
    return pl.pallas_call(
        sum_kernel,
        out_shape=(jax.ShapeDtypeStruct((24, 256), F32),) * 2,
        in_specs=[SMEM, VMEM],
        out_specs=(VMEM, VMEM),
        scratch_shapes=[pltpu.VMEM((2, 24, 256), F32)],
        compiler_params=params(),
        cost_estimate=cost(1e6, 1e6),
        name="sum_z",
    )(place, parts)


def weight_kernel(scale, copies, near_ref, far_ref, out_ref):
    logits = jnp.concatenate([near_ref[...], far_ref[...]], axis=1)
    top = jnp.max(logits, axis=-1, keepdims=True)
    powers = jnp.exp2((logits - top) * (scale * LOG2E))
    weights = (powers / jnp.sum(powers, axis=-1, keepdims=True)).astype(BF)
    for c in range(copies):
        out_ref[c] = weights


def row_weights(own, mates, scale, copies):
    return pl.pallas_call(
        functools.partial(weight_kernel, scale, copies),
        out_shape=jax.ShapeDtypeStruct((copies, 24, 512), BF),
        in_specs=[VMEM] * 2,
        out_specs=VMEM,
        compiler_params=params(),
        cost_estimate=cost(1e6, 1e6),
        name="row_weights",
    )(own, mates)


def reorder(major, minor):
    n = major * minor
    to = lax.broadcasted_iota(jnp.int32, (n, n), 0)
    at = lax.broadcasted_iota(jnp.int32, (n, n), 1)
    source = lax.rem(to, major) * minor + lax.div(to, major)
    return jnp.where(at == source, 1.0, 0.0).astype(BF)


def context_kernel(place_ref, w0, w1, w2, w3, *refs):
    value_refs, (x_ref, wo_ref, out_ref, wall, ctx) = refs[:6], refs[6:]
    p = pl.program_id(0)

    @pl.when(p == 0)
    def _():
        place = place_ref[1]
        for step, w in enumerate((w0, w1, w2, w3)):
            wall[lax.rem(place + step, 4)] = w[...]

    start = pl.multiple_of(p * 128, 64)
    left = wall[lax.div(start, 192), pl.ds(pl.multiple_of(lax.rem(start, 192), 64), 64), :]
    start = start + 64
    right = wall[lax.div(start, 192), pl.ds(pl.multiple_of(lax.rem(start, 192), 64), 64), :]
    weights = jnp.concatenate([left, right], axis=0)
    values = jnp.concatenate([ref[0] for ref in value_refs], axis=0)
    both = jnp.dot(weights, values, preferred_element_type=F32)
    first = first_head(I)
    for r in range(R):
        lanes = slice(r * 128, (r + 1) * 128)
        ctx[p, r * I : (r + 1) * I, :] = jnp.where(first, both[:I, lanes], both[I:, lanes]).astype(BF)

    @pl.when(p == PAIRS - 1)
    def _():
        context = jnp.concatenate([ctx[n] for n in range(PAIRS)], axis=1)
        update = jnp.dot(context, wo_ref[...], preferred_element_type=F32)
        after = (x_ref[...].astype(F32).reshape(R * I, D) + update).astype(BF)
        out_ref[...] = jnp.dot(reorder(R, I), after, preferred_element_type=F32).astype(BF)


def row_context(place, weights, values, x, wo):
    whole = pl.BlockSpec((192, 512), lambda p: (0, 0))
    value = [pl.BlockSpec((1, v.shape[1], R * 128), lambda p: (p, 0, 0)) for v in values]
    return pl.pallas_call(
        context_kernel,
        grid=(PAIRS,),
        out_shape=jax.ShapeDtypeStruct((R * I, D), BF),
        in_specs=[pl.BlockSpec(memory_space=pltpu.SMEM)]
        + [whole] * 4
        + value
        + [pl.BlockSpec((R, I, D), lambda p: (0, 0, 0)), pl.BlockSpec((D, D), lambda p: (0, 0))],
        out_specs=pl.BlockSpec((R * I, D), lambda p: (0, 0)),
        scratch_shapes=[pltpu.VMEM((4, 192, 512), BF), pltpu.VMEM((PAIRS, R * I, 128), BF)],
        compiler_params=params(64 * MB),
        cost_estimate=cost(2e9, 1e7),
        name="row_context",
    )(place, *weights, *values, x, wo)


def column_kernel(x_ref, wq_ref, wk_ref, wv_ref, wo_ref, out_ref, normed, total):
    g = pl.program_id(0)

    def column(c):
        return x_ref[...].astype(F32).reshape(32, 2, R, D)[:, c].reshape(256, D)

    @pl.when(g == 0)
    def _():
        for c in range(2):
            normed[c * 256 : (c + 1) * 256] = layer_norm(column(c)).astype(BF)

    rows = normed[...]
    q = jnp.dot(rows, wq_ref[...], preferred_element_type=F32).astype(BF)
    k = jnp.dot(rows, wk_ref[...], preferred_element_type=F32).astype(BF)
    v = jnp.dot(rows, wv_ref[...], preferred_element_type=F32).astype(BF)
    first = first_head(256)
    zero = jnp.zeros((256, 128), BF)
    contexts = []
    for c in range(2):
        pieces = []
        for p in range(2):
            at = (slice(c * 256, (c + 1) * 256), slice(p * 128, (p + 1) * 128))
            both = jnp.concatenate(
                [jnp.where(first, q[at], zero), jnp.where(first, zero, q[at])], axis=0
            )
            scores = lax.dot_general(both, k[at], NT, preferred_element_type=F32)
            top = jnp.max(scores, axis=-1, keepdims=True)
            powers = jnp.exp2((scores - top) * (64**-0.5 * LOG2E))
            weight = jnp.sum(powers, axis=-1, keepdims=True)
            mixed = jnp.dot(powers.astype(BF), v[at], preferred_element_type=F32) / weight
            pieces.append(jnp.where(first, mixed[:256], mixed[256:]).astype(BF))
        contexts.append(jnp.concatenate(pieces, axis=1))
    context = jnp.concatenate(contexts, axis=0)
    update = jnp.dot(context, wo_ref[...], preferred_element_type=F32)

    @pl.when(g == 0)
    def _():
        total[...] = update

    @pl.when(g == 1)
    def _():
        total[...] += update

    @pl.when(g == 2)
    def _():
        done = total[...] + update
        both = [(column(c) + done[c * 256 : (c + 1) * 256]).reshape(32, R, D) for c in range(2)]
        out_ref[...] = jnp.concatenate(both, axis=1).astype(BF)


def attend_columns(x, w, wo):
    whole = pl.BlockSpec((32, 2 * R, D), lambda g: (0, 0, 0))
    return pl.pallas_call(
        column_kernel,
        grid=(3,),
        out_shape=jax.ShapeDtypeStruct((32, 2 * R, D), BF),
        in_specs=[
            whole,
            pl.BlockSpec((D, 256), lambda g: (0, g)),
            pl.BlockSpec((D, 256), lambda g: (0, g + 3)),
            pl.BlockSpec((D, 256), lambda g: (0, g + 6)),
            pl.BlockSpec((256, D), lambda g: (g, 0)),
        ],
        out_specs=whole,
        scratch_shapes=[pltpu.VMEM((512, D), BF), pltpu.VMEM((512, D), F32)],
        compiler_params=params(),
        cost_estimate=cost(5e9, 7e6, 1600000),
        name="columns",
    )(x, w, w, w, wo)


def finish_kernel(x_ref, out_ref):
    rows = jnp.dot(reorder(I, R), x_ref[...], preferred_element_type=F32).astype(BF)
    for r in range(R):
        out_ref[r] = rows[r * I : (r + 1) * I]


def finish(x):
    return pl.pallas_call(
        finish_kernel,
        out_shape=jax.ShapeDtypeStruct((R, I, D), BF),
        in_specs=[VMEM],
        out_specs=VMEM,
        compiler_params=params(),
        cost_estimate=cost(4e8, 1.6e6),
        name="finish",
    )(x)


def shift(n, by):
    return [(i, (i + by) % n) for i in range(n)]


def per_device(x, w_row, wo_row, w_col, wo_col):
    seq = ("x", "z")
    mate = functools.partial(lax.ppermute, axis_name="core", perm=shift(2, 1))
    ways = [[(2 * y + c, 2 * ((y + 1 - 2 * c) % 4) + c) for y in range(4) for c in range(2)]]
    ways.append([(b, a) for a, b in ways[0]])
    on, back = [functools.partial(lax.ppermute, axis_name=("y", "core"), perm=way) for way in ways]
    along = [functools.partial(lax.ppermute, axis_name="x", perm=shift(4, k)) for k in range(4)]
    place = jnp.stack([lax.axis_index("core"), lax.axis_index("x")]).astype(jnp.int32)

    a, b = on(x), back(x)
    q, keys, own_values = own_projections(x, mate(x), w_row)
    a, b, q = lax.optimization_barrier((a, b, q))
    far = on(a)
    *near, near_values, keys = near_logits(place, keys, a, b, w_row, q)
    near = [near[0]] + [along[k](near[k]) for k in (1, 2, 3)]
    far, keys = lax.optimization_barrier((far, keys))
    partial = far_logits(place, keys, far, w_row, q)
    ordered = lax.optimization_barrier((*near, *partial))
    near, partial = ordered[:4], ordered[4:]
    partial = [partial[0]] + [along[k](partial[k]) for k in (1, 2, 3)]
    far, sums = lax.optimization_barrier((far, sum_x(near, partial)))
    parts = lax.all_to_all(sums, "z", 0, 0, tiled=True)
    values = far_values(far, w_row)
    parts, values = lax.optimization_barrier((parts, values))
    values = [own_values, near_values, values]
    values += [mate(v) for v in values]
    own, other = sum_z(place, parts)
    copies = row_weights(own, mate(other), float((64 * 256) ** -0.5), 8)
    mine = lax.all_to_all(copies, "z", 0, 0, tiled=True).reshape(192, 512)
    weights = [mine] + [along[4 - k](mine) for k in (1, 2, 3)]
    rows = row_context(place, weights, values, x, wo_row)
    columns = lax.all_to_all(rows.reshape(32, 2 * R, D), seq, 0, 0, tiled=True)
    columns = attend_columns(columns, w_col, wo_col)
    rows = lax.all_to_all(columns, seq, 0, 0, tiled=True)
    return finish(rows.reshape(R * I, D))


def solution(mesh):
    chips = Mesh(mesh.devices.reshape(4, 8, 4, 2), ("x", "z", "y", "core"))
    rows = P(("x", "z"), ("y", "core"), None)
    return jax.shard_map(
        per_device, mesh=chips, in_specs=(rows, P(), P(), P(), P()), out_specs=rows, check_vma=False
    )
```

time: 251 us -> 178 us (0.71)
  the two profiles are of different devices: /device:TPU:56 before, /device:TPU:1 now
where the time goes in v2:
time: 178 us; the launch traced here: 174 us
  blocking collectives  64.7 us (36%)
  Pallas kernels  44.7 us (25%)
  waiting for transfers between devices  32.6 us (18%)
  starting transfers between devices  30.4 us (17%)
    all_to_all x1, blocking collectives, per_device(): rows = lax.all_to_all(columns, seq, 0, 0, tiled=True)  28.5 us
    all_to_all x1, blocking collectives, per_device(): columns = lax.all_to_all(rows.reshape(32, 2 * R, D), seq, 0, 0, tiled=True)  22.9 us
    all_to_all x1, blocking collectives, per_device(): mine = lax.all_to_all(copies, 'z', 0, 0, tiled=True).reshape(192, 512)  13.3 us
    ppermute x2, waiting for transfers between devices, per_device(): a, b = (on(x), back(x))  12.2 us
    ppermute x3, waiting for transfers between devices, per_device(): weights = [mine] + [along[4 - k](mine) for k in (1, 2, 3)]  11.5 us
    pallas_call x1, Pallas kernels, attend_columns(): pl.pallas_call(column_kernel, grid=(3,), out_shape=jax.ShapeDtypeStruct((...  8.43 us
    pallas_call x1, Pallas kernels, row_context(): pl.pallas_call(context_kernel, grid=(PAIRS,), out_shape=jax.ShapeDtypeStr...  8.4 us
    all_to_all x1, starting transfers between devices, per_device(): parts = lax.all_to_all(sums, 'z', 0, 0, tiled=True)  8.18 us
  transfers between devices with their start and end apart: 18, of which 11 were waited for; matrix products, arithmetic and copies ran while one was open for 0% of the time, Pallas kernels for 15%

profile of v2, /device:TPU:1, one launch (start us, length us, event | category | flops | bytes accessed | tf_op | source)
XLA Modules:
  0.0 174.5 jit_solution(3587456866300165992)
XLA Ops:
  0.0 3.2 %collective-permute-start.2 = (bf16[8,64,768]{2,1,0:T(8,128)(2,1)}, bf16[8,64,768]{2,1,0:T(8,128)(2,1)}, u32[]{:S(2)}, u32[]{:S(2)}) collective-permute-start(bf16[8,64,768]{2,1,0:T(8,128)(2,1)} %refs_6_.1), channel_id=1, source_target_pairs={{0,1},{1,0},{2,3},{3,2},{4,5},{5,4},{6,7},{7,6},{8,9},{9,8},{10,11... | collective-permute-start | bytes 2359304 | tf_op jit(solution)/shard_map/ppermute | solution.py:415
  3.2 1.0 collective-permute-start
  4.7 0.8 collective-permute-done.2.mate_ref
  5.5 6.8 %own_projections.1 = (bf16[6,128,1024]{2,1,0:T(8,128)(2,1)}, bf16[6,64,1024]{2,1,0:T(8,128)(2,1)}, bf16[6,64,1024]{2,1,0:T(8,128)(2,1)}) custom-call(bf16[8,64,768]{2,1,0:T(8,128)(2,1)} %refs_6_.1, bf16[8,64,768]{2,1,0:T(8,128)(2,1)} %collective-permute-done.2.mate_ref, bf16[768,2304]{1,0:T(8,128)(2,1)} %wv_ref.6, bf16[768,2304]{1,0:T(8,128)(2,1)} %wv_ref.6, ...), custom_call_target="tpu_custom_call" | custom-call | flops 2400000000 | bytes 9000000 | tf_op jit(solution)/shard_map/own_projections/pallas_call | solution.py:139
  12.3 10.4 %collective-permute-done.a_ref = bf16[8,64,768]{2,1,0:T(8,128)(2,1)} collective-permute-done((bf16[8,64,768]{2,1,0:T(8,128)(2,1)}, bf16[8,64,768]{2,1,0:T(8,128)(2,1)}, u32[]{:S(2)}, u32[]{:S(2)}) %collective-permute-start) | collective-permute-done | bytes 786464 | tf_op jit(solution)/shard_map/ppermute | solution.py:414
  22.7 1.8 %collective-permute-done.1.b_ref = bf16[8,64,768]{2,1,0:T(8,128)(2,1)} collective-permute-done((bf16[8,64,768]{2,1,0:T(8,128)(2,1)}, bf16[8,64,768]{2,1,0:T(8,128)(2,1)}, u32[]{:S(2)}, u32[]{:S(2)}) %collective-permute-start.1) | collective-permute-done | bytes 786464 | tf_op jit(solution)/shard_map/ppermute | solution.py:414
  25.2 8.1 %near_logits.1 = (bf16[8,48,128]{2,1,0:T(8,128)(2,1)}, bf16[8,48,128]{2,1,0:T(8,128)(2,1)}, bf16[8,48,128]{2,1,0:T(8,128)(2,1)}, bf16[8,48,128]{2,1,0:T(8,128)(2...) custom-call(s32[2]{0:T(128)} %pad_add_fusion.place_ref, ...), custom_call_target="tpu_custom_call" | custom-call | flops 4000000000 | bytes 9000000 | tf_op jit(solution)/shard_map/near_logits/pallas_call | solution.py:153
  33.4 1.3 collective-permute-start.4
  34.7 2.4 %collective-permute-start.5 = (bf16[8,48,128]{2,1,0:T(8,128)(2,1)}, bf16[8,48,128]{2,1,0:T(8,128)(2,1)}, u32[]{:S(2)}, u32[]{:S(2)}) collective-permute-start(bf16[8,48,128]{2,1,0:T(8,128)(2,1)} %get-tuple-element.46), channel_id=1, source_target_pairs={{0,128},{64,192},{128,0},{192,64},{1,129},{65,193},{129,1},{193,65... | collective-permute-start | bytes 294920 | tf_op jit(solution)/shard_map/ppermute | solution.py:419
  37.1 1.2 collective-permute-start.6
  38.3 5.0 %far_logits.1 = (bf16[8,48,128]{2,1,0:T(8,128)(2,1)}, bf16[8,48,128]{2,1,0:T(8,128)(2,1)}, bf16[8,48,128]{2,1,0:T(8,128)(2,1)}, bf16[8,48,128]{2,1,0:T(8,128)(2,1)}) custom-call(s32[2]{0:T(128)} %pad_add_fusion.place_ref, bf16[6,64,1024]{2,1,0:T(8,128)(2,1)} %get-tuple-element.48.key_ref, bf16[8,64,768]{2,1,0:T(8,128)(2,1)} %collective-permute-done.3.far_ref, ...), custom_call_target="tpu_custom_call" | custom-call | flops 2000000000 | bytes 6000000 | tf_op jit(solution)/shard_map/far_logits/pallas_call | solution.py:167
  43.6 1.1 collective-permute-start.8
  44.7 1.4 collective-permute-start.9
  46.1 3.3 %collective-permute-done.7.refs_5_ = bf16[8,48,128]{2,1,0:T(8,128)(2,1)} collective-permute-done((bf16[8,48,128]{2,1,0:T(8,128)(2,1)}, bf16[8,48,128]{2,1,0:T(8,128)(2,1)}, u32[]{:S(2)}, u32[]{:S(2)}) %collective-permute-start.7) | collective-permute-done | bytes 98336 | tf_op jit(solution)/shard_map/ppermute | solution.py:424
  50.4 2.0 %sum_x.1 = bf16[8,48,256]{2,1,0:T(8,128)(2,1)} custom-call(bf16[8,48,128]{2,1,0:T(8,128)(2,1)} %get-tuple-element.53.refs_0_, bf16[8,48,128]{2,1,0:T(8,128)(2,1)} %collective-permute-done.4.refs_1_, bf16[8,48,128]{2,1,0:T(8,128)(2,1)} %collective-permute-done.5.refs_2_, bf16[8,48,128]{2,1,0:T(8,128)(2,1)} %collective-permute-done.6.refs_3_, ...), custom_call_target="tpu_custom_call" | custom-call | flops 1000000 | bytes 1000000 | tf_op jit(solution)/shard_map/sum_x/pallas_call | solution.py:203
  52.4 8.2 %all-to-all-start = ((bf16[8,48,256]{2,1,0:T(8,128)(2,1)}), bf16[8,48,256]{2,1,0:T(8,128)(2,1)}, u32[]{:S(2)}, u32[]{:S(2)}) async-start(bf16[8,48,256]{2,1,0:T(8,128)(2,1)} %sum_x.1), calls=%async_computation | async-start | bytes 393216 | tf_op jit(solution)/shard_map/all_to_all | solution.py:426
  60.5 2.7 %collective-permute-start.14 = (bf16[6,64,1024]{2,1,0:T(8,128)(2,1)}, bf16[6,64,1024]{2,1,0:T(8,128)(2,1)}, u32[]{:S(2)}, u32[]{:S(2)}) collective-permute-start(bf16[6,64,1024]{2,1,0:T(8,128)(2,1)} %get-tuple-element.66.refs_0_), channel_id=1, source_target_pairs={{0,1},{1,0},{2,3},{3,2},{4,5},{5,4},{6,7},{7,6},{8,9},{9,8},{10,11... | collective-permute-start | bytes 2359304 | tf_op jit(solution)/shard_map/ppermute | solution.py:430
  63.2 3.5 %far_values.1.refs_2_ = bf16[6,64,1024]{2,1,0:T(8,128)(2,1)} custom-call(bf16[8,64,768]{2,1,0:T(8,128)(2,1)} %collective-permute-done.3.far_ref, bf16[768,2304]{1,0:T(8,128)(2,1)} %wv_ref.6), custom_call_target="tpu_custom_call" | custom-call | flops 1200000000 | bytes 4000000 | tf_op jit(solution)/shard_map/far_values/pallas_call | solution.py:181
  66.7 2.6 %all-to-all-done.parts_ref = bf16[8,48,256]{2,1,0:T(8,128)(2,1)} async-done(((bf16[8,48,256]{2,1,0:T(8,128)(2,1)}), bf16[8,48,256]{2,1,0:T(8,128)(2,1)}, u32[]{:S(2)}, u32[]{:S(2)}) %all-to-all-start) | async-done | bytes 196640 | tf_op jit(solution)/shard_map/all_to_all | solution.py:426
  69.4 3.7 %collective-permute-start.16 = (bf16[6,64,1024]{2,1,0:T(8,128)(2,1)}, bf16[6,64,1024]{2,1,0:T(8,128)(2,1)}, u32[]{:S(2)}, u32[]{:S(2)}) collective-permute-start(bf16[6,64,1024]{2,1,0:T(8,128)(2,1)} %far_values.1.refs_2_), channel_id=1, source_target_pairs={{0,1},{1,0},{2,3},{3,2},{4,5},{5,4},{6,7},{7,6},{8,9},{9,8},{10,11... | collective-permute-start | bytes 2359304 | tf_op jit(solution)/shard_map/ppermute | solution.py:430
  73.8 1.0 sum_z.1
  74.8 1.2 collective-permute-done.10.far_ref
  76.2 13.3 %all_to_all.20 = bf16[8,24,512]{2,1,0:T(8,128)(2,1)S(1)} all-to-all(bf16[8,24,512]{2,1,0:T(8,128)(2,1)S(1)} %row_weights.1), channel_id=1, replica_groups=mesh['x'=4,'z'=8,'y'=4,'core'=2] {'z'}, dimensions={0} | all-to-all | bytes 393216 | tf_op jit(solution)/shard_map/all_to_all | solution.py:433
  89.5 2.4 %collective-permute-start.11 = (bf16[192,512]{1,0:T(8,128)(2,1)S(1)}, bf16[192,512]{1,0:T(8,128)(2,1)S(1)}, u32[]{:S(2)}, u32[]{:S(2)}) collective-permute-start(bf16[192,512]{1,0:T(8,128)(2,1)S(1)} %bitcast.7), channel_id=1, source_target_pairs={{0,192},{64,0},{128,64},{192,128},{1,193},{65,1},{129,65},{193,129... | collective-permute-start | bytes 589832 | tf_op jit(solution)/shard_map/ppermute | solution.py:434
  92.5 3.9 %collective-permute-done.11.w1 = bf16[192,512]{1,0:T(8,128)(2,1)S(1)} collective-permute-done((bf16[192,512]{1,0:T(8,128)(2,1)S(1)}, bf16[192,512]{1,0:T(8,128)(2,1)S(1)}, u32[]{:S(2)}, u32[]{:S(2)}) %collective-permute-start.11) | collective-permute-done | bytes 196640 | tf_op jit(solution)/shard_map/ppermute | solution.py:434
  96.4 2.8 %collective-permute-done.12.w2 = bf16[192,512]{1,0:T(8,128)(2,1)S(1)} collective-permute-done((bf16[192,512]{1,0:T(8,128)(2,1)S(1)}, bf16[192,512]{1,0:T(8,128)(2,1)S(1)}, u32[]{:S(2)}, u32[]{:S(2)}) %collective-permute-start.12) | collective-permute-done | bytes 196640 | tf_op jit(solution)/shard_map/ppermute | solution.py:434
  99.2 4.9 %collective-permute-done.13.w3 = bf16[192,512]{1,0:T(8,128)(2,1)S(1)} collective-permute-done((bf16[192,512]{1,0:T(8,128)(2,1)S(1)}, bf16[192,512]{1,0:T(8,128)(2,1)S(1)}, u32[]{:S(2)}, u32[]{:S(2)}) %collective-permute-start.13) | collective-permute-done | bytes 196640 | tf_op jit(solution)/shard_map/ppermute | solution.py:434
  104.8 8.4 %row_context.1 = bf16[512,768]{1,0:T(8,128)(2,1)} custom-call(s32[2]{0:T(128)} %pad_add_fusion.place_ref, bf16[192,512]{1,0:T(8,128)(2,1)} %bitcast.10, bf16[192,512]{1,0:T(8,128)(2,1)} %copy-done.3, bf16[192,512]{1,0:T(8,128)(2,1)} %copy-done.4, bf16[192,512]{1,0:T(8,128)(2,1)} %copy-done.5, bf16[6,64,1024]{2,1,0:T(8,128)(2,1)} %get-tuple-element.66.refs_0_, ...), custom_call_target="tpu_custom_call" | custom-call | flops 2000000000 | bytes 10000000 | tf_op jit(solution)/shard_map/row_context/pallas_call | solution.py:296
  113.2 22.9 %all_to_all.21.x_ref = bf16[32,16,768]{2,1,0:T(8,128)(2,1)S(1)} all-to-all(bf16[32,16,768]{2,1,0:T(8,128)(2,1)} %bitcast.6), channel_id=1, replica_groups=mesh['x'=4,'z'=8,'y'=4,'core'=2] {'x','z'}, dimensions={0} | all-to-all | bytes 1572864 | tf_op jit(solution)/shard_map/all_to_all | solution.py:436
  136.0 8.4 %columns.1 = bf16[32,16,768]{2,1,0:T(8,128)(2,1)S(1)} custom-call(bf16[32,16,768]{2,1,0:T(8,128)(2,1)S(1)} %all_to_all.21.x_ref, bf16[768,2304]{1,0:T(8,128)(2,1)} %wv_ref.7, bf16[768,2304]{1,0:T(8,128)(2,1)} %wv_ref.7, bf16[768,2304]{1,0:T(8,128)(2,1)} %wv_ref.7, bf16[768,768]{1,0:T(8,128)(2,1)S(1)} %copy-done.1), custom_call_target="tpu_custom_call" | custom-call | flops 5000000000 | bytes 7000000 | tf_op jit(solution)/shard_map/columns/pallas_call | solution.py:364
  144.5 28.5 %all_to_all.22 = bf16[32,16,768]{2,1,0:T(8,128)(2,1)S(1)} all-to-all(bf16[32,16,768]{2,1,0:T(8,128)(2,1)S(1)} %columns.1), channel_id=1, replica_groups=mesh['x'=4,'z'=8,'y'=4,'core'=2] {'x','z'}, dimensions={0} | all-to-all | bytes 1572864 | tf_op jit(solution)/shard_map/all_to_all | solution.py:438
  173.0 1.5 finish.1
  (30 shorter events, 4.8 us)
Async XLA Ops:
  0.0 5.5 %collective-permute-start.2 = (bf16[8,64,768]{2,1,0:T(8,128)(2,1)}, bf16[8,64,768]{2,1,0:T(8,128)(2,1)}, u32[]{:S(2)}, u32[]{:S(2)}) collective-permute-start(bf16[8,64,768]{2,1,0:T(8,128)(2,1)} %refs_6_.1), channel_id=1, source_target_pairs={{0,1},{1,0},{2,3},{3,2},{4,5},{5,4},{6,7},{7,6},{8,9},{9,8},{10,11... | collective-permute-start | bytes 2359304 | tf_op jit(solution)/shard_map/ppermute | solution.py:415
  3.2 19.5 %collective-permute-start = (bf16[8,64,768]{2,1,0:T(8,128)(2,1)}, bf16[8,64,768]{2,1,0:T(8,128)(2,1)}, u32[]{:S(2)}, u32[]{:S(2)}) collective-permute-start(bf16[8,64,768]{2,1,0:T(8,128)(2,1)} %refs_6_.1), channel_id=1, source_target_pairs={{0,2},{1,7},{2,4},{3,1},{4,6},{5,3},{6,0},{7,5},{8,10},{9,15},{10,... | collective-permute-start | bytes 2359304 | tf_op jit(solution)/shard_map/ppermute | solution.py:414
  4.2 20.3 %collective-permute-start.1 = (bf16[8,64,768]{2,1,0:T(8,128)(2,1)}, bf16[8,64,768]{2,1,0:T(8,128)(2,1)}, u32[]{:S(2)}, u32[]{:S(2)}) collective-permute-start(bf16[8,64,768]{2,1,0:T(8,128)(2,1)} %refs_6_.1), channel_id=1, source_target_pairs={{2,0},{7,1},{4,2},{1,3},{6,4},{3,5},{0,6},{5,7},{10,8},{15,9},{12,... | collective-permute-start | bytes 2359304 | tf_op jit(solution)/shard_map/ppermute | solution.py:414
  24.5 13.8 %collective-permute-start.3 = (bf16[8,64,768]{2,1,0:T(8,128)(2,1)}, bf16[8,64,768]{2,1,0:T(8,128)(2,1)}, u32[]{:S(2)}, u32[]{:S(2)}) collective-permute-start(bf16[8,64,768]{2,1,0:T(8,128)(2,1)} %collective-permute-done.a_ref), channel_id=1, source_target_pairs={{0,2},{1,7},{2,4},{3,1},{4,6},{5,3},{6,0},{7,5},{8,10},{9,15},{10,... | collective-permute-start | bytes 2359304 | tf_op jit(solution)/shard_map/ppermute | solution.py:417
  33.2 59.3 %collective-permute-start.15 = (bf16[6,128,1024]{2,1,0:T(8,128)(2,1)}, bf16[6,128,1024]{2,1,0:T(8,128)(2,1)}, u32[]{:S(2)}, u32[]{:S(2)}) collective-permute-start(bf16[6,128,1024]{2,1,0:T(8,128)(2,1)} %get-tuple-element.67.refs_1_), channel_id=1, source_target_pairs={{0,1},{1,0},{2,3},{3,2},{4,5},{5,4},{6,7},{7,6},{8,9},{9,8},{10,11... | collective-permute-start | bytes 4718600 | tf_op jit(solution)/shard_map/ppermute | solution.py:430
  33.4 9.8 %collective-permute-start.4 = (bf16[8,48,128]{2,1,0:T(8,128)(2,1)}, bf16[8,48,128]{2,1,0:T(8,128)(2,1)}, u32[]{:S(2)}, u32[]{:S(2)}) collective-permute-start(bf16[8,48,128]{2,1,0:T(8,128)(2,1)} %get-tuple-element.45), channel_id=1, source_target_pairs={{0,64},{64,128},{128,192},{192,0},{1,65},{65,129},{129,193},{193,1... | collective-permute-start | bytes 294920 | tf_op jit(solution)/shard_map/ppermute | solution.py:419
  34.7 8.6 %collective-permute-start.5 = (bf16[8,48,128]{2,1,0:T(8,128)(2,1)}, bf16[8,48,128]{2,1,0:T(8,128)(2,1)}, u32[]{:S(2)}, u32[]{:S(2)}) collective-permute-start(bf16[8,48,128]{2,1,0:T(8,128)(2,1)} %get-tuple-element.46), channel_id=1, source_target_pairs={{0,128},{64,192},{128,0},{192,64},{1,129},{65,193},{129,1},{193,65... | collective-permute-start | bytes 294920 | tf_op jit(solution)/shard_map/ppermute | solution.py:419
  37.1 6.1 %collective-permute-start.6 = (bf16[8,48,128]{2,1,0:T(8,128)(2,1)}, bf16[8,48,128]{2,1,0:T(8,128)(2,1)}, u32[]{:S(2)}, u32[]{:S(2)}) collective-permute-start(bf16[8,48,128]{2,1,0:T(8,128)(2,1)} %get-tuple-element.47), channel_id=1, source_target_pairs={{0,192},{64,0},{128,64},{192,128},{1,193},{65,1},{129,65},{193,129... | collective-permute-start | bytes 294920 | tf_op jit(solution)/shard_map/ppermute | solution.py:419
  43.3 6.2 %collective-permute-start.7 = (bf16[8,48,128]{2,1,0:T(8,128)(2,1)}, bf16[8,48,128]{2,1,0:T(8,128)(2,1)}, u32[]{:S(2)}, u32[]{:S(2)}) collective-permute-start(bf16[8,48,128]{2,1,0:T(8,128)(2,1)} %get-tuple-element.58), channel_id=1, source_target_pairs={{0,64},{64,128},{128,192},{192,0},{1,65},{65,129},{129,193},{193,1... | collective-permute-start | bytes 294920 | tf_op jit(solution)/shard_map/ppermute | solution.py:424
  43.6 6.0 %collective-permute-start.8 = (bf16[8,48,128]{2,1,0:T(8,128)(2,1)}, bf16[8,48,128]{2,1,0:T(8,128)(2,1)}, u32[]{:S(2)}, u32[]{:S(2)}) collective-permute-start(bf16[8,48,128]{2,1,0:T(8,128)(2,1)} %get-tuple-element.59), channel_id=1, source_target_pairs={{0,128},{64,192},{128,0},{192,64},{1,129},{65,193},{129,1},{193,65... | collective-permute-start | bytes 294920 | tf_op jit(solution)/shard_map/ppermute | solution.py:424
  44.7 5.7 %collective-permute-start.9 = (bf16[8,48,128]{2,1,0:T(8,128)(2,1)}, bf16[8,48,128]{2,1,0:T(8,128)(2,1)}, u32[]{:S(2)}, u32[]{:S(2)}) collective-permute-start(bf16[8,48,128]{2,1,0:T(8,128)(2,1)} %get-tuple-element.60), channel_id=1, source_target_pairs={{0,192},{64,0},{128,64},{192,128},{1,193},{65,1},{129,65},{193,129... | collective-permute-start | bytes 294920 | tf_op jit(solution)/shard_map/ppermute | solution.py:424
  52.4 17.0 %all-to-all-start = ((bf16[8,48,256]{2,1,0:T(8,128)(2,1)}), bf16[8,48,256]{2,1,0:T(8,128)(2,1)}, u32[]{:S(2)}, u32[]{:S(2)}) async-start(bf16[8,48,256]{2,1,0:T(8,128)(2,1)} %sum_x.1), calls=%async_computation | async-start | bytes 393216 | tf_op jit(solution)/shard_map/all_to_all | solution.py:426
  60.5 31.4 %collective-permute-start.14 = (bf16[6,64,1024]{2,1,0:T(8,128)(2,1)}, bf16[6,64,1024]{2,1,0:T(8,128)(2,1)}, u32[]{:S(2)}, u32[]{:S(2)}) collective-permute-start(bf16[6,64,1024]{2,1,0:T(8,128)(2,1)} %get-tuple-element.66.refs_0_), channel_id=1, source_target_pairs={{0,1},{1,0},{2,3},{3,2},{4,5},{5,4},{6,7},{7,6},{8,9},{9,8},{10,11... | collective-permute-start | bytes 2359304 | tf_op jit(solution)/shard_map/ppermute | solution.py:430
  69.4 35.4 %collective-permute-start.16 = (bf16[6,64,1024]{2,1,0:T(8,128)(2,1)}, bf16[6,64,1024]{2,1,0:T(8,128)(2,1)}, u32[]{:S(2)}, u32[]{:S(2)}) collective-permute-start(bf16[6,64,1024]{2,1,0:T(8,128)(2,1)} %far_values.1.refs_2_), channel_id=1, source_target_pairs={{0,1},{1,0},{2,3},{3,2},{4,5},{5,4},{6,7},{7,6},{8,9},{9,8},{10,11... | collective-permute-start | bytes 2359304 | tf_op jit(solution)/shard_map/ppermute | solution.py:430
  73.1 0.6 copy-start
  74.7 1.3 collective-permute-start.10
  89.5 2.4 %copy-start.2 = (bf16[8,24,512]{2,1,0:T(8,128)(2,1)}, bf16[8,24,512]{2,1,0:T(8,128)(2,1)S(1)}, u32[]{:S(2)}) copy-start(bf16[8,24,512]{2,1,0:T(8,128)(2,1)S(1)} %all_to_all.20) | copy-start | bytes 589828
  89.5 6.9 %collective-permute-start.11 = (bf16[192,512]{1,0:T(8,128)(2,1)S(1)}, bf16[192,512]{1,0:T(8,128)(2,1)S(1)}, u32[]{:S(2)}, u32[]{:S(2)}) collective-permute-start(bf16[192,512]{1,0:T(8,128)(2,1)S(1)} %bitcast.7), channel_id=1, source_target_pairs={{0,192},{64,0},{128,64},{192,128},{1,193},{65,1},{129,65},{193,129... | collective-permute-start | bytes 589832 | tf_op jit(solution)/shard_map/ppermute | solution.py:434
  91.9 7.3 %collective-permute-start.12 = (bf16[192,512]{1,0:T(8,128)(2,1)S(1)}, bf16[192,512]{1,0:T(8,128)(2,1)S(1)}, u32[]{:S(2)}, u32[]{:S(2)}) collective-permute-start(bf16[192,512]{1,0:T(8,128)(2,1)S(1)} %bitcast.8), channel_id=1, source_target_pairs={{0,128},{64,192},{128,0},{192,64},{1,129},{65,193},{129,1},{193,65... | collective-permute-start | bytes 589832 | tf_op jit(solution)/shard_map/ppermute | solution.py:434
  92.0 12.1 %collective-permute-start.13 = (bf16[192,512]{1,0:T(8,128)(2,1)S(1)}, bf16[192,512]{1,0:T(8,128)(2,1)S(1)}, u32[]{:S(2)}, u32[]{:S(2)}) collective-permute-start(bf16[192,512]{1,0:T(8,128)(2,1)S(1)} %bitcast.9), channel_id=1, source_target_pairs={{0,64},{64,128},{128,192},{192,0},{1,65},{65,129},{129,193},{193,1... | collective-permute-start | bytes 589832 | tf_op jit(solution)/shard_map/ppermute | solution.py:434
  96.4 7.6 %copy-start.3 = (bf16[192,512]{1,0:T(8,128)(2,1)}, bf16[192,512]{1,0:T(8,128)(2,1)S(1)}, u32[]{:S(2)}) copy-start(bf16[192,512]{1,0:T(8,128)(2,1)S(1)} %collective-permute-done.11.w1) | copy-start | bytes 589828
  99.2 4.9 %copy-start.4 = (bf16[192,512]{1,0:T(8,128)(2,1)}, bf16[192,512]{1,0:T(8,128)(2,1)S(1)}, u32[]{:S(2)}) copy-start(bf16[192,512]{1,0:T(8,128)(2,1)S(1)} %collective-permute-done.12.w2) | copy-start | bytes 589828
  104.1 0.7 copy-start.5
  113.2 22.9 %copy-start.1 = (bf16[768,768]{1,0:T(8,128)(2,1)S(1)}, bf16[768,768]{1,0:T(8,128)(2,1)}, u32[]{:S(2)}) copy-start(bf16[768,768]{1,0:T(8,128)(2,1)} %wo_ref.1) | copy-start | bytes 3538948

commit v3 on v2

v3 whole, which is shorter than its diff:
```python
import functools

import jax
import jax.numpy as jnp
from jax import lax
from jax.experimental import pallas as pl
from jax.experimental.pallas import tpu as pltpu
from jax.sharding import Mesh, PartitionSpec as P

HEADS = 12
PAIRS = 6
D = 768
R = 8
I = 64
EPS = 1e-05
LOG2E = 1.4426950408889634
NT = (((1,), (1,)), ((), ()))
BF = jnp.bfloat16
F32 = jnp.float32
VMEM = pl.BlockSpec(memory_space=pltpu.VMEM)
MB = 1024 * 1024


def params(limit=48 * MB):
    return pltpu.CompilerParams(vmem_limit_bytes=limit)


def cost(flops, bytes_accessed, transcendentals=0):
    return pl.CostEstimate(
        flops=int(flops), bytes_accessed=int(bytes_accessed), transcendentals=int(transcendentals)
    )


def layer_norm(x):
    mean = jnp.mean(x, axis=-1, keepdims=True)
    centered = x - mean
    spread = jnp.mean(centered * centered, axis=-1, keepdims=True)
    return centered * lax.rsqrt(spread + EPS)


def first_head(rows):
    return lax.broadcasted_iota(jnp.int32, (rows, 128), 1) < 64


def store_block(ref, at, first, rows):
    for p in range(PAIRS):
        for r in range(rows.shape[0] // I):
            lanes = (first + r) * 128
            piece = rows[r * I : (r + 1) * I, p * 128 : (p + 1) * 128]
            ref[p, at : at + I, lanes : lanes + 128] = piece


def store_logits(q_ref, keys, rows, out_ref):
    first = lax.rem(lax.broadcasted_iota(jnp.int32, (I, R * 128), 1), 128) < 64
    zero = jnp.zeros((I, R * 128), BF)
    core = lax.axis_index("core")
    for p in range(PAIRS):
        masked = []
        for part in range(2):
            q = q_ref[p, part * I : (part + 1) * I]
            masked += [jnp.where(first, q, zero), jnp.where(first, zero, q)]
        logits = lax.dot_general(
            jnp.concatenate(masked, axis=0), keys[p], NT, preferred_element_type=F32
        )
        rows[core, p * 128 : (p + 1) * 128] = logits[:128]
        rows[1 - core, p * 128 : (p + 1) * 128] = logits[128:]
    both = [rows[c].reshape(32, 24, 128) for c in range(2)]
    out_ref[...] = jnp.concatenate(both, axis=1).astype(BF)


def normed_rows(ref, s):
    return layer_norm(ref[4 * s : 4 * s + 4].astype(F32).reshape(4 * I, D)).astype(BF)


def project(rows, w_ref):
    return jnp.dot(rows, w_ref[...], preferred_element_type=F32).astype(BF)


def own_kernel(x_ref, mate_ref, wq_ref, wk_ref, wv_ref, q_ref, k_ref, v_ref):
    for s in range(2):
        rows = normed_rows(x_ref, s)
        store_block(q_ref, 0, 4 * s, project(rows, wq_ref))
        store_block(k_ref, 0, 4 * s, project(rows, wk_ref))
        store_block(v_ref, 0, 4 * s, project(rows, wv_ref))
        store_block(q_ref, I, 4 * s, project(normed_rows(mate_ref, s), wq_ref))


def near_kernel(key_ref, a_ref, wk_ref, q_ref, out_ref, keys, rows):
    keys[:, :I] = key_ref[...]
    for s in range(2):
        store_block(keys, I, 4 * s, project(normed_rows(a_ref, s), wk_ref))
    store_logits(q_ref, keys, rows, out_ref)


def far_kernel(b_ref, far_ref, wk_ref, q_ref, out_ref, keys, rows):
    for at, ref in ((0, b_ref), (I, far_ref)):
        for s in range(2):
            store_block(keys, at, 4 * s, project(normed_rows(ref, s), wk_ref))
    store_logits(q_ref, keys, rows, out_ref)


def value_kernel(a_ref, b_ref, far_ref, wv_ref, v_ref):
    for n, ref in enumerate((a_ref, b_ref, far_ref)):
        for s in range(2):
            store_block(v_ref, n * I, 4 * s, project(normed_rows(ref, s), wv_ref))


def block(*shape):
    return pl.BlockSpec(shape, lambda s: (0,) * len(shape))


def weight(part):
    return pl.BlockSpec((D, D), lambda s: (0, part))


LOGITS = jax.ShapeDtypeStruct((32, 48, 128), BF)
ONE = jax.ShapeDtypeStruct((PAIRS, I, R * 128), BF)
TWO = jax.ShapeDtypeStruct((PAIRS, 2 * I, R * 128), BF)
ROWS = pltpu.VMEM((2, D, 128), F32)
KEYS = pltpu.VMEM((PAIRS, 128, R * 128), BF)


def own_projections(x, mate, w):
    whole, one, two = block(R, I, D), block(*ONE.shape), block(*TWO.shape)
    return pl.pallas_call(
        own_kernel,
        grid=(1,),
        out_shape=(TWO, ONE, ONE),
        in_specs=[whole, whole, weight(0), weight(1), weight(2)],
        out_specs=(two, one, one),
        compiler_params=params(64 * MB),
        cost_estimate=cost(2.4e9, 9e6),
        name="own_projections",
    )(x, mate, w, w, w)


def near_logits(keys, a, w, q):
    whole, one, two = block(R, I, D), block(*ONE.shape), block(*TWO.shape)
    return pl.pallas_call(
        near_kernel,
        grid=(1,),
        out_shape=LOGITS,
        in_specs=[one, whole, weight(1), two],
        out_specs=block(32, 48, 128),
        scratch_shapes=[KEYS, ROWS],
        compiler_params=params(64 * MB),
        cost_estimate=cost(3e9, 8e6),
        name="near_logits",
    )(keys, a, w, q)


def far_logits(b, far, w, q):
    whole = block(R, I, D)
    return pl.pallas_call(
        far_kernel,
        grid=(1,),
        out_shape=LOGITS,
        in_specs=[whole, whole, weight(1), block(*TWO.shape)],
        out_specs=block(32, 48, 128),
        scratch_shapes=[KEYS, ROWS],
        compiler_params=params(64 * MB),
        cost_estimate=cost(3e9, 7e6),
        name="far_logits",
    )(b, far, w, q)


def other_values(a, b, far, w):
    whole, three = block(R, I, D), (PAIRS, 3 * I, R * 128)
    return pl.pallas_call(
        value_kernel,
        grid=(1,),
        out_shape=jax.ShapeDtypeStruct(three, BF),
        in_specs=[whole, whole, whole, weight(2)],
        out_specs=block(*three),
        compiler_params=params(64 * MB),
        cost_estimate=cost(2e9, 6e6),
        name="other_values",
    )(a, b, far, w)


def sum_kernel(near_ref, far_ref, mine_ref, mates_ref, rows):
    totals = [jnp.sum(ref[...].astype(F32), axis=0) for ref in (near_ref, far_ref)]
    rows[...] = jnp.concatenate(totals, axis=1).reshape(2, 24, 256)
    core = lax.axis_index("core")
    mine_ref[...] = rows[core]
    mates_ref[...] = rows[1 - core]


def sum_logits(near, far):
    return pl.pallas_call(
        sum_kernel,
        out_shape=(jax.ShapeDtypeStruct((24, 256), F32),) * 2,
        in_specs=[VMEM, VMEM],
        out_specs=(VMEM, VMEM),
        scratch_shapes=[pltpu.VMEM((2, 24, 256), F32)],
        compiler_params=params(),
        cost_estimate=cost(1e6, 1e6),
        name="sum_logits",
    )(near, far)


def weight_kernel(scale, copies, near_ref, far_ref, out_ref):
    logits = jnp.concatenate([near_ref[...], far_ref[...]], axis=1)
    top = jnp.max(logits, axis=-1, keepdims=True)
    powers = jnp.exp2((logits - top) * (scale * LOG2E))
    weights = (powers / jnp.sum(powers, axis=-1, keepdims=True)).astype(BF)
    for c in range(copies):
        out_ref[c] = weights


def row_weights(own, mates, scale, copies):
    return pl.pallas_call(
        functools.partial(weight_kernel, scale, copies),
        out_shape=jax.ShapeDtypeStruct((copies, 24, 512), BF),
        in_specs=[VMEM] * 2,
        out_specs=VMEM,
        compiler_params=params(),
        cost_estimate=cost(1e6, 1e6),
        name="row_weights",
    )(own, mates)


def reorder(major, minor):
    n = major * minor
    to = lax.broadcasted_iota(jnp.int32, (n, n), 0)
    at = lax.broadcasted_iota(jnp.int32, (n, n), 1)
    source = lax.rem(to, major) * minor + lax.div(to, major)
    return jnp.where(at == source, 1.0, 0.0).astype(BF)


HBM = pl.BlockSpec(memory_space=pltpu.HBM)


STEP = 3


def context_kernel(w0, w1, w2, w3, *refs):
    value_refs, (x_ref, wo_ref, out_ref), refs = refs[:4], refs[4:7], refs[7:]
    wall, ctx, x_own, wo, sems = refs
    g = pl.program_id(0)
    late = [
        pltpu.make_async_copy(wo_ref, wo, sems.at[0]),
        pltpu.make_async_copy(x_ref, x_own, sems.at[1]),
    ]

    @pl.when(g == 0)
    def _():
        place = lax.axis_index("x")
        for step, w in enumerate((w0, w1, w2, w3)):
            wall[lax.rem(place + step, 4)] = w[...].reshape(3, I, 512)
        for copy in late:
            copy.start()

    first = first_head(I)
    for n in range(STEP):
        pair = []
        for h in range(2):
            head = (g * STEP + n) * 2 + h
            pair.append(wall[lax.div(head, 3), lax.rem(head, 3)])
        weights = jnp.concatenate(pair, axis=0)
        values = jnp.concatenate([ref[n] for ref in value_refs], axis=0)
        both = jnp.dot(weights, values, preferred_element_type=F32)
        for r in range(R):
            lanes = slice(r * 128, (r + 1) * 128)
            piece = jnp.where(first, both[:I, lanes], both[I:, lanes]).astype(BF)
            ctx[g * STEP + n, r * I : (r + 1) * I, :] = piece

    @pl.when(g == PAIRS // STEP - 1)
    def _():
        for copy in late:
            copy.wait()
        context = jnp.concatenate([ctx[n] for n in range(PAIRS)], axis=1)
        update = jnp.dot(context, wo[...], preferred_element_type=F32)
        after = (x_own[...].astype(F32).reshape(R * I, D) + update).astype(BF)
        out_ref[...] = jnp.dot(reorder(R, I), after, preferred_element_type=F32).astype(BF)


def row_context(weights, values, x, wo):
    whole = pl.BlockSpec((192, 512), lambda p: (0, 0))
    value = [pl.BlockSpec((STEP, v.shape[1], R * 128), lambda p: (p, 0, 0)) for v in values]
    return pl.pallas_call(
        context_kernel,
        grid=(PAIRS // STEP,),
        out_shape=jax.ShapeDtypeStruct((R * I, D), BF),
        in_specs=[whole] * 4
        + value
        + [HBM, HBM],
        out_specs=pl.BlockSpec((R * I, D), lambda p: (0, 0)),
        scratch_shapes=[
            pltpu.VMEM((4, 3, I, 512), BF),
            pltpu.VMEM((PAIRS, R * I, 128), BF),
            pltpu.VMEM((R, I, D), BF),
            pltpu.VMEM((D, D), BF),
            pltpu.SemaphoreType.DMA((2,)),
        ],
        compiler_params=params(62 * MB),
        cost_estimate=cost(2e9, 1e7),
        name="row_context",
    )(*weights, *values, x, wo)


def column_kernel(x_ref, wq_ref, wk_ref, wv_ref, wo_ref, out_ref, normed, context, wo, sem):
    g = pl.program_id(0)
    late = pltpu.make_async_copy(wo_ref, wo, sem)

    def column(c):
        return x_ref[...].astype(F32).reshape(32, 2, R, D)[:, c].reshape(256, D)

    @pl.when(g == 0)
    def _():
        late.start()
        for c in range(2):
            normed[c * 256 : (c + 1) * 256] = layer_norm(column(c)).astype(BF)

    rows = normed[...]
    q = jnp.dot(rows, wq_ref[...], preferred_element_type=F32).astype(BF)
    k = jnp.dot(rows, wk_ref[...], preferred_element_type=F32).astype(BF)
    v = jnp.dot(rows, wv_ref[...], preferred_element_type=F32).astype(BF)
    first = first_head(256)
    zero = jnp.zeros((256, 128), BF)
    for c in range(2):
        rows = slice(c * 256, (c + 1) * 256)
        for p in range(2):
            at = (rows, slice(p * 128, (p + 1) * 128))
            both = jnp.concatenate(
                [jnp.where(first, q[at], zero), jnp.where(first, zero, q[at])], axis=0
            )
            scores = lax.dot_general(both, k[at], NT, preferred_element_type=F32)
            top = jnp.max(scores, axis=-1, keepdims=True)
            powers = jnp.exp2((scores - top) * (64**-0.5 * LOG2E))
            weight = jnp.sum(powers, axis=-1, keepdims=True)
            mixed = jnp.dot(powers.astype(BF), v[at], preferred_element_type=F32) / weight
            context[2 * g + p, rows] = jnp.where(first, mixed[:256], mixed[256:]).astype(BF)

    @pl.when(g == 2)
    def _():
        late.wait()
        whole = jnp.concatenate([context[p] for p in range(PAIRS)], axis=1)
        update = jnp.dot(whole, wo[...], preferred_element_type=F32)
        both = [(column(c) + update[c * 256 : (c + 1) * 256]).reshape(32, R, D) for c in range(2)]
        out_ref[...] = jnp.concatenate(both, axis=1).astype(BF)


def attend_columns(x, w, wo):
    whole = pl.BlockSpec((32, 2 * R, D), lambda g: (0, 0, 0))
    return pl.pallas_call(
        column_kernel,
        grid=(3,),
        out_shape=jax.ShapeDtypeStruct((32, 2 * R, D), BF),
        in_specs=[
            whole,
            pl.BlockSpec((D, 256), lambda g: (0, g)),
            pl.BlockSpec((D, 256), lambda g: (0, g + 3)),
            pl.BlockSpec((D, 256), lambda g: (0, g + 6)),
            HBM,
        ],
        out_specs=whole,
        scratch_shapes=[
            pltpu.VMEM((512, D), BF),
            pltpu.VMEM((PAIRS, 512, 128), BF),
            pltpu.VMEM((D, D), BF),
            pltpu.SemaphoreType.DMA,
        ],
        compiler_params=params(62 * MB),
        cost_estimate=cost(5e9, 7e6, 1600000),
        name="columns",
    )(x, w, w, w, wo)


def finish_kernel(x_ref, out_ref):
    rows = jnp.dot(reorder(I, R), x_ref[...], preferred_element_type=F32).astype(BF)
    for r in range(R):
        out_ref[r] = rows[r * I : (r + 1) * I]


def finish(x):
    return pl.pallas_call(
        finish_kernel,
        out_shape=jax.ShapeDtypeStruct((R, I, D), BF),
        in_specs=[VMEM],
        out_specs=VMEM,
        compiler_params=params(),
        cost_estimate=cost(4e8, 1.6e6),
        name="finish",
    )(x)


def shift(n, by):
    return [(i, (i + by) % n) for i in range(n)]


def per_device(x, w_row, wo_row, w_col, wo_col):
    exchange = functools.partial(
        lax.all_to_all, axis_name=("x", "z"), split_axis=0, concat_axis=0, tiled=True
    )
    mate = functools.partial(lax.ppermute, axis_name="core", perm=shift(2, 1))
    ways = [[(2 * y + c, 2 * ((y + 1 - 2 * c) % 4) + c) for y in range(4) for c in range(2)]]
    ways.append([(b, a) for a, b in ways[0]])
    on, back = [functools.partial(lax.ppermute, axis_name=("y", "core"), perm=way) for way in ways]
    along = [functools.partial(lax.ppermute, axis_name="x", perm=shift(4, k)) for k in range(4)]

    a = on(x)
    q, keys, own_values = own_projections(x, mate(x), w_row)
    later, q = lax.optimization_barrier((x, q))
    b, far = back(later), on(a)
    near = near_logits(keys, a, w_row, q)
    b, far, _ = lax.optimization_barrier((b, far, near))
    near = exchange(near)
    logits = far_logits(b, far, w_row, q)
    a, b, far, logits, near = lax.optimization_barrier((a, b, far, logits, near))
    logits = exchange(logits)
    values = other_values(a, b, far, w_row)
    logits, values = lax.optimization_barrier((logits, values))
    values = [own_values, values]
    values += [mate(v) for v in values]
    own, other = sum_logits(near, logits)
    copies = row_weights(own, mate(other), float((64 * 256) ** -0.5), 8)
    mine = lax.all_to_all(copies, "z", 0, 0, tiled=True).reshape(192, 512)
    weights = [mine] + [along[4 - k](mine) for k in (1, 2, 3)]
    rows = row_context(weights, values, x, wo_row)
    columns = exchange(rows.reshape(32, 2 * R, D))
    columns = attend_columns(columns, w_col, wo_col)
    rows = exchange(columns)
    return finish(rows.reshape(R * I, D))


def solution(mesh):
    chips = Mesh(mesh.devices.reshape(4, 8, 4, 2), ("x", "z", "y", "core"))
    rows = P(("x", "z"), ("y", "core"), None)
    return jax.shard_map(
        per_device, mesh=chips, in_specs=(rows, P(), P(), P(), P()), out_specs=rows, check_vma=False
    )
```

time: 178 us -> 172 us (0.966)
  waiting for transfers between devices: 32.6 us -> 25.9 us
  Pallas kernels: 44.7 us -> 41.6 us
  starting transfers between devices: 30.4 us -> 33.4 us
  blocking collectives: 64.7 us -> 67.5 us
    all_to_all x1 -> x2, starting transfers between devices: 8.18 us -> 21.5 us  [the longest x1 11.2 us: per_device(): near = exchange(near)]
    ppermute x9 -> x3, waiting for transfers between devices: 16.5 us -> 6.72 us  [the longest x2 4.3 us: per_device(): b, far = (back(later), on(a))]
    ppermute x9 -> x3, starting transfers between devices: 9.29 us -> 2.92 us  [the longest x2 1.92 us: per_device(): b, far = (back(later), on(a))]
    all_to_all x1 -> x2, waiting for transfers between devices: 2.64 us -> 7.4 us  [the longest x1 6.95 us: per_device(): logits = exchange(logits)]
    ppermute x3 -> x2, starting transfers between devices: 6.59 us -> 2.05 us  [per_device(): values += [mate(v) for v in values]]
    pallas_call x6 -> x5, Pallas kernels: 27.9 us -> 24.1 us  [the longest x1 6.2 us: row_context(): pl.pallas_call(context_kernel, grid=(PAIRS // STEP,), out_shape=jax.Shape...]
    ppermute x3, waiting for transfers between devices: 11.5 us -> 8.25 us  [per_device(): weights = [mine] + [along[4 - k](mine) for k in (1, 2, 3)]]
    all_to_all x2, blocking collectives: 51.4 us -> 53.8 us  [the longest x1 28.6 us: per_device(): rows = exchange(columns)]
  transfers between devices with their start and end apart: 18 -> 12, of which waited for: 11 -> 9; matrix products, arithmetic and copies ran while one was open for 0% -> 0% of each run, Pallas kernels for 15% -> 15%
where the time goes in v3:
time: 172 us; the launch traced here: 169 us
  blocking collectives  67.5 us (39%)
  Pallas kernels  41.6 us (24%)
  starting transfers between devices  33.4 us (19%)
  waiting for transfers between devices  25.9 us (15%)
    all_to_all x1, blocking collectives, per_device(): rows = exchange(columns)  28.6 us
    all_to_all x1, blocking collectives, per_device(): columns = exchange(rows.reshape(32, 2 * R, D))  25.2 us
    all_to_all x1, blocking collectives, per_device(): mine = lax.all_to_all(copies, 'z', 0, 0, tiled=True).reshape(192, 512)  13.7 us
    all_to_all x1, starting transfers between devices, per_device(): near = exchange(near)  11.2 us
    all_to_all x1, starting transfers between devices, per_device(): logits = exchange(logits)  10.3 us
    pallas_call x1, Pallas kernels, attend_columns(): pl.pallas_call(column_kernel, grid=(3,), out_shape=jax.ShapeDtypeStruct((...  9.08 us
    ppermute x3, waiting for transfers between devices, per_device(): weights = [mine] + [along[4 - k](mine) for k in (1, 2, 3)]  8.25 us
    all_to_all x1, waiting for transfers between devices, per_device(): logits = exchange(logits)  6.95 us
  transfers between devices with their start and end apart: 12, of which 9 were waited for; matrix products, arithmetic and copies ran while one was open for 0% of the time, Pallas kernels for 15%

profile of v3, /device:TPU:1, one launch (start us, length us, event | category | flops | bytes accessed | tf_op | source)
XLA Modules:
  0.0 169.2 jit_solution(10671107587452744152)
XLA Ops:
  0.0 3.2 %collective-permute-start.1 = (bf16[8,64,768]{2,1,0:T(8,128)(2,1)}, bf16[8,64,768]{2,1,0:T(8,128)(2,1)}, u32[]{:S(2)}, u32[]{:S(2)}) collective-permute-start(bf16[8,64,768]{2,1,0:T(8,128)(2,1)} %refs_4_.1), channel_id=1, source_target_pairs={{0,1},{1,0},{2,3},{3,2},{4,5},{5,4},{6,7},{7,6},{8,9},{9,8},{10,11... | collective-permute-start | bytes 2359304 | tf_op jit(solution)/shard_map/ppermute | solution.py:403
  3.2 1.0 collective-permute-start
  4.2 1.3 collective-permute-done.1.mate_ref
  5.5 6.8 %own_projections.1 = (bf16[6,128,1024]{2,1,0:T(8,128)(2,1)}, bf16[6,64,1024]{2,1,0:T(8,128)(2,1)}, bf16[6,64,1024]{2,1,0:T(8,128)(2,1)}) custom-call(bf16[8,64,768]{2,1,0:T(8,128)(2,1)} %refs_4_.1, bf16[8,64,768]{2,1,0:T(8,128)(2,1)} %collective-permute-done.1.mate_ref, bf16[768,2304]{1,0:T(8,128)(2,1)} %wv_ref.4, bf16[768,2304]{1,0:T(8,128)(2,1)} %wv_ref.4, ...), custom_call_target="tpu_custom_call" | custom-call | flops 2400000000 | bytes 9000000 | tf_op jit(solution)/shard_map/own_projections/pallas_call | solution.py:125
  12.3 2.4 %collective-permute-done.a_ref = bf16[8,64,768]{2,1,0:T(8,128)(2,1)} collective-permute-done((bf16[8,64,768]{2,1,0:T(8,128)(2,1)}, bf16[8,64,768]{2,1,0:T(8,128)(2,1)}, u32[]{:S(2)}, u32[]{:S(2)}) %collective-permute-start) | collective-permute-done | bytes 786464 | tf_op jit(solution)/shard_map/ppermute | solution.py:402
  14.7 1.9 %collective-permute-start.3 = (bf16[8,64,768]{2,1,0:T(8,128)(2,1)}, bf16[8,64,768]{2,1,0:T(8,128)(2,1)}, u32[]{:S(2)}, u32[]{:S(2)}) collective-permute-start(bf16[8,64,768]{2,1,0:T(8,128)(2,1)} %collective-permute-done.a_ref), channel_id=1, source_target_pairs={{0,2},{1,7},{2,4},{3,1},{4,6},{5,3},{6,0},{7,5},{8,10},{9,15},{10,... | collective-permute-start | bytes 2359304 | tf_op jit(solution)/shard_map/ppermute | solution.py:405
  16.6 5.0 %near_logits.1 = bf16[32,48,128]{2,1,0:T(8,128)(2,1)} custom-call(bf16[6,64,1024]{2,1,0:T(8,128)(2,1)} %get-tuple-element.23.key_ref, bf16[8,64,768]{2,1,0:T(8,128)(2,1)} %collective-permute-done.a_ref, bf16[768,2304]{1,0:T(8,128)(2,1)} %wv_ref.4, bf16[6,128,1024]{2,1,0:T(8,128)(2,1)} %get-tuple-element.24.q_ref), custom_call_target="tpu_custom_call" | custom-call | flops 3000000000 | bytes 8000000 | tf_op jit(solution)/shard_map/near_logits/pallas_call | solution.py:139
  21.7 11.2 %all-to-all-start = ((bf16[32,48,128]{2,1,0:T(8,128)(2,1)}), bf16[32,48,128]{2,1,0:T(8,128)(2,1)}, u32[]{:S(2)}, u32[]{:S(2)}) async-start(bf16[32,48,128]{2,1,0:T(8,128)(2,1)} %near_logits.1), calls=%async_computation | async-start | bytes 786432 | tf_op jit(solution)/shard_map/all_to_all | solution.py:408
  32.8 4.3 %collective-permute-done.2.b_ref = bf16[8,64,768]{2,1,0:T(8,128)(2,1)} collective-permute-done((bf16[8,64,768]{2,1,0:T(8,128)(2,1)}, bf16[8,64,768]{2,1,0:T(8,128)(2,1)}, u32[]{:S(2)}, u32[]{:S(2)}) %collective-permute-start.2) | collective-permute-done | bytes 786464 | tf_op jit(solution)/shard_map/ppermute | solution.py:405
  37.1 5.7 %far_logits.1 = bf16[32,48,128]{2,1,0:T(8,128)(2,1)} custom-call(bf16[8,64,768]{2,1,0:T(8,128)(2,1)} %collective-permute-done.2.b_ref, bf16[8,64,768]{2,1,0:T(8,128)(2,1)} %collective-permute-done.3.far_ref, bf16[768,2304]{1,0:T(8,128)(2,1)} %wv_ref.4, bf16[6,128,1024]{2,1,0:T(8,128)(2,1)} %get-tuple-element.24.q_ref), custom_call_target="tpu_custom_call" | custom-call | flops 3000000000 | bytes 7000000 | tf_op jit(solution)/shard_map/far_logits/pallas_call | solution.py:154
  42.9 0.5 all-to-all-done.near_ref
  43.3 10.3 %all-to-all-start.1 = ((bf16[32,48,128]{2,1,0:T(8,128)(2,1)}), bf16[32,48,128]{2,1,0:T(8,128)(2,1)}, u32[]{:S(2)}, u32[]{:S(2)}) async-start(bf16[32,48,128]{2,1,0:T(8,128)(2,1)} %far_logits.1), calls=%async_computation.1 | async-start | bytes 786432 | tf_op jit(solution)/shard_map/all_to_all | solution.py:411
  53.6 5.9 %other_values.1.refs_1_ = bf16[6,192,1024]{2,1,0:T(8,128)(2,1)} custom-call(bf16[8,64,768]{2,1,0:T(8,128)(2,1)} %collective-permute-done.a_ref, bf16[8,64,768]{2,1,0:T(8,128)(2,1)} %collective-permute-done.2.b_ref, bf16[8,64,768]{2,1,0:T(8,128)(2,1)} %collective-permute-done.3.far_ref, bf16[768,2304]{1,0:T(8,128)(2,1)} %wv_ref.4), custom_call_target="tpu_custom_call" | custom-call | flops 2000000000 | bytes 6000000 | tf_op jit(solution)/shard_map/other_values/pallas_call | solution.py:169
  59.6 6.9 %all-to-all-done.1.far_ref = bf16[32,48,128]{2,1,0:T(8,128)(2,1)} async-done(((bf16[32,48,128]{2,1,0:T(8,128)(2,1)}), bf16[32,48,128]{2,1,0:T(8,128)(2,1)}, u32[]{:S(2)}, u32[]{:S(2)}) %all-to-all-start.1) | async-done | bytes 393248 | tf_op jit(solution)/shard_map/all_to_all | solution.py:411
  66.5 2.0 %collective-permute-start.9 = (bf16[6,192,1024]{2,1,0:T(8,128)(2,1)}, bf16[6,192,1024]{2,1,0:T(8,128)(2,1)}, u32[]{:S(2)}, u32[]{:S(2)}) collective-permute-start(bf16[6,192,1024]{2,1,0:T(8,128)(2,1)} %other_values.1.refs_1_), channel_id=1, source_target_pairs={{0,1},{1,0},{2,3},{3,2},{4,5},{5,4},{6,7},{7,6},{8,9},{9,8},{10,11... | collective-permute-start | bytes 7077896 | tf_op jit(solution)/shard_map/ppermute | solution.py:415
  68.6 1.2 sum_logits.1
  69.8 0.6 collective-permute-start.4
  70.4 2.3 %collective-permute-done.4.far_ref = f32[24,256]{1,0:T(8,128)S(1)} collective-permute-done((f32[24,256]{1,0:T(8,128)S(1)}, f32[24,256]{1,0:T(8,128)S(1)}, u32[]{:S(2)}, u32[]{:S(2)}) %collective-permute-start.4) | collective-permute-done | bytes 24608 | tf_op jit(solution)/shard_map/ppermute | solution.py:417
  72.7 0.2 row_weights.1
  72.9 13.7 %all_to_all.25 = bf16[8,24,512]{2,1,0:T(8,128)(2,1)S(1)} all-to-all(bf16[8,24,512]{2,1,0:T(8,128)(2,1)S(1)} %row_weights.1), channel_id=1, replica_groups=mesh['x'=4,'z'=8,'y'=4,'core'=2] {'z'}, dimensions={0} | all-to-all | bytes 393216 | tf_op jit(solution)/shard_map/all_to_all | solution.py:418
  86.6 0.3 collective-permute-start.7
  86.9 1.7 %collective-permute-start.6 = (bf16[192,512]{1,0:T(8,128)(2,1)S(1)}, bf16[192,512]{1,0:T(8,128)(2,1)S(1)}, u32[]{:S(2)}, u32[]{:S(2)}) collective-permute-start(bf16[192,512]{1,0:T(8,128)(2,1)S(1)} %bitcast.6), channel_id=1, source_target_pairs={{0,128},{64,192},{128,0},{192,64},{1,129},{65,193},{129,1},{193,65... | collective-permute-start | bytes 589832 | tf_op jit(solution)/shard_map/ppermute | solution.py:419
  88.7 1.1 collective-permute-start.5
  89.8 3.9 %collective-permute-done.7.w3 = bf16[192,512]{1,0:T(8,128)(2,1)S(1)} collective-permute-done((bf16[192,512]{1,0:T(8,128)(2,1)S(1)}, bf16[192,512]{1,0:T(8,128)(2,1)S(1)}, u32[]{:S(2)}, u32[]{:S(2)}) %collective-permute-start.7) | collective-permute-done | bytes 196640 | tf_op jit(solution)/shard_map/ppermute | solution.py:419
  93.7 2.6 %collective-permute-done.6.w2 = bf16[192,512]{1,0:T(8,128)(2,1)S(1)} collective-permute-done((bf16[192,512]{1,0:T(8,128)(2,1)S(1)}, bf16[192,512]{1,0:T(8,128)(2,1)S(1)}, u32[]{:S(2)}, u32[]{:S(2)}) %collective-permute-start.6) | collective-permute-done | bytes 196640 | tf_op jit(solution)/shard_map/ppermute | solution.py:419
  96.3 1.7 %collective-permute-done.5.w1 = bf16[192,512]{1,0:T(8,128)(2,1)S(1)} collective-permute-done((bf16[192,512]{1,0:T(8,128)(2,1)S(1)}, bf16[192,512]{1,0:T(8,128)(2,1)S(1)}, u32[]{:S(2)}, u32[]{:S(2)}) %collective-permute-start.5) | collective-permute-done | bytes 196640 | tf_op jit(solution)/shard_map/ppermute | solution.py:419
  98.1 0.6 copy-done.4
  98.7 6.2 %row_context.1 = bf16[512,768]{1,0:T(8,128)(2,1)} custom-call(bf16[192,512]{1,0:T(8,128)(2,1)} %bitcast.8, bf16[192,512]{1,0:T(8,128)(2,1)} %copy-done.4, bf16[192,512]{1,0:T(8,128)(2,1)} %copy-done.3, bf16[192,512]{1,0:T(8,128)(2,1)} %copy-done.2, bf16[6,64,1024]{2,1,0:T(8,128)(2,1)} %get-tuple-element.35.refs_0_, ...), custom_call_target="tpu_custom_call" | custom-call | flops 2000000000 | bytes 10000000 | tf_op jit(solution)/shard_map/row_context/pallas_call | solution.py:281
  104.9 25.2 %all_to_all.26.x_ref = bf16[32,16,768]{2,1,0:T(8,128)(2,1)} all-to-all(bf16[32,16,768]{2,1,0:T(8,128)(2,1)} %bitcast.4), channel_id=1, replica_groups=mesh['x'=4,'z'=8,'y'=4,'core'=2] {'x','z'}, dimensions={0} | all-to-all | bytes 1572864 | tf_op jit(solution)/shard_map/all_to_all | solution.py:421
  130.1 9.1 %columns.1 = bf16[32,16,768]{2,1,0:T(8,128)(2,1)} custom-call(bf16[32,16,768]{2,1,0:T(8,128)(2,1)} %all_to_all.26.x_ref, bf16[768,2304]{1,0:T(8,128)(2,1)} %wv_ref.5, bf16[768,2304]{1,0:T(8,128)(2,1)} %wv_ref.5, bf16[768,2304]{1,0:T(8,128)(2,1)} %wv_ref.5, bf16[768,768]{1,0:T(8,128)(2,1)} %wo_ref.1), custom_call_target="tpu_custom_call" | custom-call | flops 5000000000 | bytes 7000000 | tf_op jit(solution)/shard_map/columns/pallas_call | solution.py:346
  139.2 28.6 %all_to_all.27 = bf16[32,16,768]{2,1,0:T(8,128)(2,1)S(1)} all-to-all(bf16[32,16,768]{2,1,0:T(8,128)(2,1)} %columns.1), channel_id=1, replica_groups=mesh['x'=4,'z'=8,'y'=4,'core'=2] {'x','z'}, dimensions={0} | all-to-all | bytes 1572864 | tf_op jit(solution)/shard_map/all_to_all | solution.py:423
  167.8 1.5 finish.1
  (14 shorter events, 0.0 us)
Async XLA Ops:
  0.0 5.5 %collective-permute-start.1 = (bf16[8,64,768]{2,1,0:T(8,128)(2,1)}, bf16[8,64,768]{2,1,0:T(8,128)(2,1)}, u32[]{:S(2)}, u32[]{:S(2)}) collective-permute-start(bf16[8,64,768]{2,1,0:T(8,128)(2,1)} %refs_4_.1), channel_id=1, source_target_pairs={{0,1},{1,0},{2,3},{3,2},{4,5},{5,4},{6,7},{7,6},{8,9},{9,8},{10,11... | collective-permute-start | bytes 2359304 | tf_op jit(solution)/shard_map/ppermute | solution.py:403
  3.2 11.5 %collective-permute-start = (bf16[8,64,768]{2,1,0:T(8,128)(2,1)}, bf16[8,64,768]{2,1,0:T(8,128)(2,1)}, u32[]{:S(2)}, u32[]{:S(2)}) collective-permute-start(bf16[8,64,768]{2,1,0:T(8,128)(2,1)} %refs_4_.1), channel_id=1, source_target_pairs={{0,2},{1,7},{2,4},{3,1},{4,6},{5,3},{6,0},{7,5},{8,10},{9,15},{10,... | collective-permute-start | bytes 2359304 | tf_op jit(solution)/shard_map/ppermute | solution.py:402
  14.7 18.1 %collective-permute-start.3 = (bf16[8,64,768]{2,1,0:T(8,128)(2,1)}, bf16[8,64,768]{2,1,0:T(8,128)(2,1)}, u32[]{:S(2)}, u32[]{:S(2)}) collective-permute-start(bf16[8,64,768]{2,1,0:T(8,128)(2,1)} %collective-permute-done.a_ref), channel_id=1, source_target_pairs={{0,2},{1,7},{2,4},{3,1},{4,6},{5,3},{6,0},{7,5},{8,10},{9,15},{10,... | collective-permute-start | bytes 2359304 | tf_op jit(solution)/shard_map/ppermute | solution.py:405
  16.6 20.5 %collective-permute-start.2 = (bf16[8,64,768]{2,1,0:T(8,128)(2,1)}, bf16[8,64,768]{2,1,0:T(8,128)(2,1)}, u32[]{:S(2)}, u32[]{:S(2)}) collective-permute-start(bf16[8,64,768]{2,1,0:T(8,128)(2,1)} %refs_4_.1), channel_id=1, source_target_pairs={{2,0},{7,1},{4,2},{1,3},{6,4},{3,5},{0,6},{5,7},{10,8},{15,9},{12,... | collective-permute-start | bytes 2359304 | tf_op jit(solution)/shard_map/ppermute | solution.py:405
  21.7 21.7 %all-to-all-start = ((bf16[32,48,128]{2,1,0:T(8,128)(2,1)}), bf16[32,48,128]{2,1,0:T(8,128)(2,1)}, u32[]{:S(2)}, u32[]{:S(2)}) async-start(bf16[32,48,128]{2,1,0:T(8,128)(2,1)} %near_logits.1), calls=%async_computation | async-start | bytes 786432 | tf_op jit(solution)/shard_map/all_to_all | solution.py:408
  43.3 23.2 %all-to-all-start.1 = ((bf16[32,48,128]{2,1,0:T(8,128)(2,1)}), bf16[32,48,128]{2,1,0:T(8,128)(2,1)}, u32[]{:S(2)}, u32[]{:S(2)}) async-start(bf16[32,48,128]{2,1,0:T(8,128)(2,1)} %far_logits.1), calls=%async_computation.1 | async-start | bytes 786432 | tf_op jit(solution)/shard_map/all_to_all | solution.py:411
  66.5 31.5 %collective-permute-start.9 = (bf16[6,192,1024]{2,1,0:T(8,128)(2,1)}, bf16[6,192,1024]{2,1,0:T(8,128)(2,1)}, u32[]{:S(2)}, u32[]{:S(2)}) collective-permute-start(bf16[6,192,1024]{2,1,0:T(8,128)(2,1)} %other_values.1.refs_1_), channel_id=1, source_target_pairs={{0,1},{1,0},{2,3},{3,2},{4,5},{5,4},{6,7},{7,6},{8,9},{9,8},{10,11... | collective-permute-start | bytes 7077896 | tf_op jit(solution)/shard_map/ppermute | solution.py:415
  68.6 21.2 %collective-permute-start.8 = (bf16[6,64,1024]{2,1,0:T(8,128)(2,1)}, bf16[6,64,1024]{2,1,0:T(8,128)(2,1)S(1)}, u32[]{:S(2)}, u32[]{:S(2)}) collective-permute-start(bf16[6,64,1024]{2,1,0:T(8,128)(2,1)} %get-tuple-element.35.refs_0_), channel_id=1, source_target_pairs={{0,1},{1,0},{2,3},{3,2},{4,5},{5,4},{6,7},{7,6},{8,9},{9,8},{10,11... | collective-permute-start | bytes 2359304 | tf_op jit(solution)/shard_map/ppermute | solution.py:415
  69.8 2.9 %collective-permute-start.4 = (f32[24,256]{1,0:T(8,128)S(1)}, f32[24,256]{1,0:T(8,128)S(1)}, u32[]{:S(2)}, u32[]{:S(2)}) collective-permute-start(f32[24,256]{1,0:T(8,128)S(1)} %get-tuple-element.34), channel_id=1, source_target_pairs={{0,1},{1,0},{2,3},{3,2},{4,5},{5,4},{6,7},{7,6},{8,9},{9,8},{10,11... | collective-permute-start | bytes 73736 | tf_op jit(solution)/shard_map/ppermute | solution.py:417
  86.6 11.4 %copy-start.1 = (bf16[8,24,512]{2,1,0:T(8,128)(2,1)}, bf16[8,24,512]{2,1,0:T(8,128)(2,1)S(1)}, u32[]{:S(2)}) copy-start(bf16[8,24,512]{2,1,0:T(8,128)(2,1)S(1)} %all_to_all.25) | copy-start | bytes 589828
  86.6 7.1 %collective-permute-start.7 = (bf16[192,512]{1,0:T(8,128)(2,1)S(1)}, bf16[192,512]{1,0:T(8,128)(2,1)S(1)}, u32[]{:S(2)}, u32[]{:S(2)}) collective-permute-start(bf16[192,512]{1,0:T(8,128)(2,1)S(1)} %bitcast.5), channel_id=1, source_target_pairs={{0,64},{64,128},{128,192},{192,0},{1,65},{65,129},{129,193},{193,1... | collective-permute-start | bytes 589832 | tf_op jit(solution)/shard_map/ppermute | solution.py:419
  86.9 9.4 %collective-permute-start.6 = (bf16[192,512]{1,0:T(8,128)(2,1)S(1)}, bf16[192,512]{1,0:T(8,128)(2,1)S(1)}, u32[]{:S(2)}, u32[]{:S(2)}) collective-permute-start(bf16[192,512]{1,0:T(8,128)(2,1)S(1)} %bitcast.6), channel_id=1, source_target_pairs={{0,128},{64,192},{128,0},{192,64},{1,129},{65,193},{129,1},{193,65... | collective-permute-start | bytes 589832 | tf_op jit(solution)/shard_map/ppermute | solution.py:419
  88.7 9.4 %collective-permute-start.5 = (bf16[192,512]{1,0:T(8,128)(2,1)S(1)}, bf16[192,512]{1,0:T(8,128)(2,1)S(1)}, u32[]{:S(2)}, u32[]{:S(2)}) collective-permute-start(bf16[192,512]{1,0:T(8,128)(2,1)S(1)} %bitcast.7), channel_id=1, source_target_pairs={{0,192},{64,0},{128,64},{192,128},{1,193},{65,1},{129,65},{193,129... | collective-permute-start | bytes 589832 | tf_op jit(solution)/shard_map/ppermute | solution.py:419
  89.8 8.3 %copy-start = (bf16[6,64,1024]{2,1,0:T(8,128)(2,1)}, bf16[6,64,1024]{2,1,0:T(8,128)(2,1)S(1)}, u32[]{:S(2)}) copy-start(bf16[6,64,1024]{2,1,0:T(8,128)(2,1)S(1)} %collective-permute-done.8.refs_2_) | copy-start | bytes 2359300
  93.7 4.3 %copy-start.2 = (bf16[192,512]{1,0:T(8,128)(2,1)}, bf16[192,512]{1,0:T(8,128)(2,1)S(1)}, u32[]{:S(2)}) copy-start(bf16[192,512]{1,0:T(8,128)(2,1)S(1)} %collective-permute-done.7.w3) | copy-start | bytes 589828
  96.3 1.8 %copy-start.3 = (bf16[192,512]{1,0:T(8,128)(2,1)}, bf16[192,512]{1,0:T(8,128)(2,1)S(1)}, u32[]{:S(2)}) copy-start(bf16[192,512]{1,0:T(8,128)(2,1)S(1)} %collective-permute-done.6.w2) | copy-start | bytes 589828
  98.0 0.7 copy-start.4

commit v4 on v3

--- a/solution.py
+++ b/solution.py
@@ -76,12 +76,11 @@
     return jnp.dot(rows, w_ref[...], preferred_element_type=F32).astype(BF)
 
 
-def own_kernel(x_ref, mate_ref, wq_ref, wk_ref, wv_ref, q_ref, k_ref, v_ref):
+def own_kernel(x_ref, mate_ref, wq_ref, wk_ref, q_ref, k_ref):
     for s in range(2):
         rows = normed_rows(x_ref, s)
         store_block(q_ref, 0, 4 * s, project(rows, wq_ref))
         store_block(k_ref, 0, 4 * s, project(rows, wk_ref))
-        store_block(v_ref, 0, 4 * s, project(rows, wv_ref))
         store_block(q_ref, I, 4 * s, project(normed_rows(mate_ref, s), wq_ref))
 
 
@@ -99,12 +98,6 @@
     store_logits(q_ref, keys, rows, out_ref)
 
 
-def value_kernel(a_ref, b_ref, far_ref, wv_ref, v_ref):
-    for n, ref in enumerate((a_ref, b_ref, far_ref)):
-        for s in range(2):
-            store_block(v_ref, n * I, 4 * s, project(normed_rows(ref, s), wv_ref))
-
-
 def block(*shape):
     return pl.BlockSpec(shape, lambda s: (0,) * len(shape))
 
@@ -125,13 +118,13 @@
     return pl.pallas_call(
         own_kernel,
         grid=(1,),
-        out_shape=(TWO, ONE, ONE),
-        in_specs=[whole, whole, weight(0), weight(1), weight(2)],
-        out_specs=(two, one, one),
+        out_shape=(TWO, ONE),
+        in_specs=[whole, whole, weight(0), weight(1)],
+        out_specs=(two, one),
         compiler_params=params(64 * MB),
         cost_estimate=cost(2.4e9, 9e6),
         name="own_projections",
-    )(x, mate, w, w, w)
+    )(x, mate, w, w)
 
 
 def near_logits(keys, a, w, q):
@@ -164,18 +157,60 @@
     )(b, far, w, q)
 
 
-def other_values(a, b, far, w):
-    whole, three = block(R, I, D), (PAIRS, 3 * I, R * 128)
-    return pl.pallas_call(
-        value_kernel,
-        grid=(1,),
-        out_shape=jax.ShapeDtypeStruct(three, BF),
-        in_specs=[whole, whole, whole, weight(2)],
-        out_specs=block(*three),
+HBM = pl.BlockSpec(memory_space=pltpu.HBM)
+BLOCKS = 8
+
+
+def value_kernel(core, *refs):
+    block_refs, w_ref = refs[:BLOCKS], refs[BLOCKS]
+    out_ref, rows, wv, done, loaded, stored, weighed = refs[-7:]
+
+    @pl.when(lax.axis_index("core") == core)
+    def _():
+        weights = pltpu.make_async_copy(w_ref.at[:, pl.ds(2 * D, D)], wv, weighed)
+        loads, stores = [], []
+        for n, ref in enumerate(block_refs):
+            slot = n % 2
+            loads.append(pltpu.make_async_copy(ref, rows.at[slot], loaded.at[slot]))
+            target = out_ref.at[:, pl.ds(n * I, I)]
+            stores.append(pltpu.make_async_copy(done.at[slot], target, stored.at[slot]))
+        weights.start()
+        loads[0].start()
+        weights.wait()
+        for n in range(BLOCKS):
+            slot = n % 2
+            if n + 1 < BLOCKS:
+                loads[n + 1].start()
+            loads[n].wait()
+            if n >= 2:
+                stores[n - 2].wait()
+            for s in range(2):
+                store_block(done.at[slot], 0, 4 * s, project(normed_rows(rows.at[slot], s), wv))
+            stores[n].start()
+        stores[BLOCKS - 2].wait()
+        stores[BLOCKS - 1].wait()
+
+
+def all_values(core, blocks, w, before=None):
+    operands = [*blocks, w] + ([] if before is None else [before])
+    return pl.pallas_call(
+        functools.partial(value_kernel, core),
+        out_shape=jax.ShapeDtypeStruct((PAIRS, BLOCKS * I, R * 128), BF),
+        in_specs=[HBM] * len(operands),
+        out_specs=HBM,
+        input_output_aliases={} if before is None else {BLOCKS + 1: 0},
+        scratch_shapes=[
+            pltpu.VMEM((2, R, I, D), BF),
+            pltpu.VMEM((D, D), BF),
+            pltpu.VMEM((2, PAIRS, I, R * 128), BF),
+            pltpu.SemaphoreType.DMA((2,)),
+            pltpu.SemaphoreType.DMA((2,)),
+            pltpu.SemaphoreType.DMA,
+        ],
         compiler_params=params(64 * MB),
-        cost_estimate=cost(2e9, 6e6),
-        name="other_values",
-    )(a, b, far, w)
+        cost_estimate=cost(5e9, 1.5e7),
+        name="values_%d" % core,
+    )(*operands)
 
 
 def sum_kernel(near_ref, far_ref, mine_ref, mates_ref, rows):
@@ -228,15 +263,10 @@
     return jnp.where(at == source, 1.0, 0.0).astype(BF)
 
 
-HBM = pl.BlockSpec(memory_space=pltpu.HBM)
-
-
 STEP = 3
 
 
-def context_kernel(w0, w1, w2, w3, *refs):
-    value_refs, (x_ref, wo_ref, out_ref), refs = refs[:4], refs[4:7], refs[7:]
-    wall, ctx, x_own, wo, sems = refs
+def context_kernel(w0, w1, w2, w3, value_ref, x_ref, wo_ref, out_ref, wall, ctx, x_own, wo, sems):
     g = pl.program_id(0)
     late = [
         pltpu.make_async_copy(wo_ref, wo, sems.at[0]),
@@ -258,8 +288,7 @@
             head = (g * STEP + n) * 2 + h
             pair.append(wall[lax.div(head, 3), lax.rem(head, 3)])
         weights = jnp.concatenate(pair, axis=0)
-        values = jnp.concatenate([ref[n] for ref in value_refs], axis=0)
-        both = jnp.dot(weights, values, preferred_element_type=F32)
+        both = jnp.dot(weights, value_ref[n], preferred_element_type=F32)
         for r in range(R):
             lanes = slice(r * 128, (r + 1) * 128)
             piece = jnp.where(first, both[:I, lanes], both[I:, lanes]).astype(BF)
@@ -277,14 +306,13 @@
 
 def row_context(weights, values, x, wo):
     whole = pl.BlockSpec((192, 512), lambda p: (0, 0))
-    value = [pl.BlockSpec((STEP, v.shape[1], R * 128), lambda p: (p, 0, 0)) for v in values]
+    value = pl.BlockSpec((STEP, BLOCKS * I, R * 128), lambda p: (p, 0, 0))
     return pl.pallas_call(
         context_kernel,
         grid=(PAIRS // STEP,),
         out_shape=jax.ShapeDtypeStruct((R * I, D), BF),
         in_specs=[whole] * 4
-        + value
-        + [HBM, HBM],
+        + [value, HBM, HBM],
         out_specs=pl.BlockSpec((R * I, D), lambda p: (0, 0)),
         scratch_shapes=[
             pltpu.VMEM((4, 3, I, 512), BF),
@@ -296,7 +324,7 @@
         compiler_params=params(62 * MB),
         cost_estimate=cost(2e9, 1e7),
         name="row_context",
-    )(*weights, *values, x, wo)
+    )(*weights, values, x, wo)
 
 
 def column_kernel(x_ref, wq_ref, wk_ref, wv_ref, wo_ref, out_ref, normed, context, wo, sem):
@@ -399,22 +427,25 @@
     on, back = [functools.partial(lax.ppermute, axis_name=("y", "core"), perm=way) for way in ways]
     along = [functools.partial(lax.ppermute, axis_name="x", perm=shift(4, k)) for k in range(4)]
 
-    a = on(x)
-    q, keys, own_values = own_projections(x, mate(x), w_row)
+    a, own = on(x), mate(x)
+    q, keys = own_projections(x, own, w_row)
     later, q = lax.optimization_barrier((x, q))
     b, far = back(later), on(a)
     near = near_logits(keys, a, w_row, q)
     b, far, _ = lax.optimization_barrier((b, far, near))
     near = exchange(near)
     logits = far_logits(b, far, w_row, q)
-    a, b, far, logits, near = lax.optimization_barrier((a, b, far, logits, near))
+    b, far, logits = lax.optimization_barrier((b, far, logits))
+    logits, near = lax.optimization_barrier((logits, near))
+    blocks = (x, a, b, far, own, mate(a), mate(b), mate(far))
     logits = exchange(logits)
-    values = other_values(a, b, far, w_row)
+    values = all_values(0, blocks, w_row)
     logits, values = lax.optimization_barrier((logits, values))
-    values = [own_values, values]
-    values += [mate(v) for v in values]
-    own, other = sum_logits(near, logits)
-    copies = row_weights(own, mate(other), float((64 * 256) ** -0.5), 8)
+    mine, other = sum_logits(near, logits)
+    copies = row_weights(mine, mate(other), float((64 * 256) ** -0.5), 8)
+    copies, values = lax.optimization_barrier((copies, values))
+    values = all_values(1, blocks, w_row, values)
+    copies, values = lax.optimization_barrier((copies, values))
     mine = lax.all_to_all(copies, "z", 0, 0, tiled=True).reshape(192, 512)
     weights = [mine] + [along[4 - k](mine) for k in (1, 2, 3)]
     rows = row_context(weights, values, x, wo_row)

time: 172 us -> 166 us (0.965); the launches traced: 169 us -> 165 us
  blocking collectives: 67.5 us -> 56.4 us
  Pallas kernels: 41.6 us -> 45.7 us
  starting transfers between devices: 33.4 us -> 37.2 us
    all_to_all x1, blocking collectives: 28.6 us -> 23.2 us  [per_device(): rows = exchange(columns)]
    all_to_all x1, waiting for transfers between devices: 6.95 us -> 11.9 us  [per_device(): logits = exchange(logits)]
    all_to_all x1, blocking collectives: 25.2 us -> 20.5 us  [per_device(): columns = exchange(rows.reshape(32, 2 * R, D))]
    pallas_call x2 -> x3, Pallas kernels: 12.7 us -> 17 us  [the longest x2 11.3 us: all_values(): pl.pallas_call(functools.partial(value_kernel, core), out_shape=jax.Shape...]
    ppermute x3, waiting for transfers between devices: 8.25 us -> 4.56 us  [per_device(): weights = [mine] + [along[4 - k](mine) for k in (1, 2, 3)]]
    ppermute x5 -> x6, starting transfers between devices: 6.88 us -> 10.2 us  [the longest x2 4.24 us: per_device(): a, own = (on(x), mate(x))]
    ppermute x2, waiting for transfers between devices: 4.3 us -> 2.3 us  [per_device(): b, far = (back(later), on(a))]
    ppermute x5 -> x6, waiting for transfers between devices: 5.94 us -> 5.58 us  [the longest x2 4.72 us: per_device(): a, own = (on(x), mate(x))]
  transfers between devices with their start and end apart: 12 -> 13, of which waited for: 9 -> 8; matrix products, arithmetic and copies ran while one was open for 0% -> 0% of each run, Pallas kernels for 15% -> 10%
where the time goes in v4:
time: 166 us; the launch traced here: 165 us
  blocking collectives  56.4 us (34%)
  Pallas kernels  45.7 us (28%)
  starting transfers between devices  37.2 us (22%)
  waiting for transfers between devices  24.4 us (15%)
    all_to_all x1, blocking collectives, per_device(): rows = exchange(columns)  23.2 us
    all_to_all x1, blocking collectives, per_device(): columns = exchange(rows.reshape(32, 2 * R, D))  20.5 us
    all_to_all x1, blocking collectives, per_device(): mine = lax.all_to_all(copies, 'z', 0, 0, tiled=True).reshape(192, 512)  12.7 us
    all_to_all x1, waiting for transfers between devices, per_device(): logits = exchange(logits)  11.9 us
    pallas_call x2, Pallas kernels, all_values(): pl.pallas_call(functools.partial(value_kernel, core), out_shape=jax.Shape...  11.3 us
    all_to_all x1, starting transfers between devices, per_device(): near = exchange(near)  11.2 us
    all_to_all x1, starting transfers between devices, per_device(): logits = exchange(logits)  10.1 us
    pallas_call x1, Pallas kernels, attend_columns(): pl.pallas_call(column_kernel, grid=(3,), out_shape=jax.ShapeDtypeStruct((...  9.08 us
  transfers between devices with their start and end apart: 13, of which 8 were waited for; matrix products, arithmetic and copies ran while one was open for 0% of the time, Pallas kernels for 10%

profile of v4, /device:TPU:1, one launch (start us, length us, event | category | flops | bytes accessed | tf_op | source)
XLA Modules:
  0.0 165.2 jit_solution(5222931470655098820)
XLA Ops:
  0.0 3.2 %collective-permute-start = (bf16[8,64,768]{2,1,0:T(8,128)(2,1)}, bf16[8,64,768]{2,1,0:T(8,128)(2,1)}, u32[]{:S(2)}, u32[]{:S(2)}) collective-permute-start(bf16[8,64,768]{2,1,0:T(8,128)(2,1)} %x_ref.3), channel_id=1, source_target_pairs={{0,1},{1,0},{2,3},{3,2},{4,5},{5,4},{6,7},{7,6},{8,9},{9,8},{10,11... | collective-permute-start | bytes 2359304 | tf_op jit(solution)/shard_map/ppermute | solution.py:430
  3.2 1.0 collective-permute-start.2
  4.2 1.3 collective-permute-done.mate_ref.refs_4_
  5.5 5.7 %own_projections.1 = (bf16[6,128,1024]{2,1,0:T(8,128)(2,1)}, bf16[6,64,1024]{2,1,0:T(8,128)(2,1)}) custom-call(bf16[8,64,768]{2,1,0:T(8,128)(2,1)} %x_ref.3, bf16[8,64,768]{2,1,0:T(8,128)(2,1)} %collective-permute-done.mate_ref.refs_4_, bf16[768,2304]{1,0:T(8,128)(2,1)} %refs_8_.3, bf16[768,2304]{1,0:T(8,128)(2,1)} %refs_8_.3), custom_call_target="tpu_custom_call" | custom-call | flops 2400000000 | bytes 9000000 | tf_op jit(solution)/shard_map/own_projections/pallas_call | solution.py:118
  11.2 3.5 %collective-permute-done.2.a_ref.refs_1_ = bf16[8,64,768]{2,1,0:T(8,128)(2,1)} collective-permute-done((bf16[8,64,768]{2,1,0:T(8,128)(2,1)}, bf16[8,64,768]{2,1,0:T(8,128)(2,1)}, u32[]{:S(2)}, u32[]{:S(2)}) %collective-permute-start.2) | collective-permute-done | bytes 786464 | tf_op jit(solution)/shard_map/ppermute | solution.py:430
  14.7 1.9 %collective-permute-start.3 = (bf16[8,64,768]{2,1,0:T(8,128)(2,1)}, bf16[8,64,768]{2,1,0:T(8,128)(2,1)}, u32[]{:S(2)}, u32[]{:S(2)}) collective-permute-start(bf16[8,64,768]{2,1,0:T(8,128)(2,1)} %collective-permute-done.2.a_ref.refs_1_), channel_id=1, source_target_pairs={{0,2},{1,7},{2,4},{3,1},{4,6},{5,3},{6,0},{7,5},{8,10},{9,15},{10,... | collective-permute-start | bytes 2359304 | tf_op jit(solution)/shard_map/ppermute | solution.py:433
  16.6 5.0 %near_logits.1 = bf16[32,48,128]{2,1,0:T(8,128)(2,1)} custom-call(bf16[6,64,1024]{2,1,0:T(8,128)(2,1)} %get-tuple-element.26.key_ref, bf16[8,64,768]{2,1,0:T(8,128)(2,1)} %collective-permute-done.2.a_ref.refs_1_, bf16[768,2304]{1,0:T(8,128)(2,1)} %refs_8_.3, bf16[6,128,1024]{2,1,0:T(8,128)(2,1)} %get-tuple-element.27.q_ref), custom_call_target="tpu_custom_call" | custom-call | flops 3000000000 | bytes 8000000 | tf_op jit(solution)/shard_map/near_logits/pallas_call | solution.py:132
  21.6 11.2 %all-to-all-start = ((bf16[32,48,128]{2,1,0:T(8,128)(2,1)}), bf16[32,48,128]{2,1,0:T(8,128)(2,1)}, u32[]{:S(2)}, u32[]{:S(2)}) async-start(bf16[32,48,128]{2,1,0:T(8,128)(2,1)} %near_logits.1), calls=%async_computation | async-start | bytes 786432 | tf_op jit(solution)/shard_map/all_to_all | solution.py:436
  32.8 2.0 %collective-permute-start.4 = (bf16[8,64,768]{2,1,0:T(8,128)(2,1)}, bf16[8,64,768]{2,1,0:T(8,128)(2,1)}, u32[]{:S(2)}, u32[]{:S(2)}) collective-permute-start(bf16[8,64,768]{2,1,0:T(8,128)(2,1)} %collective-permute-done.2.a_ref.refs_1_), channel_id=1, source_target_pairs={{0,1},{1,0},{2,3},{3,2},{4,5},{5,4},{6,7},{7,6},{8,9},{9,8},{10,11... | collective-permute-start | bytes 2359304 | tf_op jit(solution)/shard_map/ppermute | solution.py:440
  34.8 2.3 %collective-permute-done.1.b_ref.refs_2_ = bf16[8,64,768]{2,1,0:T(8,128)(2,1)} collective-permute-done((bf16[8,64,768]{2,1,0:T(8,128)(2,1)}, bf16[8,64,768]{2,1,0:T(8,128)(2,1)}, u32[]{:S(2)}, u32[]{:S(2)}) %collective-permute-start.1) | collective-permute-done | bytes 786464 | tf_op jit(solution)/shard_map/ppermute | solution.py:433
  37.1 5.7 %far_logits.1 = bf16[32,48,128]{2,1,0:T(8,128)(2,1)} custom-call(bf16[8,64,768]{2,1,0:T(8,128)(2,1)} %collective-permute-done.1.b_ref.refs_2_, bf16[8,64,768]{2,1,0:T(8,128)(2,1)} %collective-permute-done.3.far_ref.refs_3_, bf16[768,2304]{1,0:T(8,128)(2,1)} %refs_8_.3, bf16[6,128,1024]{2,1,0:T(8,128)(2,1)} %get-tuple-element.27.q_ref), custom_call_target="tpu_custom_call" | custom-call | flops 3000000000 | bytes 7000000 | tf_op jit(solution)/shard_map/far_logits/pallas_call | solution.py:147
  42.9 1.0 collective-permute-start.5
  43.8 10.1 %all-to-all-start.1 = ((bf16[32,48,128]{2,1,0:T(8,128)(2,1)}), bf16[32,48,128]{2,1,0:T(8,128)(2,1)}, u32[]{:S(2)}, u32[]{:S(2)}) async-start(bf16[32,48,128]{2,1,0:T(8,128)(2,1)} %far_logits.1), calls=%async_computation.1 | async-start | bytes 786432 | tf_op jit(solution)/shard_map/all_to_all | solution.py:441
  54.3 11.9 %all-to-all-done.1.far_ref = bf16[32,48,128]{2,1,0:T(8,128)(2,1)} async-done(((bf16[32,48,128]{2,1,0:T(8,128)(2,1)}), bf16[32,48,128]{2,1,0:T(8,128)(2,1)}, u32[]{:S(2)}, u32[]{:S(2)}) %all-to-all-start.1) | async-done | bytes 393248 | tf_op jit(solution)/shard_map/all_to_all | solution.py:441
  66.2 1.2 sum_logits.1
  67.4 3.0 %collective-permute-start.7 = (f32[24,256]{1,0:T(8,128)S(1)}, f32[24,256]{1,0:T(8,128)S(1)}, u32[]{:S(2)}, u32[]{:S(2)}) collective-permute-start(f32[24,256]{1,0:T(8,128)S(1)} %get-tuple-element.37), channel_id=1, source_target_pairs={{0,1},{1,0},{2,3},{3,2},{4,5},{5,4},{6,7},{7,6},{8,9},{9,8},{10,11... | collective-permute-start | bytes 73736 | tf_op jit(solution)/shard_map/ppermute | solution.py:445
  70.4 0.8 collective-permute-done.7.far_ref
  71.4 0.7 copy-done
  72.1 11.1 %values_1.1.value_ref = bf16[6,512,1024]{2,1,0:T(8,128)(2,1)} custom-call(bf16[8,64,768]{2,1,0:T(8,128)(2,1)} %x_ref.3, bf16[8,64,768]{2,1,0:T(8,128)(2,1)} %collective-permute-done.2.a_ref.refs_1_, bf16[8,64,768]{2,1,0:T(8,128)(2,1)} %collective-permute-done.1.b_ref.refs_2_, ...), custom_call_target="tpu_custom_call", output_to_operand_aliasing={{}: (9, {})} | custom-call | flops 5000000000 | bytes 15000000 | tf_op jit(solution)/shard_map/values_1/pallas_call | solution.py:196
  83.2 12.7 %all_to_all.25 = bf16[8,24,512]{2,1,0:T(8,128)(2,1)S(1)} all-to-all(bf16[8,24,512]{2,1,0:T(8,128)(2,1)} %copy-done), channel_id=1, replica_groups=mesh['x'=4,'z'=8,'y'=4,'core'=2] {'z'}, dimensions={0} | all-to-all | bytes 393216 | tf_op jit(solution)/shard_map/all_to_all | solution.py:449
  95.8 0.3 collective-permute-start.10
  96.2 2.4 %collective-permute-start.9 = (bf16[192,512]{1,0:T(8,128)(2,1)S(1)}, bf16[192,512]{1,0:T(8,128)(2,1)S(1)}, u32[]{:S(2)}, u32[]{:S(2)}) collective-permute-start(bf16[192,512]{1,0:T(8,128)(2,1)S(1)} %bitcast.6), channel_id=1, source_target_pairs={{0,128},{64,192},{128,0},{192,64},{1,129},{65,193},{129,1},{193,65... | collective-permute-start | bytes 589832 | tf_op jit(solution)/shard_map/ppermute | solution.py:450
  98.6 1.1 collective-permute-start.8
  99.7 1.9 %collective-permute-done.10.w3 = bf16[192,512]{1,0:T(8,128)(2,1)S(1)} collective-permute-done((bf16[192,512]{1,0:T(8,128)(2,1)S(1)}, bf16[192,512]{1,0:T(8,128)(2,1)S(1)}, u32[]{:S(2)}, u32[]{:S(2)}) %collective-permute-start.10) | collective-permute-done | bytes 196640 | tf_op jit(solution)/shard_map/ppermute | solution.py:450
  101.6 2.2 %collective-permute-done.9.w2 = bf16[192,512]{1,0:T(8,128)(2,1)S(1)} collective-permute-done((bf16[192,512]{1,0:T(8,128)(2,1)S(1)}, bf16[192,512]{1,0:T(8,128)(2,1)S(1)}, u32[]{:S(2)}, u32[]{:S(2)}) %collective-permute-start.9) | collective-permute-done | bytes 196640 | tf_op jit(solution)/shard_map/ppermute | solution.py:450
  103.7 0.5 collective-permute-done.8.w1
  104.4 0.7 copy-done.4
  105.1 5.9 %row_context.1 = bf16[512,768]{1,0:T(8,128)(2,1)} custom-call(bf16[192,512]{1,0:T(8,128)(2,1)} %bitcast.8, bf16[192,512]{1,0:T(8,128)(2,1)} %copy-done.4, bf16[192,512]{1,0:T(8,128)(2,1)} %copy-done.3, bf16[192,512]{1,0:T(8,128)(2,1)} %copy-done.2, bf16[6,512,1024]{2,1,0:T(8,128)(2,1)} %values_1.1.value_ref, bf16[8,64,768]{2,1,0:T(8,128)(2,1)} %x_ref.3, ...), custom_call_target="tpu_custom_call" | custom-call | flops 2000000000 | bytes 10000000 | tf_op jit(solution)/shard_map/row_context/pallas_call | solution.py:310
  111.0 20.5 %all_to_all.26.x_ref = bf16[32,16,768]{2,1,0:T(8,128)(2,1)} all-to-all(bf16[32,16,768]{2,1,0:T(8,128)(2,1)} %bitcast.4), channel_id=1, replica_groups=mesh['x'=4,'z'=8,'y'=4,'core'=2] {'x','z'}, dimensions={0} | all-to-all | bytes 1572864 | tf_op jit(solution)/shard_map/all_to_all | solution.py:452
  131.5 9.1 %columns.1 = bf16[32,16,768]{2,1,0:T(8,128)(2,1)} custom-call(bf16[32,16,768]{2,1,0:T(8,128)(2,1)} %all_to_all.26.x_ref, bf16[768,2304]{1,0:T(8,128)(2,1)} %wv_ref.1, bf16[768,2304]{1,0:T(8,128)(2,1)} %wv_ref.1, bf16[768,2304]{1,0:T(8,128)(2,1)} %wv_ref.1, bf16[768,768]{1,0:T(8,128)(2,1)} %wo_ref.3), custom_call_target="tpu_custom_call" | custom-call | flops 5000000000 | bytes 7000000 | tf_op jit(solution)/shard_map/columns/pallas_call | solution.py:374
  140.6 23.2 %all_to_all.27 = bf16[32,16,768]{2,1,0:T(8,128)(2,1)S(1)} all-to-all(bf16[32,16,768]{2,1,0:T(8,128)(2,1)} %columns.1), channel_id=1, replica_groups=mesh['x'=4,'z'=8,'y'=4,'core'=2] {'x','z'}, dimensions={0} | all-to-all | bytes 1572864 | tf_op jit(solution)/shard_map/all_to_all | solution.py:454
  163.8 1.5 finish.1
  (17 shorter events, 0.6 us)
Async XLA Ops:
  0.0 5.5 %collective-permute-start = (bf16[8,64,768]{2,1,0:T(8,128)(2,1)}, bf16[8,64,768]{2,1,0:T(8,128)(2,1)}, u32[]{:S(2)}, u32[]{:S(2)}) collective-permute-start(bf16[8,64,768]{2,1,0:T(8,128)(2,1)} %x_ref.3), channel_id=1, source_target_pairs={{0,1},{1,0},{2,3},{3,2},{4,5},{5,4},{6,7},{7,6},{8,9},{9,8},{10,11... | collective-permute-start | bytes 2359304 | tf_op jit(solution)/shard_map/ppermute | solution.py:430
  3.2 11.5 %collective-permute-start.2 = (bf16[8,64,768]{2,1,0:T(8,128)(2,1)}, bf16[8,64,768]{2,1,0:T(8,128)(2,1)}, u32[]{:S(2)}, u32[]{:S(2)}) collective-permute-start(bf16[8,64,768]{2,1,0:T(8,128)(2,1)} %x_ref.3), channel_id=1, source_target_pairs={{0,2},{1,7},{2,4},{3,1},{4,6},{5,3},{6,0},{7,5},{8,10},{9,15},{10,... | collective-permute-start | bytes 2359304 | tf_op jit(solution)/shard_map/ppermute | solution.py:430
  14.7 20.1 %collective-permute-start.3 = (bf16[8,64,768]{2,1,0:T(8,128)(2,1)}, bf16[8,64,768]{2,1,0:T(8,128)(2,1)}, u32[]{:S(2)}, u32[]{:S(2)}) collective-permute-start(bf16[8,64,768]{2,1,0:T(8,128)(2,1)} %collective-permute-done.2.a_ref.refs_1_), channel_id=1, source_target_pairs={{0,2},{1,7},{2,4},{3,1},{4,6},{5,3},{6,0},{7,5},{8,10},{9,15},{10,... | collective-permute-start | bytes 2359304 | tf_op jit(solution)/shard_map/ppermute | solution.py:433
  16.6 20.5 %collective-permute-start.1 = (bf16[8,64,768]{2,1,0:T(8,128)(2,1)}, bf16[8,64,768]{2,1,0:T(8,128)(2,1)}, u32[]{:S(2)}, u32[]{:S(2)}) collective-permute-start(bf16[8,64,768]{2,1,0:T(8,128)(2,1)} %x_ref.3), channel_id=1, source_target_pairs={{2,0},{7,1},{4,2},{1,3},{6,4},{3,5},{0,6},{5,7},{10,8},{15,9},{12,... | collective-permute-start | bytes 2359304 | tf_op jit(solution)/shard_map/ppermute | solution.py:433
  21.6 22.2 %all-to-all-start = ((bf16[32,48,128]{2,1,0:T(8,128)(2,1)}), bf16[32,48,128]{2,1,0:T(8,128)(2,1)}, u32[]{:S(2)}, u32[]{:S(2)}) async-start(bf16[32,48,128]{2,1,0:T(8,128)(2,1)} %near_logits.1), calls=%async_computation | async-start | bytes 786432 | tf_op jit(solution)/shard_map/all_to_all | solution.py:436
  32.8 21.2 %collective-permute-start.4 = (bf16[8,64,768]{2,1,0:T(8,128)(2,1)}, bf16[8,64,768]{2,1,0:T(8,128)(2,1)}, u32[]{:S(2)}, u32[]{:S(2)}) collective-permute-start(bf16[8,64,768]{2,1,0:T(8,128)(2,1)} %collective-permute-done.2.a_ref.refs_1_), channel_id=1, source_target_pairs={{0,1},{1,0},{2,3},{3,2},{4,5},{5,4},{6,7},{7,6},{8,9},{9,8},{10,11... | collective-permute-start | bytes 2359304 | tf_op jit(solution)/shard_map/ppermute | solution.py:440
  42.9 11.1 %collective-permute-start.5 = (bf16[8,64,768]{2,1,0:T(8,128)(2,1)}, bf16[8,64,768]{2,1,0:T(8,128)(2,1)}, u32[]{:S(2)}, u32[]{:S(2)}) collective-permute-start(bf16[8,64,768]{2,1,0:T(8,128)(2,1)} %collective-permute-done.1.b_ref.refs_2_), channel_id=1, source_target_pairs={{0,1},{1,0},{2,3},{3,2},{4,5},{5,4},{6,7},{7,6},{8,9},{9,8},{10,11... | collective-permute-start | bytes 2359304 | tf_op jit(solution)/shard_map/ppermute | solution.py:440
  43.8 10.2 %collective-permute-start.6 = (bf16[8,64,768]{2,1,0:T(8,128)(2,1)}, bf16[8,64,768]{2,1,0:T(8,128)(2,1)}, u32[]{:S(2)}, u32[]{:S(2)}) collective-permute-start(bf16[8,64,768]{2,1,0:T(8,128)(2,1)} %collective-permute-done.3.far_ref.refs_3_), channel_id=1, source_target_pairs={{0,1},{1,0},{2,3},{3,2},{4,5},{5,4},{6,7},{7,6},{8,9},{9,8},{10,11... | collective-permute-start | bytes 2359304 | tf_op jit(solution)/shard_map/ppermute | solution.py:440
  43.8 22.4 %all-to-all-start.1 = ((bf16[32,48,128]{2,1,0:T(8,128)(2,1)}), bf16[32,48,128]{2,1,0:T(8,128)(2,1)}, u32[]{:S(2)}, u32[]{:S(2)}) async-start(bf16[32,48,128]{2,1,0:T(8,128)(2,1)} %far_logits.1), calls=%async_computation.1 | async-start | bytes 786432 | tf_op jit(solution)/shard_map/all_to_all | solution.py:441
  67.4 3.8 %collective-permute-start.7 = (f32[24,256]{1,0:T(8,128)S(1)}, f32[24,256]{1,0:T(8,128)S(1)}, u32[]{:S(2)}, u32[]{:S(2)}) collective-permute-start(f32[24,256]{1,0:T(8,128)S(1)} %get-tuple-element.37), channel_id=1, source_target_pairs={{0,1},{1,0},{2,3},{3,2},{4,5},{5,4},{6,7},{7,6},{8,9},{9,8},{10,11... | collective-permute-start | bytes 73736 | tf_op jit(solution)/shard_map/ppermute | solution.py:445
  71.4 0.7 copy-start
  95.8 8.4 %copy-start.1 = (bf16[8,24,512]{2,1,0:T(8,128)(2,1)}, bf16[8,24,512]{2,1,0:T(8,128)(2,1)S(1)}, u32[]{:S(2)}) copy-start(bf16[8,24,512]{2,1,0:T(8,128)(2,1)S(1)} %all_to_all.25) | copy-start | bytes 589828
  95.8 5.7 %collective-permute-start.10 = (bf16[192,512]{1,0:T(8,128)(2,1)S(1)}, bf16[192,512]{1,0:T(8,128)(2,1)S(1)}, u32[]{:S(2)}, u32[]{:S(2)}) collective-permute-start(bf16[192,512]{1,0:T(8,128)(2,1)S(1)} %bitcast.5), channel_id=1, source_target_pairs={{0,64},{64,128},{128,192},{192,0},{1,65},{65,129},{129,193},{193,1... | collective-permute-start | bytes 589832 | tf_op jit(solution)/shard_map/ppermute | solution.py:450
  96.2 7.6 %collective-permute-start.9 = (bf16[192,512]{1,0:T(8,128)(2,1)S(1)}, bf16[192,512]{1,0:T(8,128)(2,1)S(1)}, u32[]{:S(2)}, u32[]{:S(2)}) collective-permute-start(bf16[192,512]{1,0:T(8,128)(2,1)S(1)} %bitcast.6), channel_id=1, source_target_pairs={{0,128},{64,192},{128,0},{192,64},{1,129},{65,193},{129,1},{193,65... | collective-permute-start | bytes 589832 | tf_op jit(solution)/shard_map/ppermute | solution.py:450
  98.6 5.7 %collective-permute-start.8 = (bf16[192,512]{1,0:T(8,128)(2,1)S(1)}, bf16[192,512]{1,0:T(8,128)(2,1)S(1)}, u32[]{:S(2)}, u32[]{:S(2)}) collective-permute-start(bf16[192,512]{1,0:T(8,128)(2,1)S(1)} %bitcast.7), channel_id=1, source_target_pairs={{0,192},{64,0},{128,64},{192,128},{1,193},{65,1},{129,65},{193,129... | collective-permute-start | bytes 589832 | tf_op jit(solution)/shard_map/ppermute | solution.py:450
  101.6 2.7 %copy-start.2 = (bf16[192,512]{1,0:T(8,128)(2,1)}, bf16[192,512]{1,0:T(8,128)(2,1)S(1)}, u32[]{:S(2)}) copy-start(bf16[192,512]{1,0:T(8,128)(2,1)S(1)} %collective-permute-done.10.w3) | copy-start | bytes 589828
  103.7 0.7 copy-start.3
  104.4 0.7 copy-start.4

commit v5 on v4

--- a/solution.py
+++ b/solution.py
@@ -91,11 +91,14 @@
     store_logits(q_ref, keys, rows, out_ref)
 
 
-def far_kernel(b_ref, far_ref, wk_ref, q_ref, out_ref, keys, rows):
+def far_kernel(b_ref, far_ref, wk_ref, q_ref, out_ref, keys, rows, q, sem):
+    queries = pltpu.make_async_copy(q_ref, q, sem)
+    queries.start()
     for at, ref in ((0, b_ref), (I, far_ref)):
         for s in range(2):
             store_block(keys, at, 4 * s, project(normed_rows(ref, s), wk_ref))
-    store_logits(q_ref, keys, rows, out_ref)
+    queries.wait()
+    store_logits(q, keys, rows, out_ref)
 
 
 def block(*shape):
@@ -106,6 +109,7 @@
     return pl.BlockSpec((D, D), lambda s: (0, part))
 
 
+HBM = pl.BlockSpec(memory_space=pltpu.HBM)
 LOGITS = jax.ShapeDtypeStruct((32, 48, 128), BF)
 ONE = jax.ShapeDtypeStruct((PAIRS, I, R * 128), BF)
 TWO = jax.ShapeDtypeStruct((PAIRS, 2 * I, R * 128), BF)
@@ -148,16 +152,15 @@
         far_kernel,
         grid=(1,),
         out_shape=LOGITS,
-        in_specs=[whole, whole, weight(1), block(*TWO.shape)],
+        in_specs=[whole, whole, weight(1), HBM],
         out_specs=block(32, 48, 128),
-        scratch_shapes=[KEYS, ROWS],
+        scratch_shapes=[KEYS, ROWS, KEYS, pltpu.SemaphoreType.DMA],
         compiler_params=params(64 * MB),
         cost_estimate=cost(3e9, 7e6),
         name="far_logits",
     )(b, far, w, q)
 
 
-HBM = pl.BlockSpec(memory_space=pltpu.HBM)
 BLOCKS = 8
 
 
@@ -207,7 +210,7 @@
             pltpu.SemaphoreType.DMA((2,)),
             pltpu.SemaphoreType.DMA,
         ],
-        compiler_params=params(64 * MB),
+        compiler_params=params(62 * MB if core else 64 * MB),
         cost_estimate=cost(5e9, 1.5e7),
         name="values_%d" % core,
     )(*operands)
@@ -346,19 +349,18 @@
     v = jnp.dot(rows, wv_ref[...], preferred_element_type=F32).astype(BF)
     first = first_head(256)
     zero = jnp.zeros((256, 128), BF)
-    for c in range(2):
-        rows = slice(c * 256, (c + 1) * 256)
-        for p in range(2):
-            at = (rows, slice(p * 128, (p + 1) * 128))
-            both = jnp.concatenate(
-                [jnp.where(first, q[at], zero), jnp.where(first, zero, q[at])], axis=0
-            )
-            scores = lax.dot_general(both, k[at], NT, preferred_element_type=F32)
-            top = jnp.max(scores, axis=-1, keepdims=True)
-            powers = jnp.exp2((scores - top) * (64**-0.5 * LOG2E))
-            weight = jnp.sum(powers, axis=-1, keepdims=True)
-            mixed = jnp.dot(powers.astype(BF), v[at], preferred_element_type=F32) / weight
-            context[2 * g + p, rows] = jnp.where(first, mixed[:256], mixed[256:]).astype(BF)
+    cells = [(c, p) for c in range(2) for p in range(2)]
+    ats = [(slice(c * 256, (c + 1) * 256), slice(p * 128, (p + 1) * 128)) for c, p in cells]
+    scores = []
+    for at in ats:
+        both = jnp.concatenate([jnp.where(first, q[at], zero), jnp.where(first, zero, q[at])], axis=0)
+        scores.append(lax.dot_general(both, k[at], NT, preferred_element_type=F32))
+    for (c, p), at, score in zip(cells, ats, scores):
+        top = jnp.max(score, axis=-1, keepdims=True)
+        powers = jnp.exp2((score - top) * (64**-0.5 * LOG2E))
+        weight = jnp.sum(powers, axis=-1, keepdims=True)
+        mixed = jnp.dot(powers.astype(BF), v[at], preferred_element_type=F32) / weight
+        context[2 * g + p, at[0]] = jnp.where(first, mixed[:256], mixed[256:]).astype(BF)
 
     @pl.when(g == 2)
     def _():

time: 166 us -> 164 us (0.988)
  no operation moved by 1% of the time
where the time goes in v5:
time: 164 us; the launch traced here: 163 us
  blocking collectives  56 us (34%)
  Pallas kernels  44.7 us (27%)
  starting transfers between devices  37.3 us (23%)
  waiting for transfers between devices  24.3 us (15%)
    all_to_all x1, blocking collectives, per_device(): rows = exchange(columns)  23.1 us
    all_to_all x1, blocking collectives, per_device(): columns = exchange(rows.reshape(32, 2 * R, D))  20.4 us
    all_to_all x1, blocking collectives, per_device(): mine = lax.all_to_all(copies, 'z', 0, 0, tiled=True).reshape(192, 512)  12.5 us
    all_to_all x1, waiting for transfers between devices, per_device(): logits = exchange(logits)  12 us
    pallas_call x2, Pallas kernels, all_values(): pl.pallas_call(functools.partial(value_kernel, core), out_shape=jax.Shape...  11.6 us
    all_to_all x1, starting transfers between devices, per_device(): near = exchange(near)  11.2 us
    all_to_all x1, starting transfers between devices, per_device(): logits = exchange(logits)  10.1 us
    pallas_call x1, Pallas kernels, attend_columns(): pl.pallas_call(column_kernel, grid=(3,), out_shape=jax.ShapeDtypeStruct((...  8.22 us
  transfers between devices with their start and end apart: 13, of which 8 were waited for; matrix products, arithmetic and copies ran while one was open for 0% of the time, Pallas kernels for 10%

profile of v5, /device:TPU:1, one launch (start us, length us, event | category | flops | bytes accessed | tf_op | source)
XLA Modules:
  0.0 163.4 jit_solution(11624611732630452192)
XLA Ops:
  0.0 3.2 %collective-permute-start = (bf16[8,64,768]{2,1,0:T(8,128)(2,1)}, bf16[8,64,768]{2,1,0:T(8,128)(2,1)}, u32[]{:S(2)}, u32[]{:S(2)}) collective-permute-start(bf16[8,64,768]{2,1,0:T(8,128)(2,1)} %x_ref.3), channel_id=1, source_target_pairs={{0,1},{1,0},{2,3},{3,2},{4,5},{5,4},{6,7},{7,6},{8,9},{9,8},{10,11... | collective-permute-start | bytes 2359304 | tf_op jit(solution)/shard_map/ppermute | solution.py:432
  3.2 1.0 collective-permute-start.2
  4.2 1.3 collective-permute-done.mate_ref.refs_4_
  5.5 5.7 %own_projections.1 = (bf16[6,128,1024]{2,1,0:T(8,128)(2,1)}, bf16[6,64,1024]{2,1,0:T(8,128)(2,1)}) custom-call(bf16[8,64,768]{2,1,0:T(8,128)(2,1)} %x_ref.3, bf16[8,64,768]{2,1,0:T(8,128)(2,1)} %collective-permute-done.mate_ref.refs_4_, bf16[768,2304]{1,0:T(8,128)(2,1)} %refs_8_.3, bf16[768,2304]{1,0:T(8,128)(2,1)} %refs_8_.3), custom_call_target="tpu_custom_call" | custom-call | flops 2400000000 | bytes 9000000 | tf_op jit(solution)/shard_map/own_projections/pallas_call | solution.py:122
  11.2 3.5 %collective-permute-done.2.a_ref.refs_1_ = bf16[8,64,768]{2,1,0:T(8,128)(2,1)} collective-permute-done((bf16[8,64,768]{2,1,0:T(8,128)(2,1)}, bf16[8,64,768]{2,1,0:T(8,128)(2,1)}, u32[]{:S(2)}, u32[]{:S(2)}) %collective-permute-start.2) | collective-permute-done | bytes 786464 | tf_op jit(solution)/shard_map/ppermute | solution.py:432
  14.7 1.9 %collective-permute-start.3 = (bf16[8,64,768]{2,1,0:T(8,128)(2,1)}, bf16[8,64,768]{2,1,0:T(8,128)(2,1)}, u32[]{:S(2)}, u32[]{:S(2)}) collective-permute-start(bf16[8,64,768]{2,1,0:T(8,128)(2,1)} %collective-permute-done.2.a_ref.refs_1_), channel_id=1, source_target_pairs={{0,2},{1,7},{2,4},{3,1},{4,6},{5,3},{6,0},{7,5},{8,10},{9,15},{10,... | collective-permute-start | bytes 2359304 | tf_op jit(solution)/shard_map/ppermute | solution.py:435
  16.6 5.0 %near_logits.1 = bf16[32,48,128]{2,1,0:T(8,128)(2,1)} custom-call(bf16[6,64,1024]{2,1,0:T(8,128)(2,1)} %get-tuple-element.26.key_ref, bf16[8,64,768]{2,1,0:T(8,128)(2,1)} %collective-permute-done.2.a_ref.refs_1_, bf16[768,2304]{1,0:T(8,128)(2,1)} %refs_8_.3, bf16[6,128,1024]{2,1,0:T(8,128)(2,1)} %get-tuple-element.27.q_ref), custom_call_target="tpu_custom_call" | custom-call | flops 3000000000 | bytes 8000000 | tf_op jit(solution)/shard_map/near_logits/pallas_call | solution.py:136
  21.7 11.2 %all-to-all-start = ((bf16[32,48,128]{2,1,0:T(8,128)(2,1)}), bf16[32,48,128]{2,1,0:T(8,128)(2,1)}, u32[]{:S(2)}, u32[]{:S(2)}) async-start(bf16[32,48,128]{2,1,0:T(8,128)(2,1)} %near_logits.1), calls=%async_computation | async-start | bytes 786432 | tf_op jit(solution)/shard_map/all_to_all | solution.py:438
  32.8 2.0 %collective-permute-start.4 = (bf16[8,64,768]{2,1,0:T(8,128)(2,1)}, bf16[8,64,768]{2,1,0:T(8,128)(2,1)}, u32[]{:S(2)}, u32[]{:S(2)}) collective-permute-start(bf16[8,64,768]{2,1,0:T(8,128)(2,1)} %collective-permute-done.2.a_ref.refs_1_), channel_id=1, source_target_pairs={{0,1},{1,0},{2,3},{3,2},{4,5},{5,4},{6,7},{7,6},{8,9},{9,8},{10,11... | collective-permute-start | bytes 2359304 | tf_op jit(solution)/shard_map/ppermute | solution.py:442
  34.8 2.3 %collective-permute-done.1.b_ref.refs_2_ = bf16[8,64,768]{2,1,0:T(8,128)(2,1)} collective-permute-done((bf16[8,64,768]{2,1,0:T(8,128)(2,1)}, bf16[8,64,768]{2,1,0:T(8,128)(2,1)}, u32[]{:S(2)}, u32[]{:S(2)}) %collective-permute-start.1) | collective-permute-done | bytes 786464 | tf_op jit(solution)/shard_map/ppermute | solution.py:435
  37.1 5.4 %far_logits.1 = bf16[32,48,128]{2,1,0:T(8,128)(2,1)} custom-call(bf16[8,64,768]{2,1,0:T(8,128)(2,1)} %collective-permute-done.1.b_ref.refs_2_, bf16[8,64,768]{2,1,0:T(8,128)(2,1)} %collective-permute-done.3.far_ref.refs_3_, bf16[768,2304]{1,0:T(8,128)(2,1)} %refs_8_.3, bf16[6,128,1024]{2,1,0:T(8,128)(2,1)} %get-tuple-element.27.q_ref), custom_call_target="tpu_custom_call" | custom-call | flops 3000000000 | bytes 7000000 | tf_op jit(solution)/shard_map/far_logits/pallas_call | solution.py:151
  42.5 1.0 collective-permute-start.5
  43.7 10.1 %all-to-all-start.1 = ((bf16[32,48,128]{2,1,0:T(8,128)(2,1)}), bf16[32,48,128]{2,1,0:T(8,128)(2,1)}, u32[]{:S(2)}, u32[]{:S(2)}) async-start(bf16[32,48,128]{2,1,0:T(8,128)(2,1)} %far_logits.1), calls=%async_computation.1 | async-start | bytes 786432 | tf_op jit(solution)/shard_map/all_to_all | solution.py:443
  54.0 12.0 %all-to-all-done.1.far_ref = bf16[32,48,128]{2,1,0:T(8,128)(2,1)} async-done(((bf16[32,48,128]{2,1,0:T(8,128)(2,1)}), bf16[32,48,128]{2,1,0:T(8,128)(2,1)}, u32[]{:S(2)}, u32[]{:S(2)}) %all-to-all-start.1) | async-done | bytes 393248 | tf_op jit(solution)/shard_map/all_to_all | solution.py:443
  66.0 1.2 sum_logits.1
  67.3 2.8 %collective-permute-start.7 = (f32[24,256]{1,0:T(8,128)S(1)}, f32[24,256]{1,0:T(8,128)S(1)}, u32[]{:S(2)}, u32[]{:S(2)}) collective-permute-start(f32[24,256]{1,0:T(8,128)S(1)} %get-tuple-element.37), channel_id=1, source_target_pairs={{0,1},{1,0},{2,3},{3,2},{4,5},{5,4},{6,7},{7,6},{8,9},{9,8},{10,11... | collective-permute-start | bytes 73736 | tf_op jit(solution)/shard_map/ppermute | solution.py:447
  70.1 0.8 collective-permute-done.7.far_ref
  71.1 11.3 %values_1.1.value_ref = bf16[6,512,1024]{2,1,0:T(8,128)(2,1)} custom-call(bf16[8,64,768]{2,1,0:T(8,128)(2,1)} %x_ref.3, bf16[8,64,768]{2,1,0:T(8,128)(2,1)} %collective-permute-done.2.a_ref.refs_1_, bf16[8,64,768]{2,1,0:T(8,128)(2,1)} %collective-permute-done.1.b_ref.refs_2_, ...), custom_call_target="tpu_custom_call", output_to_operand_aliasing={{}: (9, {})} | custom-call | flops 5000000000 | bytes 15000000 | tf_op jit(solution)/shard_map/values_1/pallas_call | solution.py:199
  82.5 12.5 %all_to_all.25 = bf16[8,24,512]{2,1,0:T(8,128)(2,1)S(1)} all-to-all(bf16[8,24,512]{2,1,0:T(8,128)(2,1)S(1)} %row_weights.1), channel_id=1, replica_groups=mesh['x'=4,'z'=8,'y'=4,'core'=2] {'z'}, dimensions={0} | all-to-all | bytes 393216 | tf_op jit(solution)/shard_map/all_to_all | solution.py:451
  95.0 0.4 collective-permute-start.10
  95.4 2.5 %collective-permute-start.9 = (bf16[192,512]{1,0:T(8,128)(2,1)S(1)}, bf16[192,512]{1,0:T(8,128)(2,1)S(1)}, u32[]{:S(2)}, u32[]{:S(2)}) collective-permute-start(bf16[192,512]{1,0:T(8,128)(2,1)S(1)} %bitcast.6), channel_id=1, source_target_pairs={{0,128},{64,192},{128,0},{192,64},{1,129},{65,193},{129,1},{193,65... | collective-permute-start | bytes 589832 | tf_op jit(solution)/shard_map/ppermute | solution.py:452
  97.9 1.1 collective-permute-start.8
  99.0 1.8 %collective-permute-done.10.w3 = bf16[192,512]{1,0:T(8,128)(2,1)S(1)} collective-permute-done((bf16[192,512]{1,0:T(8,128)(2,1)S(1)}, bf16[192,512]{1,0:T(8,128)(2,1)S(1)}, u32[]{:S(2)}, u32[]{:S(2)}) %collective-permute-start.10) | collective-permute-done | bytes 196640 | tf_op jit(solution)/shard_map/ppermute | solution.py:452
  100.8 2.3 %collective-permute-done.9.w2 = bf16[192,512]{1,0:T(8,128)(2,1)S(1)} collective-permute-done((bf16[192,512]{1,0:T(8,128)(2,1)S(1)}, bf16[192,512]{1,0:T(8,128)(2,1)S(1)}, u32[]{:S(2)}, u32[]{:S(2)}) %collective-permute-start.9) | collective-permute-done | bytes 196640 | tf_op jit(solution)/shard_map/ppermute | solution.py:452
  103.0 0.4 collective-permute-done.8.w1
  103.4 0.2 copy-done.2
  103.7 0.7 copy-done.3
  104.4 5.9 %row_context.1 = bf16[512,768]{1,0:T(8,128)(2,1)} custom-call(bf16[192,512]{1,0:T(8,128)(2,1)} %bitcast.8, bf16[192,512]{1,0:T(8,128)(2,1)} %copy-done.3, bf16[192,512]{1,0:T(8,128)(2,1)} %copy-done.2, bf16[192,512]{1,0:T(8,128)(2,1)} %copy-done.1, bf16[6,512,1024]{2,1,0:T(8,128)(2,1)} %values_1.1.value_ref, bf16[8,64,768]{2,1,0:T(8,128)(2,1)} %x_ref.3, ...), custom_call_target="tpu_custom_call" | custom-call | flops 2000000000 | bytes 10000000 | tf_op jit(solution)/shard_map/row_context/pallas_call | solution.py:313
  110.3 20.4 %all_to_all.26.x_ref = bf16[32,16,768]{2,1,0:T(8,128)(2,1)} all-to-all(bf16[32,16,768]{2,1,0:T(8,128)(2,1)} %bitcast.4), channel_id=1, replica_groups=mesh['x'=4,'z'=8,'y'=4,'core'=2] {'x','z'}, dimensions={0} | all-to-all | bytes 1572864 | tf_op jit(solution)/shard_map/all_to_all | solution.py:454
  130.6 8.2 %columns.1 = bf16[32,16,768]{2,1,0:T(8,128)(2,1)} custom-call(bf16[32,16,768]{2,1,0:T(8,128)(2,1)} %all_to_all.26.x_ref, bf16[768,2304]{1,0:T(8,128)(2,1)} %wv_ref.1, bf16[768,2304]{1,0:T(8,128)(2,1)} %wv_ref.1, bf16[768,2304]{1,0:T(8,128)(2,1)} %wv_ref.1, bf16[768,768]{1,0:T(8,128)(2,1)} %wo_ref.3), custom_call_target="tpu_custom_call" | custom-call | flops 5000000000 | bytes 7000000 | tf_op jit(solution)/shard_map/columns/pallas_call | solution.py:376
  138.9 23.1 %all_to_all.27 = bf16[32,16,768]{2,1,0:T(8,128)(2,1)S(1)} all-to-all(bf16[32,16,768]{2,1,0:T(8,128)(2,1)} %columns.1), channel_id=1, replica_groups=mesh['x'=4,'z'=8,'y'=4,'core'=2] {'x','z'}, dimensions={0} | all-to-all | bytes 1572864 | tf_op jit(solution)/shard_map/all_to_all | solution.py:456
  162.0 1.5 finish.1
  (15 shorter events, 0.6 us)
Async XLA Ops:
  0.0 5.5 %collective-permute-start = (bf16[8,64,768]{2,1,0:T(8,128)(2,1)}, bf16[8,64,768]{2,1,0:T(8,128)(2,1)}, u32[]{:S(2)}, u32[]{:S(2)}) collective-permute-start(bf16[8,64,768]{2,1,0:T(8,128)(2,1)} %x_ref.3), channel_id=1, source_target_pairs={{0,1},{1,0},{2,3},{3,2},{4,5},{5,4},{6,7},{7,6},{8,9},{9,8},{10,11... | collective-permute-start | bytes 2359304 | tf_op jit(solution)/shard_map/ppermute | solution.py:432
  3.2 11.5 %collective-permute-start.2 = (bf16[8,64,768]{2,1,0:T(8,128)(2,1)}, bf16[8,64,768]{2,1,0:T(8,128)(2,1)}, u32[]{:S(2)}, u32[]{:S(2)}) collective-permute-start(bf16[8,64,768]{2,1,0:T(8,128)(2,1)} %x_ref.3), channel_id=1, source_target_pairs={{0,2},{1,7},{2,4},{3,1},{4,6},{5,3},{6,0},{7,5},{8,10},{9,15},{10,... | collective-permute-start | bytes 2359304 | tf_op jit(solution)/shard_map/ppermute | solution.py:432
  14.7 20.1 %collective-permute-start.3 = (bf16[8,64,768]{2,1,0:T(8,128)(2,1)}, bf16[8,64,768]{2,1,0:T(8,128)(2,1)}, u32[]{:S(2)}, u32[]{:S(2)}) collective-permute-start(bf16[8,64,768]{2,1,0:T(8,128)(2,1)} %collective-permute-done.2.a_ref.refs_1_), channel_id=1, source_target_pairs={{0,2},{1,7},{2,4},{3,1},{4,6},{5,3},{6,0},{7,5},{8,10},{9,15},{10,... | collective-permute-start | bytes 2359304 | tf_op jit(solution)/shard_map/ppermute | solution.py:435
  16.6 20.5 %collective-permute-start.1 = (bf16[8,64,768]{2,1,0:T(8,128)(2,1)}, bf16[8,64,768]{2,1,0:T(8,128)(2,1)}, u32[]{:S(2)}, u32[]{:S(2)}) collective-permute-start(bf16[8,64,768]{2,1,0:T(8,128)(2,1)} %x_ref.3), channel_id=1, source_target_pairs={{2,0},{7,1},{4,2},{1,3},{6,4},{3,5},{0,6},{5,7},{10,8},{15,9},{12,... | collective-permute-start | bytes 2359304 | tf_op jit(solution)/shard_map/ppermute | solution.py:435
  21.7 22.0 %all-to-all-start = ((bf16[32,48,128]{2,1,0:T(8,128)(2,1)}), bf16[32,48,128]{2,1,0:T(8,128)(2,1)}, u32[]{:S(2)}, u32[]{:S(2)}) async-start(bf16[32,48,128]{2,1,0:T(8,128)(2,1)} %near_logits.1), calls=%async_computation | async-start | bytes 786432 | tf_op jit(solution)/shard_map/all_to_all | solution.py:438
  32.8 21.0 %collective-permute-start.4 = (bf16[8,64,768]{2,1,0:T(8,128)(2,1)}, bf16[8,64,768]{2,1,0:T(8,128)(2,1)}, u32[]{:S(2)}, u32[]{:S(2)}) collective-permute-start(bf16[8,64,768]{2,1,0:T(8,128)(2,1)} %collective-permute-done.2.a_ref.refs_1_), channel_id=1, source_target_pairs={{0,1},{1,0},{2,3},{3,2},{4,5},{5,4},{6,7},{7,6},{8,9},{9,8},{10,11... | collective-permute-start | bytes 2359304 | tf_op jit(solution)/shard_map/ppermute | solution.py:442
  42.5 11.2 %collective-permute-start.5 = (bf16[8,64,768]{2,1,0:T(8,128)(2,1)}, bf16[8,64,768]{2,1,0:T(8,128)(2,1)}, u32[]{:S(2)}, u32[]{:S(2)}) collective-permute-start(bf16[8,64,768]{2,1,0:T(8,128)(2,1)} %collective-permute-done.1.b_ref.refs_2_), channel_id=1, source_target_pairs={{0,1},{1,0},{2,3},{3,2},{4,5},{5,4},{6,7},{7,6},{8,9},{9,8},{10,11... | collective-permute-start | bytes 2359304 | tf_op jit(solution)/shard_map/ppermute | solution.py:442
  43.6 10.2 %collective-permute-start.6 = (bf16[8,64,768]{2,1,0:T(8,128)(2,1)}, bf16[8,64,768]{2,1,0:T(8,128)(2,1)}, u32[]{:S(2)}, u32[]{:S(2)}) collective-permute-start(bf16[8,64,768]{2,1,0:T(8,128)(2,1)} %collective-permute-done.3.far_ref.refs_3_), channel_id=1, source_target_pairs={{0,1},{1,0},{2,3},{3,2},{4,5},{5,4},{6,7},{7,6},{8,9},{9,8},{10,11... | collective-permute-start | bytes 2359304 | tf_op jit(solution)/shard_map/ppermute | solution.py:442
  43.7 22.3 %all-to-all-start.1 = ((bf16[32,48,128]{2,1,0:T(8,128)(2,1)}), bf16[32,48,128]{2,1,0:T(8,128)(2,1)}, u32[]{:S(2)}, u32[]{:S(2)}) async-start(bf16[32,48,128]{2,1,0:T(8,128)(2,1)} %far_logits.1), calls=%async_computation.1 | async-start | bytes 786432 | tf_op jit(solution)/shard_map/all_to_all | solution.py:443
  67.3 3.7 %collective-permute-start.7 = (f32[24,256]{1,0:T(8,128)S(1)}, f32[24,256]{1,0:T(8,128)S(1)}, u32[]{:S(2)}, u32[]{:S(2)}) collective-permute-start(f32[24,256]{1,0:T(8,128)S(1)} %get-tuple-element.37), channel_id=1, source_target_pairs={{0,1},{1,0},{2,3},{3,2},{4,5},{5,4},{6,7},{7,6},{8,9},{9,8},{10,11... | collective-permute-start | bytes 73736 | tf_op jit(solution)/shard_map/ppermute | solution.py:447
  95.0 8.4 %copy-start = (bf16[8,24,512]{2,1,0:T(8,128)(2,1)}, bf16[8,24,512]{2,1,0:T(8,128)(2,1)S(1)}, u32[]{:S(2)}) copy-start(bf16[8,24,512]{2,1,0:T(8,128)(2,1)S(1)} %all_to_all.25) | copy-start | bytes 589828
  95.0 5.7 %collective-permute-start.10 = (bf16[192,512]{1,0:T(8,128)(2,1)S(1)}, bf16[192,512]{1,0:T(8,128)(2,1)S(1)}, u32[]{:S(2)}, u32[]{:S(2)}) collective-permute-start(bf16[192,512]{1,0:T(8,128)(2,1)S(1)} %bitcast.5), channel_id=1, source_target_pairs={{0,64},{64,128},{128,192},{192,0},{1,65},{65,129},{129,193},{193,1... | collective-permute-start | bytes 589832 | tf_op jit(solution)/shard_map/ppermute | solution.py:452
  95.4 7.6 %collective-permute-start.9 = (bf16[192,512]{1,0:T(8,128)(2,1)S(1)}, bf16[192,512]{1,0:T(8,128)(2,1)S(1)}, u32[]{:S(2)}, u32[]{:S(2)}) collective-permute-start(bf16[192,512]{1,0:T(8,128)(2,1)S(1)} %bitcast.6), channel_id=1, source_target_pairs={{0,128},{64,192},{128,0},{192,64},{1,129},{65,193},{129,1},{193,65... | collective-permute-start | bytes 589832 | tf_op jit(solution)/shard_map/ppermute | solution.py:452
  97.9 5.6 %collective-permute-start.8 = (bf16[192,512]{1,0:T(8,128)(2,1)S(1)}, bf16[192,512]{1,0:T(8,128)(2,1)S(1)}, u32[]{:S(2)}, u32[]{:S(2)}) collective-permute-start(bf16[192,512]{1,0:T(8,128)(2,1)S(1)} %bitcast.7), channel_id=1, source_target_pairs={{0,192},{64,0},{128,64},{192,128},{1,193},{65,1},{129,65},{193,129... | collective-permute-start | bytes 589832 | tf_op jit(solution)/shard_map/ppermute | solution.py:452
  100.8 2.7 %copy-start.1 = (bf16[192,512]{1,0:T(8,128)(2,1)}, bf16[192,512]{1,0:T(8,128)(2,1)S(1)}, u32[]{:S(2)}) copy-start(bf16[192,512]{1,0:T(8,128)(2,1)S(1)} %collective-permute-done.10.w3) | copy-start | bytes 589828
  103.0 0.7 copy-start.2
  103.7 0.7 copy-start.3

commit v6 on v5

--- a/solution.py
+++ b/solution.py
@@ -164,8 +164,9 @@
 BLOCKS = 8
 
 
-def value_kernel(core, *refs):
-    block_refs, w_ref = refs[:BLOCKS], refs[BLOCKS]
+def value_kernel(core, places, *refs):
+    count = len(places)
+    block_refs, w_ref = refs[:count], refs[count]
     out_ref, rows, wv, done, loaded, stored, weighed = refs[-7:]
 
     @pl.when(lax.axis_index("core") == core)
@@ -175,14 +176,14 @@
         for n, ref in enumerate(block_refs):
             slot = n % 2
             loads.append(pltpu.make_async_copy(ref, rows.at[slot], loaded.at[slot]))
-            target = out_ref.at[:, pl.ds(n * I, I)]
+            target = out_ref.at[:, pl.ds(places[n] * I, I)]
             stores.append(pltpu.make_async_copy(done.at[slot], target, stored.at[slot]))
         weights.start()
         loads[0].start()
         weights.wait()
-        for n in range(BLOCKS):
+        for n in range(count):
             slot = n % 2
-            if n + 1 < BLOCKS:
+            if n + 1 < count:
                 loads[n + 1].start()
             loads[n].wait()
             if n >= 2:
@@ -190,18 +191,18 @@
             for s in range(2):
                 store_block(done.at[slot], 0, 4 * s, project(normed_rows(rows.at[slot], s), wv))
             stores[n].start()
-        stores[BLOCKS - 2].wait()
-        stores[BLOCKS - 1].wait()
-
-
-def all_values(core, blocks, w, before=None):
+        stores[count - 2].wait()
+        stores[count - 1].wait()
+
+
+def all_values(core, places, blocks, w, before=None):
     operands = [*blocks, w] + ([] if before is None else [before])
     return pl.pallas_call(
-        functools.partial(value_kernel, core),
+        functools.partial(value_kernel, core, places),
         out_shape=jax.ShapeDtypeStruct((PAIRS, BLOCKS * I, R * 128), BF),
         in_specs=[HBM] * len(operands),
         out_specs=HBM,
-        input_output_aliases={} if before is None else {BLOCKS + 1: 0},
+        input_output_aliases={} if before is None else {len(places) + 1: 0},
         scratch_shapes=[
             pltpu.VMEM((2, R, I, D), BF),
             pltpu.VMEM((D, D), BF),
@@ -212,7 +213,7 @@
         ],
         compiler_params=params(62 * MB if core else 64 * MB),
         cost_estimate=cost(5e9, 1.5e7),
-        name="values_%d" % core,
+        name="values_%d_%d" % (core, len(places)),
     )(*operands)
 
 
@@ -432,6 +433,8 @@
     a, own = on(x), mate(x)
     q, keys = own_projections(x, own, w_row)
     later, q = lax.optimization_barrier((x, q))
+    values = all_values(0, (0, 4), (x, own), w_row)
+    a, values = lax.optimization_barrier((a, values))
     b, far = back(later), on(a)
     near = near_logits(keys, a, w_row, q)
     b, far, _ = lax.optimization_barrier((b, far, near))
@@ -441,12 +444,13 @@
     logits, near = lax.optimization_barrier((logits, near))
     blocks = (x, a, b, far, own, mate(a), mate(b), mate(far))
     logits = exchange(logits)
-    values = all_values(0, blocks, w_row)
+    others = [blocks[n] for n in (1, 2, 3, 5, 6, 7)]
+    values = all_values(0, (1, 2, 3, 5, 6, 7), others, w_row, values)
     logits, values = lax.optimization_barrier((logits, values))
     mine, other = sum_logits(near, logits)
     copies = row_weights(mine, mate(other), float((64 * 256) ** -0.5), 8)
     copies, values = lax.optimization_barrier((copies, values))
-    values = all_values(1, blocks, w_row, values)
+    values = all_values(1, tuple(range(BLOCKS)), blocks, w_row, values)
     copies, values = lax.optimization_barrier((copies, values))
     mine = lax.all_to_all(copies, "z", 0, 0, tiled=True).reshape(192, 512)
     weights = [mine] + [along[4 - k](mine) for k in (1, 2, 3)]

time: 164 us -> 164 us (level)
  waiting for transfers between devices: 24.3 us -> 28 us
  starting transfers between devices: 37.3 us -> 34.1 us
    all_to_all x1, waiting for transfers between devices: 0.01 us -> 5.98 us  [per_device(): near = exchange(near)]
    all_to_all x1, starting transfers between devices: 10.1 us -> 7.49 us  [per_device(): logits = exchange(logits)]
    ppermute x2, waiting for transfers between devices: 2.3 us -> 0.01 us  [per_device(): b, far = (back(later), on(a))]
    pallas_call x2 -> x3, Pallas kernels: 11.6 us -> 11.4 us  [all_values(): pl.pallas_call(functools.partial(value_kernel, core, places), out_shape=j...]
  transfers between devices with their start and end apart: 13 -> 13, of which waited for: 8 -> 7; matrix products, arithmetic and copies ran while one was open for 0% -> 0% of each run, Pallas kernels for 10% -> 10%
where the time goes in v6:
time: 164 us; the launch traced here: 163 us
  blocking collectives  55.6 us (34%)
  Pallas kernels  44.6 us (27%)
  starting transfers between devices  34.1 us (21%)
  waiting for transfers between devices  28 us (17%)
    all_to_all x1, blocking collectives, per_device(): rows = exchange(columns)  23.1 us
    all_to_all x1, blocking collectives, per_device(): columns = exchange(rows.reshape(32, 2 * R, D))  20.4 us
    all_to_all x1, blocking collectives, per_device(): mine = lax.all_to_all(copies, 'z', 0, 0, tiled=True).reshape(192, 512)  12 us
    pallas_call x3, Pallas kernels, all_values(): pl.pallas_call(functools.partial(value_kernel, core, places), out_shape=j...  11.4 us
    all_to_all x1, waiting for transfers between devices, per_device(): logits = exchange(logits)  11.2 us
    all_to_all x1, starting transfers between devices, per_device(): near = exchange(near)  10.5 us
    pallas_call x1, Pallas kernels, attend_columns(): pl.pallas_call(column_kernel, grid=(3,), out_shape=jax.ShapeDtypeStruct((...  8.22 us
    all_to_all x1, starting transfers between devices, per_device(): logits = exchange(logits)  7.49 us
  transfers between devices with their start and end apart: 13, of which 7 were waited for; matrix products, arithmetic and copies ran while one was open for 0% of the time, Pallas kernels for 10%

profile of v6, /device:TPU:1, one launch (start us, length us, event | category | flops | bytes accessed | tf_op | source)
XLA Modules:
  0.0 163.3 jit_solution(8557043982526463344)
XLA Ops:
  0.0 3.2 %collective-permute-start = (bf16[8,64,768]{2,1,0:T(8,128)(2,1)}, bf16[8,64,768]{2,1,0:T(8,128)(2,1)}, u32[]{:S(2)}, u32[]{:S(2)}) collective-permute-start(bf16[8,64,768]{2,1,0:T(8,128)(2,1)} %x_ref.3), channel_id=1, source_target_pairs={{0,1},{1,0},{2,3},{3,2},{4,5},{5,4},{6,7},{7,6},{8,9},{9,8},{10,11... | collective-permute-start | bytes 2359304 | tf_op jit(solution)/shard_map/ppermute | solution.py:433
  3.2 1.0 collective-permute-start.2
  4.2 1.3 collective-permute-done.mate_ref.refs_1_.refs_4_
  5.5 5.7 %own_projections.1 = (bf16[6,128,1024]{2,1,0:T(8,128)(2,1)}, bf16[6,64,1024]{2,1,0:T(8,128)(2,1)}) custom-call(bf16[8,64,768]{2,1,0:T(8,128)(2,1)} %x_ref.3, bf16[8,64,768]{2,1,0:T(8,128)(2,1)} %collective-permute-done.mate_ref.refs_1_.refs_4_, bf16[768,2304]{1,0:T(8,128)(2,1)} %refs_8_.1, bf16[768,2304]{1,0:T(8,128)(2,1)} %refs_8_.1), custom_call_target="tpu_custom_call" | custom-call | flops 2400000000 | bytes 9000000 | tf_op jit(solution)/shard_map/own_projections/pallas_call | solution.py:122
  11.3 3.4 %collective-permute-done.2.a_ref.refs_0_.refs_1_ = bf16[8,64,768]{2,1,0:T(8,128)(2,1)} collective-permute-done((bf16[8,64,768]{2,1,0:T(8,128)(2,1)}, bf16[8,64,768]{2,1,0:T(8,128)(2,1)}, u32[]{:S(2)}, u32[]{:S(2)}) %collective-permute-start.2) | collective-permute-done | bytes 786464 | tf_op jit(solution)/shard_map/ppermute | solution.py:433
  14.7 1.9 %collective-permute-start.3 = (bf16[8,64,768]{2,1,0:T(8,128)(2,1)}, bf16[8,64,768]{2,1,0:T(8,128)(2,1)}, u32[]{:S(2)}, u32[]{:S(2)}) collective-permute-start(bf16[8,64,768]{2,1,0:T(8,128)(2,1)} %collective-permute-done.2.a_ref.refs_0_.refs_1_), channel_id=1, source_target_pairs={{0,2},{1,7},{2,4},{3,1},{4,6},{5,3},{6,0},{7,5},{8,10},{9,15},{10,... | collective-permute-start | bytes 2359304 | tf_op jit(solution)/shard_map/ppermute | solution.py:438
  16.6 1.7 %collective-permute-start.4 = (bf16[8,64,768]{2,1,0:T(8,128)(2,1)}, bf16[8,64,768]{2,1,0:T(8,128)(2,1)}, u32[]{:S(2)}, u32[]{:S(2)}) collective-permute-start(bf16[8,64,768]{2,1,0:T(8,128)(2,1)} %collective-permute-done.2.a_ref.refs_0_.refs_1_), channel_id=1, source_target_pairs={{0,1},{1,0},{2,3},{3,2},{4,5},{5,4},{6,7},{7,6},{8,9},{9,8},{10,11... | collective-permute-start | bytes 2359304 | tf_op jit(solution)/shard_map/ppermute | solution.py:445
  18.3 5.1 %near_logits.1 = bf16[32,48,128]{2,1,0:T(8,128)(2,1)} custom-call(bf16[6,64,1024]{2,1,0:T(8,128)(2,1)} %get-tuple-element.29.key_ref, bf16[8,64,768]{2,1,0:T(8,128)(2,1)} %collective-permute-done.2.a_ref.refs_0_.refs_1_, bf16[768,2304]{1,0:T(8,128)(2,1)} %refs_8_.1, bf16[6,128,1024]{2,1,0:T(8,128)(2,1)} %get-tuple-element.30.q_ref), custom_call_target="tpu_custom_call" | custom-call | flops 3000000000 | bytes 8000000 | tf_op jit(solution)/shard_map/near_logits/pallas_call | solution.py:136
  23.3 10.5 %all-to-all-start = ((bf16[32,48,128]{2,1,0:T(8,128)(2,1)}), bf16[32,48,128]{2,1,0:T(8,128)(2,1)}, u32[]{:S(2)}, u32[]{:S(2)}) async-start(bf16[32,48,128]{2,1,0:T(8,128)(2,1)} %near_logits.1), calls=%async_computation | async-start | bytes 786432 | tf_op jit(solution)/shard_map/all_to_all | solution.py:441
  33.9 5.4 %far_logits.1 = bf16[32,48,128]{2,1,0:T(8,128)(2,1)} custom-call(bf16[8,64,768]{2,1,0:T(8,128)(2,1)} %collective-permute-done.1.b_ref.refs_1_.refs_2_, bf16[8,64,768]{2,1,0:T(8,128)(2,1)} %collective-permute-done.3.far_ref.refs_2_.refs_3_, bf16[768,2304]{1,0:T(8,128)(2,1)} %refs_8_.1, bf16[6,128,1024]{2,1,0:T(8,128)(2,1)} %get-tuple-element.30.q_ref), custom_call_target="tpu_custom_call" | custom-call | flops 3000000000 | bytes 7000000 | tf_op jit(solution)/shard_map/far_logits/pallas_call | solution.py:151
  39.3 0.5 collective-permute-start.5
  39.8 0.2 collective-permute-start.6
  40.1 6.0 %all-to-all-done.near_ref = bf16[32,48,128]{2,1,0:T(8,128)(2,1)} async-done(((bf16[32,48,128]{2,1,0:T(8,128)(2,1)}), bf16[32,48,128]{2,1,0:T(8,128)(2,1)}, u32[]{:S(2)}, u32[]{:S(2)}) %all-to-all-start) | async-done | bytes 393248 | tf_op jit(solution)/shard_map/all_to_all | solution.py:441
  46.0 7.5 %all-to-all-start.1 = ((bf16[32,48,128]{2,1,0:T(8,128)(2,1)}), bf16[32,48,128]{2,1,0:T(8,128)(2,1)}, u32[]{:S(2)}, u32[]{:S(2)}) async-start(bf16[32,48,128]{2,1,0:T(8,128)(2,1)} %far_logits.1), calls=%async_computation.1 | async-start | bytes 786432 | tf_op jit(solution)/shard_map/all_to_all | solution.py:446
  53.6 11.2 %all-to-all-done.1.far_ref = bf16[32,48,128]{2,1,0:T(8,128)(2,1)} async-done(((bf16[32,48,128]{2,1,0:T(8,128)(2,1)}), bf16[32,48,128]{2,1,0:T(8,128)(2,1)}, u32[]{:S(2)}, u32[]{:S(2)}) %all-to-all-start.1) | async-done | bytes 393248 | tf_op jit(solution)/shard_map/all_to_all | solution.py:446
  64.8 1.2 sum_logits.1
  66.1 4.3 %collective-permute-start.7 = (f32[24,256]{1,0:T(8,128)S(1)}, f32[24,256]{1,0:T(8,128)S(1)}, u32[]{:S(2)}, u32[]{:S(2)}) collective-permute-start(f32[24,256]{1,0:T(8,128)S(1)} %get-tuple-element.41), channel_id=1, source_target_pairs={{0,1},{1,0},{2,3},{3,2},{4,5},{5,4},{6,7},{7,6},{8,9},{9,8},{10,11... | collective-permute-start | bytes 73736 | tf_op jit(solution)/shard_map/ppermute | solution.py:451
  70.4 0.8 collective-permute-done.7.far_ref
  71.3 0.2 row_weights.1
  71.5 11.3 %values_1_8.1.value_ref = bf16[6,512,1024]{2,1,0:T(8,128)(2,1)} custom-call(bf16[8,64,768]{2,1,0:T(8,128)(2,1)} %x_ref.3, bf16[8,64,768]{2,1,0:T(8,128)(2,1)} %collective-permute-done.2.a_ref.refs_0_.refs_1_, bf16[8,64,768]{2,1,0:T(8,128)(2,1)} %collective-permute-done.1.b_ref.refs_1_.refs_2_, ...), custom_call_target="tpu_custom_call", output_to_operand_aliasing={{}: (9, {})} | custom-call | flops 5000000000 | bytes 15000000 | tf_op jit(solution)/shard_map/values_1_8/pallas_call | solution.py:200
  82.8 12.0 %all_to_all.25 = bf16[8,24,512]{2,1,0:T(8,128)(2,1)S(1)} all-to-all(bf16[8,24,512]{2,1,0:T(8,128)(2,1)S(1)} %row_weights.1), channel_id=1, replica_groups=mesh['x'=4,'z'=8,'y'=4,'core'=2] {'z'}, dimensions={0} | all-to-all | bytes 393216 | tf_op jit(solution)/shard_map/all_to_all | solution.py:455
  94.8 0.3 collective-permute-start.10
  95.1 1.8 %collective-permute-start.9 = (bf16[192,512]{1,0:T(8,128)(2,1)S(1)}, bf16[192,512]{1,0:T(8,128)(2,1)S(1)}, u32[]{:S(2)}, u32[]{:S(2)}) collective-permute-start(bf16[192,512]{1,0:T(8,128)(2,1)S(1)} %bitcast.6), channel_id=1, source_target_pairs={{0,128},{64,192},{128,0},{192,64},{1,129},{65,193},{129,1},{193,65... | collective-permute-start | bytes 589832 | tf_op jit(solution)/shard_map/ppermute | solution.py:456
  96.9 1.1 collective-permute-start.8
  98.0 4.7 %collective-permute-done.10.w3 = bf16[192,512]{1,0:T(8,128)(2,1)S(1)} collective-permute-done((bf16[192,512]{1,0:T(8,128)(2,1)S(1)}, bf16[192,512]{1,0:T(8,128)(2,1)S(1)}, u32[]{:S(2)}, u32[]{:S(2)}) %collective-permute-start.10) | collective-permute-done | bytes 196640 | tf_op jit(solution)/shard_map/ppermute | solution.py:456
  102.6 0.6 collective-permute-done.8.w1
  103.4 0.7 copy-done.3
  104.1 5.9 %row_context.1 = bf16[512,768]{1,0:T(8,128)(2,1)} custom-call(bf16[192,512]{1,0:T(8,128)(2,1)} %bitcast.8, bf16[192,512]{1,0:T(8,128)(2,1)} %copy-done.3, bf16[192,512]{1,0:T(8,128)(2,1)} %copy-done.2, bf16[192,512]{1,0:T(8,128)(2,1)} %copy-done.1, bf16[6,512,1024]{2,1,0:T(8,128)(2,1)} %values_1_8.1.value_ref, bf16[8,64,768]{2,1,0:T(8,128)(2,1)} %x_ref.3, ...), custom_call_target="tpu_custom_call" | custom-call | flops 2000000000 | bytes 10000000 | tf_op jit(solution)/shard_map/row_context/pallas_call | solution.py:314
  110.0 20.4 %all_to_all.26.x_ref = bf16[32,16,768]{2,1,0:T(8,128)(2,1)} all-to-all(bf16[32,16,768]{2,1,0:T(8,128)(2,1)} %bitcast.4), channel_id=1, replica_groups=mesh['x'=4,'z'=8,'y'=4,'core'=2] {'x','z'}, dimensions={0} | all-to-all | bytes 1572864 | tf_op jit(solution)/shard_map/all_to_all | solution.py:458
  130.4 8.2 %columns.1 = bf16[32,16,768]{2,1,0:T(8,128)(2,1)} custom-call(bf16[32,16,768]{2,1,0:T(8,128)(2,1)} %all_to_all.26.x_ref, bf16[768,2304]{1,0:T(8,128)(2,1)} %wv_ref.1, bf16[768,2304]{1,0:T(8,128)(2,1)} %wv_ref.1, bf16[768,2304]{1,0:T(8,128)(2,1)} %wv_ref.1, bf16[768,768]{1,0:T(8,128)(2,1)} %wo_ref.3), custom_call_target="tpu_custom_call" | custom-call | flops 5000000000 | bytes 7000000 | tf_op jit(solution)/shard_map/columns/pallas_call | solution.py:377
  138.7 23.1 %all_to_all.27 = bf16[32,16,768]{2,1,0:T(8,128)(2,1)S(1)} all-to-all(bf16[32,16,768]{2,1,0:T(8,128)(2,1)} %columns.1), channel_id=1, replica_groups=mesh['x'=4,'z'=8,'y'=4,'core'=2] {'x','z'}, dimensions={0} | all-to-all | bytes 1572864 | tf_op jit(solution)/shard_map/all_to_all | solution.py:460
  161.8 1.5 finish.1
  (16 shorter events, 0.3 us)
Async XLA Ops:
  0.0 5.5 %collective-permute-start = (bf16[8,64,768]{2,1,0:T(8,128)(2,1)}, bf16[8,64,768]{2,1,0:T(8,128)(2,1)}, u32[]{:S(2)}, u32[]{:S(2)}) collective-permute-start(bf16[8,64,768]{2,1,0:T(8,128)(2,1)} %x_ref.3), channel_id=1, source_target_pairs={{0,1},{1,0},{2,3},{3,2},{4,5},{5,4},{6,7},{7,6},{8,9},{9,8},{10,11... | collective-permute-start | bytes 2359304 | tf_op jit(solution)/shard_map/ppermute | solution.py:433
  3.2 11.5 %collective-permute-start.2 = (bf16[8,64,768]{2,1,0:T(8,128)(2,1)}, bf16[8,64,768]{2,1,0:T(8,128)(2,1)}, u32[]{:S(2)}, u32[]{:S(2)}) collective-permute-start(bf16[8,64,768]{2,1,0:T(8,128)(2,1)} %x_ref.3), channel_id=1, source_target_pairs={{0,2},{1,7},{2,4},{3,1},{4,6},{5,3},{6,0},{7,5},{8,10},{9,15},{10,... | collective-permute-start | bytes 2359304 | tf_op jit(solution)/shard_map/ppermute | solution.py:433
  11.2 22.6 %collective-permute-start.1 = (bf16[8,64,768]{2,1,0:T(8,128)(2,1)}, bf16[8,64,768]{2,1,0:T(8,128)(2,1)}, u32[]{:S(2)}, u32[]{:S(2)}) collective-permute-start(bf16[8,64,768]{2,1,0:T(8,128)(2,1)} %x_ref.3), channel_id=1, source_target_pairs={{2,0},{7,1},{4,2},{1,3},{6,4},{3,5},{0,6},{5,7},{10,8},{15,9},{12,... | collective-permute-start | bytes 2359304 | tf_op jit(solution)/shard_map/ppermute | solution.py:438
  14.7 19.2 %collective-permute-start.3 = (bf16[8,64,768]{2,1,0:T(8,128)(2,1)}, bf16[8,64,768]{2,1,0:T(8,128)(2,1)}, u32[]{:S(2)}, u32[]{:S(2)}) collective-permute-start(bf16[8,64,768]{2,1,0:T(8,128)(2,1)} %collective-permute-done.2.a_ref.refs_0_.refs_1_), channel_id=1, source_target_pairs={{0,2},{1,7},{2,4},{3,1},{4,6},{5,3},{6,0},{7,5},{8,10},{9,15},{10,... | collective-permute-start | bytes 2359304 | tf_op jit(solution)/shard_map/ppermute | solution.py:438
  16.6 36.9 %collective-permute-start.4 = (bf16[8,64,768]{2,1,0:T(8,128)(2,1)}, bf16[8,64,768]{2,1,0:T(8,128)(2,1)}, u32[]{:S(2)}, u32[]{:S(2)}) collective-permute-start(bf16[8,64,768]{2,1,0:T(8,128)(2,1)} %collective-permute-done.2.a_ref.refs_0_.refs_1_), channel_id=1, source_target_pairs={{0,1},{1,0},{2,3},{3,2},{4,5},{5,4},{6,7},{7,6},{8,9},{9,8},{10,11... | collective-permute-start | bytes 2359304 | tf_op jit(solution)/shard_map/ppermute | solution.py:445
  23.3 22.7 %all-to-all-start = ((bf16[32,48,128]{2,1,0:T(8,128)(2,1)}), bf16[32,48,128]{2,1,0:T(8,128)(2,1)}, u32[]{:S(2)}, u32[]{:S(2)}) async-start(bf16[32,48,128]{2,1,0:T(8,128)(2,1)} %near_logits.1), calls=%async_computation | async-start | bytes 786432 | tf_op jit(solution)/shard_map/all_to_all | solution.py:441
  39.3 14.3 %collective-permute-start.5 = (bf16[8,64,768]{2,1,0:T(8,128)(2,1)}, bf16[8,64,768]{2,1,0:T(8,128)(2,1)}, u32[]{:S(2)}, u32[]{:S(2)}) collective-permute-start(bf16[8,64,768]{2,1,0:T(8,128)(2,1)} %collective-permute-done.1.b_ref.refs_1_.refs_2_), channel_id=1, source_target_pairs={{0,1},{1,0},{2,3},{3,2},{4,5},{5,4},{6,7},{7,6},{8,9},{9,8},{10,11... | collective-permute-start | bytes 2359304 | tf_op jit(solution)/shard_map/ppermute | solution.py:445
  39.8 13.7 %collective-permute-start.6 = (bf16[8,64,768]{2,1,0:T(8,128)(2,1)}, bf16[8,64,768]{2,1,0:T(8,128)(2,1)}, u32[]{:S(2)}, u32[]{:S(2)}) collective-permute-start(bf16[8,64,768]{2,1,0:T(8,128)(2,1)} %collective-permute-done.3.far_ref.refs_2_.refs_3_), channel_id=1, source_target_pairs={{0,1},{1,0},{2,3},{3,2},{4,5},{5,4},{6,7},{7,6},{8,9},{9,8},{10,11... | collective-permute-start | bytes 2359304 | tf_op jit(solution)/shard_map/ppermute | solution.py:445
  46.0 18.8 %all-to-all-start.1 = ((bf16[32,48,128]{2,1,0:T(8,128)(2,1)}), bf16[32,48,128]{2,1,0:T(8,128)(2,1)}, u32[]{:S(2)}, u32[]{:S(2)}) async-start(bf16[32,48,128]{2,1,0:T(8,128)(2,1)} %far_logits.1), calls=%async_computation.1 | async-start | bytes 786432 | tf_op jit(solution)/shard_map/all_to_all | solution.py:446
  66.1 5.2 %collective-permute-start.7 = (f32[24,256]{1,0:T(8,128)S(1)}, f32[24,256]{1,0:T(8,128)S(1)}, u32[]{:S(2)}, u32[]{:S(2)}) collective-permute-start(f32[24,256]{1,0:T(8,128)S(1)} %get-tuple-element.41), channel_id=1, source_target_pairs={{0,1},{1,0},{2,3},{3,2},{4,5},{5,4},{6,7},{7,6},{8,9},{9,8},{10,11... | collective-permute-start | bytes 73736 | tf_op jit(solution)/shard_map/ppermute | solution.py:451
  94.8 8.5 %copy-start = (bf16[8,24,512]{2,1,0:T(8,128)(2,1)}, bf16[8,24,512]{2,1,0:T(8,128)(2,1)S(1)}, u32[]{:S(2)}) copy-start(bf16[8,24,512]{2,1,0:T(8,128)(2,1)S(1)} %all_to_all.25) | copy-start | bytes 589828
  94.8 7.8 %collective-permute-start.10 = (bf16[192,512]{1,0:T(8,128)(2,1)S(1)}, bf16[192,512]{1,0:T(8,128)(2,1)S(1)}, u32[]{:S(2)}, u32[]{:S(2)}) collective-permute-start(bf16[192,512]{1,0:T(8,128)(2,1)S(1)} %bitcast.5), channel_id=1, source_target_pairs={{0,64},{64,128},{128,192},{192,0},{1,65},{65,129},{129,193},{193,1... | collective-permute-start | bytes 589832 | tf_op jit(solution)/shard_map/ppermute | solution.py:456
  95.1 7.5 %collective-permute-start.9 = (bf16[192,512]{1,0:T(8,128)(2,1)S(1)}, bf16[192,512]{1,0:T(8,128)(2,1)S(1)}, u32[]{:S(2)}, u32[]{:S(2)}) collective-permute-start(bf16[192,512]{1,0:T(8,128)(2,1)S(1)} %bitcast.6), channel_id=1, source_target_pairs={{0,128},{64,192},{128,0},{192,64},{1,129},{65,193},{129,1},{193,65... | collective-permute-start | bytes 589832 | tf_op jit(solution)/shard_map/ppermute | solution.py:456
  96.9 6.4 %collective-permute-start.8 = (bf16[192,512]{1,0:T(8,128)(2,1)S(1)}, bf16[192,512]{1,0:T(8,128)(2,1)S(1)}, u32[]{:S(2)}, u32[]{:S(2)}) collective-permute-start(bf16[192,512]{1,0:T(8,128)(2,1)S(1)} %bitcast.7), channel_id=1, source_target_pairs={{0,192},{64,0},{128,64},{192,128},{1,193},{65,1},{129,65},{193,129... | collective-permute-start | bytes 589832 | tf_op jit(solution)/shard_map/ppermute | solution.py:456
  102.6 0.7 copy-start.1
  102.6 0.8 copy-start.2
  103.4 0.7 copy-start.3
